TPU v7x, 256 devices: a whole 4x4x8 slice. The times are simulated.
256 devices in a mesh: role: 4 (over z_hi, core), dp: 4 (over x), tensor: 16 (over y, z_lo).
Axes of the slice: x: 4, y: 4, z: 8 (z_hi: 2, z_lo: 4; z = z_hi * 4 + z_lo), core: 2. Of those that a mesh axis runs over, the one named last changes fastest.
Arguments:
- teacher_act: bfloat16 [4, 512, 28672], P(None, 'dp', ('role', 'tensor')), may hold values from -6 to 6
- teacher_down: bfloat16 [28672, 8192], P(('role', 'tensor')), may hold values from -0.09375 to 0.09375
- teacher_resid: bfloat16 [2048, 8192], P(('role', 'dp'), 'tensor'), may hold values from -6 to 6
- attn_out: bfloat16 [2048, 4096], P(('role', 'dp'), 'tensor'), may hold values from -6 to 6
- out_proj: bfloat16 [4096, 4096], P('tensor'), may hold values from -0.09375 to 0.09375
- student_resid: bfloat16 [2048, 4096], P(('role', 'dp')), may hold values from -6 to 6
- proj: bfloat16 [4096, 8192], P(('role', 'dp'), 'tensor'), may hold values from -0.09375 to 0.09375
Outputs:
- attn_grad: bfloat16 [2048, 4096], P(('role', 'dp'), 'tensor')
- proj_grad: float32 [4096, 8192], P(('role', 'dp'), 'tensor')
All inputs are finite; a program needn't handle non-finite values.
Results may differ from a plain program's by a relative error of at most 0.024.
Values may be sent and summed in bfloat16 or wider, within the bound.
No kernel may reach another device: no remote copies, remote signals or barrier semaphores. Data moves between devices by JAX's collectives and lax.ppermute only.
A program may use at most 128 MiB of HBM per device.

v0:
```python
import math

import jax
import jax.numpy as jnp
from jax import lax
from jax.sharding import PartitionSpec as P


def on_device(teacher_act, teacher_down, teacher_resid, attn_out, out_proj, student_resid, proj):
    tok_rows = attn_out.shape[0]
    teacher_term = jnp.einsum(
        "ksf,fd->ksd", teacher_act, teacher_down, preferred_element_type=jnp.float32
    )
    col_part = lax.psum_scatter(
        teacher_term.astype(jnp.bfloat16), "tensor", scatter_dimension=2, tiled=True
    )
    row_part = lax.psum_scatter(col_part, "role", scatter_dimension=0, tiled=True).astype(
        jnp.float32
    )
    teacher_sum = row_part.reshape(tok_rows, row_part.shape[2])
    teacher_hidden = (teacher_resid.astype(jnp.float32) + teacher_sum).astype(jnp.bfloat16)
    local_proj = jnp.dot(attn_out, out_proj, preferred_element_type=jnp.float32)
    summed = lax.psum(local_proj, "tensor")
    student_hidden = (student_resid.astype(jnp.float32) + summed).astype(jnp.bfloat16)
    proj_cols = lax.all_gather(proj, ("role", "dp"), axis=0, tiled=True)
    mapped = jnp.dot(student_hidden, proj_cols, preferred_element_type=jnp.float32)
    err = (mapped - teacher_hidden.astype(jnp.float32)).astype(jnp.bfloat16)
    back_part = lax.dot_general(
        err, proj_cols, (((1,), (1,)), ((), ())), preferred_element_type=jnp.float32
    )
    back = lax.psum(back_part.astype(jnp.bfloat16), "tensor")
    attn_grad = lax.dot_general(
        back, out_proj, (((1,), (1,)), ((), ())), preferred_element_type=jnp.float32
    ).astype(jnp.bfloat16)
    scale_factor = 1.0 / math.sqrt(tok_rows * lax.axis_size("role") * lax.axis_size("dp"))
    product = lax.dot_general(
        student_hidden, err, (((0,), (0,)), ((), ())), preferred_element_type=jnp.float32
    )
    proj_grad = lax.psum_scatter(
        (product * scale_factor).astype(jnp.bfloat16),
        ("role", "dp"),
        scatter_dimension=0,
        tiled=True,
    ).astype(jnp.float32)
    return (attn_grad, proj_grad)


def solution(mesh):
    return jax.shard_map(
        on_device,
        mesh=mesh,
        in_specs=(
            P(None, "dp", ("role", "tensor")),
            P(("role", "tensor"), None),
            P(("role", "dp"), "tensor"),
            P(("role", "dp"), "tensor"),
            P("tensor", None),
            P(("role", "dp"), None),
            P(("role", "dp"), "tensor"),
        ),
        out_specs=(P(("role", "dp"), "tensor"), P(("role", "dp"), "tensor")),
        check_vma=False,
    )
```

profile of v0, /device:TPU:46, one launch (start us, length us, event | category | flops | bytes accessed | tf_op | source)
XLA Modules:
  0.0 653.0 jit_solution(16042586798531421094)
XLA Ops:
  8.0 0.0 copy-start
  8.0 0.0 reduce-scatter.4.cloned.1.call-start
  8.1 11.1 %convolution_convert_fusion = bf16[4,128,8192]{2,1,0:T(8,128)(2,1)} fusion(bf16[4,128,448]{1,2,0:T(8,128)(2,1)} %param.7, bf16[448,8192]{1,0:T(8,128)(2,1)} %param.8), kind=kOutput, calls=%fused_computation | convolution fusion | flops 3762290688 | bytes 16187392 | tf_op jit(solution)/shard_map/ksf,fd->ksd/dot_general | solution.py:11
  19.2 0.0 copy-start.4
  19.2 0.0 reduce-scatter.4.cloned.1.call-update
  19.2 0.0 copy-start.2
  19.2 0.0 copy-start.3
  19.3 0.0 all-reduce.3.cloned.1.call-start
  19.3 0.0 copy-done
  19.3 0.7 copy-done.4
  20.0 1.8 fusion.3
  21.8 0.0 all-reduce.3.cloned.1.call-update
  21.8 0.0 all-gather.2.cloned.1.call-start
  21.9 0.5 all-gather.2.cloned.1.call-update
  22.4 0.0 reduce-scatter.6.cloned.1.call-start
  22.5 210.0 %reduce-scatter.4.cloned.1.call-done = bf16[4,128,512]{2,1,0:T(8,128)(2,1)} async-done(((bf16[4,128,8192]{2,1,0:T(8,128)(2,1)}), bf16[4,128,512]{2,1,0:T(8,128)(2,1)}) %reduce-scatter.4.cloned.1.call-update) | async-done | bytes 524304 | tf_op jit(solution)/shard_map/reduce_scatter | solution.py:14
  232.5 0.0 reduce-scatter.6.cloned.1.call-update
  232.5 0.0 all-reduce.5.cloned.1.call-start
  232.6 175.2 %all-reduce.3.cloned.1.call-done = f32[128,4096]{1,0:T(8,128)} async-done(((f32[128,4096]{1,0:T(8,128)}), f32[128,4096]{1,0:T(8,128)}) %all-reduce.3.cloned.1.call-update) | async-done | bytes 2097168 | tf_op jit(solution)/shard_map/psum | solution.py:23
  407.7 0.0 all-gather.2.cloned.1.call-done
  407.7 45.1 %reduce-scatter.6.cloned.1.call-done = bf16[1,128,512]{2,1,0:T(8,128)(2,1)} async-done(((bf16[4,128,512]{2,1,0:T(8,128)(2,1)}), bf16[1,128,512]{2,1,0:T(8,128)(2,1)}) %reduce-scatter.6.cloned.1.call-update) | async-done | bytes 131088 | tf_op jit(solution)/shard_map/reduce_scatter | solution.py:17
  452.9 0.0 copy-done.2
  452.9 0.0 copy-done.3
  452.9 0.0 copy-start.1
  452.9 3.7 fusion.1
  456.6 0.4 copy-done.1
  457.0 2.5 convolution_convert_fusion.1
  459.5 0.0 all-reduce.5.cloned.1.call-update
  459.5 0.0 reduce-scatter.8.cloned.1.call-start
  459.5 4.8 multiply_convert_fusion
  464.4 0.0 reduce-scatter.8.cloned.1.call-update
  464.4 177.0 %all-reduce.5.cloned.1.call-done = bf16[128,4096]{1,0:T(8,128)(2,1)} async-done(((bf16[128,4096]{1,0:T(8,128)(2,1)}), bf16[128,4096]{1,0:T(8,128)(2,1)}) %all-reduce.5.cloned.1.call-update) | async-done | bytes 1048592 | tf_op jit(solution)/shard_map/psum | solution.py:31
  641.4 2.7 convolution_convert_fusion.2
  644.1 0.0 reduce-scatter.8.cloned.1.call-done
  644.1 1.8 convert_element_type.44
Async XLA Ops:
  8.0 11.3 %copy-start = (bf16[256,4096]{1,0:T(8,128)(2,1)S(1)}, bf16[256,4096]{1,0:T(8,128)(2,1)}, u32[]{:S(2)}) copy-start(bf16[256,4096]{1,0:T(8,128)(2,1)} %param.11) | copy-start | bytes 6291460
  8.0 224.5 %reduce-scatter.4.cloned.1.call-start = ((), (), s32[]{:S(2)}) async-start(), calls=%async_computation.5 | async-start | bytes 8912896 | tf_op jit(solution)/shard_map/reduce_scatter | solution.py:14
  19.2 0.8 copy-start.4
  19.2 433.7 %copy-start.2 = (bf16[128,4096]{1,0:T(8,128)(2,1)S(1)}, bf16[128,4096]{1,0:T(8,128)(2,1)}, u32[]{:S(2)}) copy-start(bf16[128,4096]{1,0:T(8,128)(2,1)} %param.12) | copy-start | bytes 3145732
  19.2 433.6 %copy-start.3 = (bf16[128,512]{1,0:T(8,128)(2,1)S(1)}, bf16[128,512]{1,0:T(8,128)(2,1)}, u32[]{:S(2)}) copy-start(bf16[128,512]{1,0:T(8,128)(2,1)} %param.9) | copy-start | bytes 393220
  19.3 388.5 %all-reduce.3.cloned.1.call-start = ((), (), s32[]{:S(2)}) async-start(), calls=%async_computation.3 | async-start | bytes 4194304 | tf_op jit(solution)/shard_map/psum | solution.py:23
  21.8 385.9 %all-gather.2.cloned.1.call-start = ((), (), s32[]{:S(2)}) async-start(), calls=%async_computation.4 | async-start | bytes 4456448 | tf_op jit(solution)/shard_map/all_gather | solution.py:25
  22.4 430.5 %reduce-scatter.6.cloned.1.call-start = ((), (), s32[]{:S(2)}) async-start(), calls=%async_computation.6 | async-start | bytes 655360 | tf_op jit(solution)/shard_map/reduce_scatter | solution.py:17
  232.5 408.8 %all-reduce.5.cloned.1.call-start = ((), (), s32[]{:S(2)}) async-start(), calls=%async_computation.7 | async-start | bytes 2097152 | tf_op jit(solution)/shard_map/psum | solution.py:31
  452.9 4.1 copy-start.1
  459.5 184.6 %reduce-scatter.8.cloned.1.call-start = ((), (), s32[]{:S(2)}) async-start(), calls=%async_computation.8 | async-start | bytes 4456448 | tf_op jit(solution)/shard_map/reduce_scatter | solution.py:39
Sparse Core Ops, SparseCore 0:
  19.4 213.0 reduce-scatter.3
  235.1 172.5 all-reduce.2
  410.5 42.3 reduce-scatter.5
  459.6 181.7 all-reduce.4
Sparse Core Ops, SparseCore 1:
  25.4 95.6 all-gather.1
  464.5 101.5 reduce-scatter.7
where the time goes:
time: 659 us; the launch traced here: 653 us
  waiting for transfers between devices  608 us (92%)
  matrix products  26.6 us (4%)
  between operations  15.3 us (2%)
    reduce_scatter x1, waiting for transfers between devices, on_device(): lax.psum_scatter(teacher_term.astype(jnp.bfloat16), 'tensor', scatter_dim...  210 us
    psum x1, waiting for transfers between devices, on_device(): back = lax.psum(back_part.astype(jnp.bfloat16), 'tensor')  177 us
    psum x1, waiting for transfers between devices, on_device(): summed = lax.psum(local_proj, 'tensor')  175 us
    reduce_scatter x1, waiting for transfers between devices, on_device(): lax.psum_scatter(col_part, 'role', scatter_dimension=0, tiled=True)  45.1 us
  transfers between devices with their start and end apart: 6, of which 4 were waited for; matrix products, arithmetic and copies ran while one was open for 1% of the time, Pallas kernels for 0%

commit v1 on v0

v1 whole, which is shorter than its diff:
```python
import math

import jax
import jax.numpy as jnp
from jax import lax
from jax.sharding import Mesh
from jax.sharding import PartitionSpec as P

BF = jnp.bfloat16
F32 = jnp.float32
SWAP = [(0, 1), (1, 0)]


def spread(x, axes, dim):
    n = lax.axis_size(axes)
    shape = x.shape
    x = x.reshape(shape[:dim] + (n, shape[dim] // n) + shape[dim + 1 :])
    x = jnp.moveaxis(x, dim, 0)
    return lax.all_to_all(x, axes, 0, 0, tiled=True)


def added(x):
    return jnp.sum(x.astype(F32), axis=0)


def gathered(x, axes):
    n = lax.axis_size(axes)
    return lax.all_to_all(jnp.broadcast_to(x[None], (n,) + x.shape), axes, 0, 0, tiled=True)


def columns(x):
    n, rows, cols = x.shape
    return jnp.moveaxis(x, 0, 1).reshape(rows, n * cols)


def on_device(act, down, t_resid, attn, out_proj, s_resid, proj):
    core = lax.axis_index("c")
    tensor = ("y", "zl")
    tok = attn.shape[0]
    proj_all = lax.all_gather(proj, ("zh", "c", "x"), axis=0, tiled=True)

    act4 = act.reshape(2, 2, tok, act.shape[2])
    theirs = lax.dynamic_index_in_dim(act4, 1 - core, 1, keepdims=False)
    mine = lax.dynamic_index_in_dim(act4, core, 1, keepdims=False)
    sent = jnp.einsum("ksf,fd->ksd", theirs, down, preferred_element_type=F32).astype(BF)
    came = lax.ppermute(sent, "c", SWAP)
    student_part = jnp.dot(attn, out_proj, preferred_element_type=F32).astype(BF)
    own = jnp.einsum("ksf,fd->ksd", mine, down, preferred_element_type=F32)
    chip = (own + came.astype(F32)).astype(BF)
    over_y = added(spread(chip, "y", 2)).astype(BF)
    zh, _, wide = over_y.shape
    zl = lax.axis_size("zl")
    to_z = over_y.reshape(zh, tok, zl, wide // zl)
    to_z = jnp.moveaxis(to_z, 2, 1).reshape(zh * zl, tok, wide // zl)
    teacher_sum = added(lax.all_to_all(to_z, ("zh", "zl"), 0, 0, tiled=True))
    teacher_hidden = (t_resid.astype(F32) + teacher_sum).astype(BF)

    cols = attn.shape[1]
    at = lax.axis_index(tensor) * cols
    resid = lax.dynamic_slice_in_dim(s_resid, at, cols, 1)
    hidden_cols = (resid.astype(F32) + added(spread(student_part, tensor, 1))).astype(BF)
    hidden = columns(gathered(hidden_cols, tensor))

    mapped = jnp.dot(hidden, proj_all, preferred_element_type=F32)
    err = (mapped - teacher_hidden.astype(F32)).astype(BF)

    scale = 1.0 / math.sqrt(tok * 16)
    parts = hidden.reshape(tok, 2, 2, 4 * proj.shape[0])
    h_theirs = lax.dynamic_index_in_dim(parts, 1 - core, 2, keepdims=False).reshape(tok, -1)
    h_mine = lax.dynamic_index_in_dim(parts, core, 2, keepdims=False).reshape(tok, -1)
    contract = (((0,), (0,)), ((), ()))
    g_sent = lax.dot_general(h_theirs, err, contract, preferred_element_type=F32)
    g_came = lax.ppermute((g_sent * scale).astype(BF), "c", SWAP)
    back_part = lax.dot_general(
        err, proj_all, (((1,), (1,)), ((), ())), preferred_element_type=F32
    ).astype(BF)
    g_own = lax.dot_general(h_mine, err, contract, preferred_element_type=F32)
    g_chip = (g_own * scale + g_came.astype(F32)).astype(BF)
    proj_grad = lax.psum_scatter(g_chip, ("zh", "x"), scatter_dimension=0, tiled=True).astype(F32)

    back_cols = added(spread(back_part, tensor, 1)).astype(BF)
    back = columns(gathered(back_cols, tensor))
    attn_grad = lax.dot_general(
        back, out_proj, (((1,), (1,)), ((), ())), preferred_element_type=F32
    ).astype(BF)
    return (attn_grad, proj_grad)


def solution(mesh):
    fine = Mesh(mesh.devices.reshape(2, 2, 4, 4, 4), ("zh", "c", "x", "y", "zl"))
    role, group, tensor = ("zh", "c"), ("zh", "c", "x"), ("y", "zl")
    return jax.shard_map(
        on_device,
        mesh=fine,
        in_specs=(
            P(None, "x", ("zh", "c", "y", "zl")),
            P(("zh", "c", "y", "zl"), None),
            P(group, tensor),
            P(group, tensor),
            P(tensor, None),
            P(group, None),
            P(group, tensor),
        ),
        out_specs=(P(group, tensor), P(group, tensor)),
        check_vma=False,
    )
```

time: 659 us -> 305 us (0.46)
  waiting for transfers between devices: 608 us -> 161 us
  blocking collectives: 0 us -> 44.3 us
  starting transfers between devices: 0.25 us -> 38 us
  other arithmetic: 1.8 us -> 9.62 us
  local copies, waits for them, and re-layouts: 1.12 us -> 8.73 us
    psum x2 -> x0, waiting for transfers between devices: 352 us -> none  [the longest x1 177 us: on_device(): back = lax.psum(back_part.astype(jnp.bfloat16), 'tensor')]
    reduce_scatter x3 -> x1, waiting for transfers between devices: 255 us -> 28.2 us  [on_device(): lax.psum_scatter(g_chip, ('zh', 'x'), scatter_dimension=0, tiled=True)]
    all_to_all x0 -> x5, waiting for transfers between devices: none -> 132 us  [the longest x3 91.4 us: spread(): return lax.all_to_all(x, axes, 0, 0, tiled=True)]
    all_to_all x0 -> x1, blocking collectives: none -> 44.3 us  [gathered(): lax.all_to_all(jnp.broadcast_to(x[None], (n,) + x.shape), axes, 0, 0, til...]
    all_to_all x0 -> x5, starting transfers between devices: none -> 37.9 us  [the longest x3 21.1 us: spread(): return lax.all_to_all(x, axes, 0, 0, tiled=True)]
    dot_general x5 -> x7, matrix products: 23.9 us -> 25.4 us  [the longest x1 7.7 us: on_device(): jnp.einsum('ksf,fd->ksd', theirs, down, preferred_element_type=F32)]
  transfers between devices with their start and end apart: 6 -> 9, of which waited for: 4 -> 6; matrix products, arithmetic and copies ran while one was open for 1% -> 10% of each run, Pallas kernels for 0% -> 0%
where the time goes in v1:
time: 305 us; the launch traced here: 303 us
  waiting for transfers between devices  161 us (53%)
  blocking collectives  44.3 us (15%)
  starting transfers between devices  38 us (12%)
  matrix products  26.9 us (9%)
  between operations  14.2 us (5%)
  other arithmetic  9.62 us (3%)
  local copies, waits for them, and re-layouts  8.73 us (3%)
    all_to_all x3, waiting for transfers between devices, spread(): return lax.all_to_all(x, axes, 0, 0, tiled=True)  91.4 us
    all_to_all x1, blocking collectives, gathered(): lax.all_to_all(jnp.broadcast_to(x[None], (n,) + x.shape), axes, 0, 0, til...  44.3 us
    reduce_scatter x1, waiting for transfers between devices, on_device(): lax.psum_scatter(g_chip, ('zh', 'x'), scatter_dimension=0, tiled=True)  28.2 us
    all_to_all x1, waiting for transfers between devices, on_device(): teacher_sum = added(lax.all_to_all(to_z, ('zh', 'zl'), 0, 0, tiled=True))  25.2 us
    all_to_all x3, starting transfers between devices, spread(): return lax.all_to_all(x, axes, 0, 0, tiled=True)  21.1 us
    all_to_all x1, waiting for transfers between devices, gathered(): lax.all_to_all(jnp.broadcast_to(x[None], (n,) + x.shape), axes, 0, 0, til...  15.7 us
    all_to_all x1, starting transfers between devices, gathered(): lax.all_to_all(jnp.broadcast_to(x[None], (n,) + x.shape), axes, 0, 0, til...  8.95 us
    all_to_all x1, starting transfers between devices, on_device(): teacher_sum = added(lax.all_to_all(to_z, ('zh', 'zl'), 0, 0, tiled=True))  7.9 us
  transfers between devices with their start and end apart: 9, of which 6 were waited for; matrix products, arithmetic and copies ran while one was open for 10% of the time, Pallas kernels for 0%

profile of v1, /device:TPU:46, one launch (start us, length us, event | category | flops | bytes accessed | tf_op | source)
XLA Modules:
  0.0 302.9 jit_solution(17675722910759807264)
XLA Ops:
  7.2 0.0 copy-start
  7.2 0.0 copy-start.3
  7.2 7.7 %convolution_convert_fusion = bf16[2,128,8192]{2,1,0:T(8,128)(2,1)} fusion(bf16[448,8192]{1,0:T(8,128)(2,1)} %param.8, bf16[2,2,128,448]{2,3,1,0:T(8,128)(2,1)} %bitcast.74, s32[]{:T(128)S(6)} %select_n.15), kind=kOutput, calls=%fused_computation | convolution fusion | flops 1881145344 | bytes 11763716 | tf_op jit(solution)/shard_map/ksf,fd->ksd/dot_general | solution.py:45
  14.9 0.0 collective-permute-start
  14.9 0.0 copy-done
  14.9 0.0 copy-done.3
  14.9 0.4 convolution_convert_fusion.2
  15.4 1.1 copy.41
  16.5 8.5 %all-to-all-start = ((bf16[16,128,256]{2,1,0:T(8,128)(2,1)}), bf16[16,128,256]{2,1,0:T(8,128)(2,1)S(1)}, u32[]{:S(2)}, u32[]{:S(2)}) async-start(bf16[16,128,256]{2,1,0:T(8,128)(2,1)} %bitcast.68), calls=%async_computation | async-start | bytes 2097152 | tf_op jit(solution)/shard_map/all_to_all | solution.py:19
  25.1 0.0 all-gather.2.cloned.1.call-start
  25.1 0.7 all-gather.2.cloned.1.call-update
  25.8 0.0 collective-permute-done
  25.8 6.8 %add_convert_fusion = bf16[2,128,8192]{2,1,0:T(8,128)(2,1)S(1)} fusion(bf16[2,128,8192]{2,1,0:T(8,128)(2,1)} %collective-permute-done, bf16[448,8192]{1,0:T(8,128)(2,1)} %param.8, bf16[2,2,128,448]{2,3,1,0:T(8,128)(2,1)} %bitcast.75, s32[]{:T(128)S(6)} %select_n.14), kind=kOutput, calls=%fused_computation.1 | convolution fusion | flops 1885339648 | bytes 15958020 | tf_op jit(solution)/shard_map/ksf,fd->ksd/dot_general | solution.py:48
  32.6 2.5 copy.39
  35.1 19.8 %all-to-all-done = bf16[16,128,256]{2,1,0:T(8,128)(2,1)S(1)} async-done(((bf16[16,128,256]{2,1,0:T(8,128)(2,1)}), bf16[16,128,256]{2,1,0:T(8,128)(2,1)S(1)}, u32[]{:S(2)}, u32[]{:S(2)}) %all-to-all-start) | async-done | bytes 1048608 | tf_op jit(solution)/shard_map/all_to_all | solution.py:19
  54.9 5.3 %all-to-all-start.2 = ((bf16[4,2,128,2048]{3,2,1,0:T(8,128)(2,1)}), bf16[4,2,128,2048]{3,2,1,0:T(8,128)(2,1)}, u32[]{:S(2)}, u32[]{:S(2)}) async-start(bf16[4,2,128,2048]{3,2,1,0:T(8,128)(2,1)} %bitcast.63), calls=%async_computation.2 | async-start | bytes 8388608 | tf_op jit(solution)/shard_map/all_to_all | solution.py:19
  60.3 0.1 convert_reduce_fusion.1
  60.4 0.9 add_convert_fusion.3
  61.3 0.1 copy.23
  61.4 45.6 %all-to-all-done.2 = bf16[4,2,128,2048]{3,2,1,0:T(8,128)(2,1)} async-done(((bf16[4,2,128,2048]{3,2,1,0:T(8,128)(2,1)}), bf16[4,2,128,2048]{3,2,1,0:T(8,128)(2,1)}, u32[]{:S(2)}, u32[]{:S(2)}) %all-to-all-start.2) | async-done | bytes 4194336 | tf_op jit(solution)/shard_map/all_to_all | solution.py:19
  107.0 1.3 broadcast_in_dim.4
  108.3 8.9 %all-to-all-start.1 = ((bf16[16,128,256]{1,2,0:T(8,128)(2,1)}), bf16[16,128,256]{1,2,0:T(8,128)(2,1)S(1)}, u32[]{:S(2)}, u32[]{:S(2)}) async-start(bf16[16,128,256]{1,2,0:T(8,128)(2,1)} %broadcast_in_dim.4), calls=%async_computation.1 | async-start | bytes 2097152 | tf_op jit(solution)/shard_map/all_to_all | solution.py:28
  117.2 4.2 %reduce_sum.43 = bf16[2,128,2048]{2,1,0:T(8,128)(2,1)} reduce(bf16[4,2,128,2048]{3,2,1,0:T(8,128)(2,1)} %all-to-all-done.2, bf16[]{:T(256)} %constant.43.clone.1), dimensions={0}, to_apply=%region_1.2 | reduce | flops 1572864 | bytes 5242882 | tf_op jit(solution)/shard_map/reduce_sum | solution.py:23
  121.4 1.3 fusion.12
  122.7 1.0 pad_maximum_fusion
  123.7 15.7 %all-to-all-done.1 = bf16[16,128,256]{1,2,0:T(8,128)(2,1)S(1)} async-done(((bf16[16,128,256]{1,2,0:T(8,128)(2,1)}), bf16[16,128,256]{1,2,0:T(8,128)(2,1)S(1)}, u32[]{:S(2)}, u32[]{:S(2)}) %all-to-all-start.1) | async-done | bytes 1048608 | tf_op jit(solution)/shard_map/all_to_all | solution.py:28
  139.4 7.9 %all-to-all-start.3 = ((bf16[8,128,512]{2,1,0:T(8,128)(2,1)}), bf16[8,128,512]{2,1,0:T(8,128)(2,1)}, u32[]{:S(2)}, u32[]{:S(2)}) async-start(bf16[8,128,512]{2,1,0:T(8,128)(2,1)} %bitcast.70), calls=%async_computation.3 | async-start | bytes 2097152 | tf_op jit(solution)/shard_map/all_to_all | solution.py:55
  147.3 1.1 constant_dynamic-slice_fusion.1
  148.4 25.2 %all-to-all-done.3 = bf16[8,128,512]{2,1,0:T(8,128)(2,1)} async-done(((bf16[8,128,512]{2,1,0:T(8,128)(2,1)}), bf16[8,128,512]{2,1,0:T(8,128)(2,1)}, u32[]{:S(2)}, u32[]{:S(2)}) %all-to-all-start.3) | async-done | bytes 1048608 | tf_op jit(solution)/shard_map/all_to_all | solution.py:55
  173.5 1.4 convert_reduce_fusion
  174.9 0.0 all-gather.2.cloned.1.call-done
  175.0 0.0 copy-start.2
  175.0 0.0 copy-start.1
  175.0 3.1 %fusion.5 = bf16[128,512]{1,0:T(8,128)(2,1)S(1)} fusion(bf16[128,4096]{0,1:T(8,128)(2,1)S(1)} %bitcast.65, bf16[4096,512]{1,0:T(8,128)(2,1)} %all-gather.2.cloned.1.call-done, f32[128,512]{1,0:T(8,128)S(1)} %convert_reduce_fusion, bf16[128,512]{1,0:T(8,128)(2,1)} %param.9), kind=kOutput, calls=%fused_computation.13 | convolution fusion | flops 537264128 | bytes 5767168 | tf_op jit(solution)/shard_map/dot_general | solution.py:64
  178.1 0.0 copy-done.2
  178.1 2.0 multiply_convert_fusion
  180.1 0.0 collective-permute-start.1
  180.1 0.0 copy-done.1
  180.1 1.5 convolution_convert_fusion.1
  181.6 1.1 copy.40
  182.7 7.2 %all-to-all-start.4 = ((bf16[16,128,256]{2,1,0:T(8,128)(2,1)}), bf16[16,128,256]{2,1,0:T(8,128)(2,1)S(1)}, u32[]{:S(2)}, u32[]{:S(2)}) async-start(bf16[16,128,256]{2,1,0:T(8,128)(2,1)} %bitcast.69), calls=%async_computation.4 | async-start | bytes 2097152 | tf_op jit(solution)/shard_map/all_to_all | solution.py:19
  189.9 0.0 reduce-scatter.2.cloned.1.call-start
  189.9 0.0 collective-permute-done.1
  189.9 3.8 %add_convert_fusion.1 = bf16[2048,512]{1,0:T(8,128)(2,1)} fusion(bf16[2048,512]{1,0:T(8,128)(2,1)} %collective-permute-done.1, bf16[128,2048]{0,1:T(8,128)(2,1)} %bitcast.72, bf16[128,512]{1,0:T(8,128)(2,1)S(1)} %fusion.5), kind=kOutput, calls=%fused_computation.8 | convolution fusion | flops 272629760 | bytes 4849664 | tf_op jit(solution)/shard_map/dot_general | solution.py:77
  193.7 0.0 reduce-scatter.2.cloned.1.call-update
  193.8 26.0 %all-to-all-done.4 = bf16[16,128,256]{2,1,0:T(8,128)(2,1)S(1)} async-done(((bf16[16,128,256]{2,1,0:T(8,128)(2,1)}), bf16[16,128,256]{2,1,0:T(8,128)(2,1)S(1)}, u32[]{:S(2)}, u32[]{:S(2)}) %all-to-all-start.4) | async-done | bytes 1048608 | tf_op jit(solution)/shard_map/all_to_all | solution.py:19
  219.7 0.1 reduce_sum.45
  219.9 0.1 copy.29
  220.0 0.2 broadcast_in_dim.5
  220.2 44.3 %all_to_all.30 = bf16[16,128,256]{1,2,0:T(8,128)(2,1)S(1)} all-to-all(bf16[16,128,256]{1,2,0:T(8,128)(2,1)S(1)} %broadcast_in_dim.5), channel_id=1, replica_groups=mesh['zh'=2,'c'=2,'x'=4,'y'=4,'zl'=4] {'y','zl'}, dimensions={0} | all-to-all | bytes 2097152 | tf_op jit(solution)/shard_map/all_to_all | solution.py:28
  264.5 1.5 convolution_convert_fusion.3
  266.0 28.2 %reduce-scatter.2.cloned.1.call-done = bf16[256,512]{1,0:T(8,128)(2,1)} async-done(((bf16[2048,512]{1,0:T(8,128)(2,1)}), bf16[256,512]{1,0:T(8,128)(2,1)}) %reduce-scatter.2.cloned.1.call-update) | async-done | bytes 262160 | tf_op jit(solution)/shard_map/reduce_scatter | solution.py:79
  294.2 1.8 convert_element_type.75
Async XLA Ops:
  7.2 7.7 %copy-start = (bf16[256,4096]{1,0:T(8,128)(2,1)S(1)}, bf16[256,4096]{1,0:T(8,128)(2,1)}, u32[]{:S(2)}) copy-start(bf16[256,4096]{1,0:T(8,128)(2,1)} %param.11) | copy-start | bytes 6291460
  7.2 7.7 %copy-start.3 = (bf16[128,256]{1,0:T(8,128)(2,1)S(1)}, bf16[128,256]{1,0:T(8,128)(2,1)}, u32[]{:S(2)}) copy-start(bf16[128,256]{1,0:T(8,128)(2,1)} %param.10) | copy-start | bytes 196612
  14.9 10.9 %collective-permute-start = (bf16[2,128,8192]{2,1,0:T(8,128)(2,1)}, bf16[2,128,8192]{2,1,0:T(8,128)(2,1)}, u32[]{:S(2)}, u32[]{:S(2)}) collective-permute-start(bf16[2,128,8192]{2,1,0:T(8,128)(2,1)} %convolution_convert_fusion), channel_id=1, source_target_pairs={{0,64},{64,0},{1,65},{65,1},{2,66},{66,2},{3,67},{67,3},{4,68},{68... | collective-permute-start | bytes 12582920 | tf_op jit(solution)/shard_map/ppermute | solution.py:46
  16.5 38.4 %all-to-all-start = ((bf16[16,128,256]{2,1,0:T(8,128)(2,1)}), bf16[16,128,256]{2,1,0:T(8,128)(2,1)S(1)}, u32[]{:S(2)}, u32[]{:S(2)}) async-start(bf16[16,128,256]{2,1,0:T(8,128)(2,1)} %bitcast.68), calls=%async_computation | async-start | bytes 2097152 | tf_op jit(solution)/shard_map/all_to_all | solution.py:19
  25.1 149.9 %all-gather.2.cloned.1.call-start = ((), (), s32[]{:S(2)}) async-start(), calls=%async_computation.7 | async-start | bytes 4456448 | tf_op jit(solution)/shard_map/all_gather | solution.py:40
  54.9 52.0 %all-to-all-start.2 = ((bf16[4,2,128,2048]{3,2,1,0:T(8,128)(2,1)}), bf16[4,2,128,2048]{3,2,1,0:T(8,128)(2,1)}, u32[]{:S(2)}, u32[]{:S(2)}) async-start(bf16[4,2,128,2048]{3,2,1,0:T(8,128)(2,1)} %bitcast.63), calls=%async_computation.2 | async-start | bytes 8388608 | tf_op jit(solution)/shard_map/all_to_all | solution.py:19
  108.3 31.1 %all-to-all-start.1 = ((bf16[16,128,256]{1,2,0:T(8,128)(2,1)}), bf16[16,128,256]{1,2,0:T(8,128)(2,1)S(1)}, u32[]{:S(2)}, u32[]{:S(2)}) async-start(bf16[16,128,256]{1,2,0:T(8,128)(2,1)} %broadcast_in_dim.4), calls=%async_computation.1 | async-start | bytes 2097152 | tf_op jit(solution)/shard_map/all_to_all | solution.py:28
  139.4 34.1 %all-to-all-start.3 = ((bf16[8,128,512]{2,1,0:T(8,128)(2,1)}), bf16[8,128,512]{2,1,0:T(8,128)(2,1)}, u32[]{:S(2)}, u32[]{:S(2)}) async-start(bf16[8,128,512]{2,1,0:T(8,128)(2,1)} %bitcast.70), calls=%async_computation.3 | async-start | bytes 2097152 | tf_op jit(solution)/shard_map/all_to_all | solution.py:55
  175.0 3.1 %copy-start.2 = (bf16[128,2,1,1024]{0,3,2,1:T(8,128)(2,1)S(1)}, bf16[128,2,1,1024]{0,3,2,1:T(8,128)(2,1)}, u32[]{:S(2)}) copy-start(bf16[128,2,1,1024]{0,3,2,1:T(8,128)(2,1)} %get-tuple-element.3) | copy-start | bytes 1572868
  175.0 5.2 %copy-start.1 = (bf16[4096,512]{1,0:T(8,128)(2,1)S(1)}, bf16[4096,512]{1,0:T(8,128)(2,1)}, u32[]{:S(2)}) copy-start(bf16[4096,512]{1,0:T(8,128)(2,1)} %all-gather.2.cloned.1.call-done) | copy-start | bytes 12582916
  180.1 9.8 %collective-permute-start.1 = (bf16[2048,512]{1,0:T(8,128)(2,1)}, bf16[2048,512]{1,0:T(8,128)(2,1)}, u32[]{:S(2)}, u32[]{:S(2)}) collective-permute-start(bf16[2048,512]{1,0:T(8,128)(2,1)} %multiply_convert_fusion), channel_id=1, source_target_pairs={{0,64},{64,0},{1,65},{65,1},{2,66},{66,2},{3,67},{67,3},{4,68},{68... | collective-permute-start | bytes 6291464 | tf_op jit(solution)/shard_map/ppermute | solution.py:73
  182.7 37.0 %all-to-all-start.4 = ((bf16[16,128,256]{2,1,0:T(8,128)(2,1)}), bf16[16,128,256]{2,1,0:T(8,128)(2,1)S(1)}, u32[]{:S(2)}, u32[]{:S(2)}) async-start(bf16[16,128,256]{2,1,0:T(8,128)(2,1)} %bitcast.69), calls=%async_computation.4 | async-start | bytes 2097152 | tf_op jit(solution)/shard_map/all_to_all | solution.py:19
  189.9 104.4 %reduce-scatter.2.cloned.1.call-start = ((), (), s32[]{:S(2)}) async-start(), calls=%async_computation.8 | async-start | bytes 2359296 | tf_op jit(solution)/shard_map/reduce_scatter | solution.py:79
Sparse Core Ops, SparseCore 0:
  28.6 77.5 all-gather.1
  194.8 99.4 reduce-scatter.1

commit v2 on v1

v2 whole, which is shorter than its diff:
```python
import functools
import math

import jax
import jax.numpy as jnp
from jax import lax
from jax.experimental import pallas as pl
from jax.experimental.pallas import tpu as pltpu
from jax.sharding import Mesh
from jax.sharding import PartitionSpec as P

BF = jnp.bfloat16
F32 = jnp.float32
Z = ("zh", "zl")
NT = (((1,), (1,)), ((), ()))
TN = (((0,), (0,)), ((), ()))
VMEM = pl.BlockSpec(memory_space=pltpu.VMEM)
SMEM = pl.BlockSpec(memory_space=pltpu.SMEM)


COST = pl.CostEstimate(flops=1, bytes_accessed=1, transcendentals=0)


def call(body, outs, args, specs=None):
    return pl.pallas_call(
        body,
        out_shape=outs,
        in_specs=specs or [VMEM] * len(args),
        out_specs=[VMEM] * len(outs),
        compiler_params=pltpu.CompilerParams(vmem_limit_bytes=16 * 2**20),
        cost_estimate=COST,
    )(*args)


def moved_by(x, axes, step):
    n = lax.axis_size(axes)
    return lax.ppermute(x, axes, [(i, (i + step) % n) for i in range(n)])


def swapped(x, axis):
    return lax.ppermute(x, axis, [(0, 1), (1, 0)])


def exchanged(x, axes):
    return lax.all_to_all(x, axes, 0, 0, tiled=True)


def added(x):
    return jnp.sum(x.astype(F32), axis=0)


def teacher_body(at_ref, a_ref, w_ref, their_ref, own_ref, rows_ref):
    tok, width = own_ref.shape[-2:]

    @pl.when(pl.program_id(0) == 0)
    def _():
        for side in range(2):
            for zh in range(2):
                role = zh * 2 + lax.rem(at_ref[1] + 1 - side, 2)
                row = (2 * side + zh) * tok
                rows_ref[row : row + tok, :] = a_ref[role].T

    for zl in range(2):
        block = w_ref[:, zl * width : (zl + 1) * width]
        part = jnp.dot(rows_ref[...], block, preferred_element_type=F32).astype(BF)
        for side, ref in enumerate((their_ref, own_ref)):
            for zh in range(2):
                row = (2 * side + zh) * tok
                ref[0, zh, zl] = part[row : row + tok]


def teacher_terms(at, act, w):
    _, tok, depth = act.shape
    width = w.shape[1] // 16
    shape = jax.ShapeDtypeStruct((4, 2, 4, tok, width), BF)
    out = pl.BlockSpec((1, 2, 2, tok, width), lambda i, at: (i // 2, 0, i % 2, 0, 0))
    terms = pl.pallas_call(
        teacher_body,
        grid_spec=pltpu.PrefetchScalarGridSpec(
            num_scalar_prefetch=1,
            grid=(8,),
            in_specs=[
                pl.BlockSpec((4, depth, tok), lambda i, at: (0, 0, 0)),
                pl.BlockSpec((depth, 2 * width), lambda i, at: (0, lax.rem(at[0] + 2 + i // 2, 4) * 2 + i % 2)),
            ],
            out_specs=[out, out],
            scratch_shapes=[pltpu.VMEM((4 * tok, depth), BF)],
        ),
        out_shape=[shape, shape],
        compiler_params=pltpu.CompilerParams(vmem_limit_bytes=56 * 2**20),
        cost_estimate=COST,
    )(at, jnp.swapaxes(act, 1, 2), w)
    return [t.reshape(4, 8, tok, width) for t in terms]


def student_body(a_ref, w_ref, o_ref):
    width = o_ref.shape[-1]
    for i in range(16):
        block = w_ref[:, i * width : (i + 1) * width]
        o_ref[i // 4, i % 4] = jnp.dot(a_ref[...], block, preferred_element_type=F32).astype(BF)


def hidden_body(x_ref, resid_ref, o_ref):
    hidden = (resid_ref[...].astype(F32) + added(x_ref[...])).astype(BF)
    for i in range(o_ref.shape[0]):
        o_ref[i] = hidden


def mapped_body(at_ref, h_ref, one_ref, two_ref, out_ref):
    total = None
    for i in range(16):
        block = (one_ref, two_ref)[i // 8][i % 8]
        term = jnp.dot(h_ref[at_ref[i]], block, preferred_element_type=F32)
        total = term if total is None else total + term
    out_ref[...] = total


def err_body(at_ref, mapped_ref, resid_ref, terms_ref, one_ref, two_ref, err_ref, back_ref):
    teacher = (resid_ref[...].astype(F32) + added(terms_ref[...])).astype(BF)
    err = (mapped_ref[...] - teacher.astype(F32)).astype(BF)
    err_ref[...] = err
    for i in range(16):
        block = (one_ref, two_ref)[i // 8][i % 8]
        at = at_ref[i]
        back = lax.dot_general(err, block, NT, preferred_element_type=F32)
        back_ref[at // 4, lax.rem(at, 4)] = back.astype(BF)


def grad_body(scale, first, at_ref, h_ref, err_ref, *refs):
    err = err_ref[...]
    outs = refs[-4:] if first == 0 else refs
    for i in range(8):
        term = lax.dot_general(h_ref[at_ref[first + i]], err, TN, preferred_element_type=F32) * scale
        if first == 0:
            outs[i // 2][i % 2] = (term + refs[0][i].astype(F32)).astype(BF)
        else:
            outs[0][i] = term.astype(BF)


def grad_sum_body(*refs):
    terms, (own_ref, sent_ref) = refs[:-2], refs[-2:]
    for z, ref in enumerate((own_ref, sent_ref)):
        total = terms[0][z].astype(F32)
        for term in terms[1:]:
            total = total + term[z].astype(F32)
        ref[...] = total.astype(ref.dtype)


def sum_body(x_ref, o_ref):
    total = x_ref[0].astype(F32)
    for i in range(1, x_ref.shape[0]):
        total = total + x_ref[i].astype(F32)
    total = total.astype(BF)
    for i in range(o_ref.shape[0]):
        o_ref[i] = total


def terms_body(*refs):
    total = refs[0][...].astype(F32)
    for ref in refs[1:-1]:
        total = total + ref[...].astype(F32)
    refs[-1][...] = total.astype(BF)


def attn_body(y_ref, w_ref, *refs):
    back_refs, o_ref = refs[:-1], refs[-1]
    total = None
    cols = back_refs[0].shape[-1]
    for step in range(4):
        for zl in range(4):
            at = pl.multiple_of((lax.rem(y_ref[0] + step, 4) * 4 + zl) * cols, cols)
            block = w_ref[:, pl.ds(at, cols)]
            term = lax.dot_general(back_refs[step][zl], block, NT, preferred_element_type=F32)
            total = term if total is None else total + term
    o_ref[...] = total.astype(BF)


def tied(*arrays):
    return lax.optimization_barrier(arrays)


def on_device(act, down, t_resid, attn, out_proj, s_resid, proj):
    core, zh, x, y = (lax.axis_index(a) for a in ("c", "zh", "x", "y"))
    tok, cols = attn.shape
    tensor = ("y", "zl")
    plus = lambda a, b: a.astype(F32) + b.astype(F32)
    shape = lambda *dims, dtype=BF: jax.ShapeDtypeStruct(dims, dtype)
    here = jnp.stack([y, core]).astype(jnp.int32)

    proj_z = swapped(proj, "zh")
    rows_x = [proj] + [moved_by(proj, "x", -step) for step in (1, 2, 3)]
    idx = jnp.stack(
        [
            ((zh + dz) % 2 * 2 + (core + dc) % 2) * 4 + (x + dx) % 4
            for dc in range(2)
            for dx in range(4)
            for dz in range(2)
        ]
    ).astype(jnp.int32)
    at_cols = (idx // 4 - y + 4) % 4 * 4 + idx % 4

    at = lax.axis_index(tensor) * cols
    resid = lax.dynamic_slice_in_dim(s_resid, at, cols, 1)
    part = call(student_body, [shape(4, 4, tok, cols)], [attn, out_proj])[0]
    act, part = tied(act, part)
    student = exchanged(part, "y")

    sent, mine = teacher_terms(here, act, down)
    student = call(sum_body, [shape(1, 4, tok, cols)], [student])[0][0]
    sent, student = tied(sent, student)
    came = swapped(sent, "c")
    up, down_ = plus(mine[0, :4], came[0, :4]).astype(BF), plus(mine[0, 4:], came[0, 4:]).astype(BF)
    up, down_, proj_z = tied(up, down_, proj_z)
    up, down_ = tied(moved_by(up, "y", 1), moved_by(down_, "y", -1))
    rows_z = [proj_z] + [moved_by(proj_z, "x", -step) for step in (1, 2, 3)]
    student = exchanged(student, "zl")
    near = plus(mine[3], came[3])
    up = jnp.concatenate([near[:4] + up.astype(F32), near[4:]], axis=0).astype(BF)
    near = plus(mine[1], came[1])
    down_ = jnp.concatenate([near[:4], near[4:] + down_.astype(F32)], axis=0).astype(BF)
    hidden = call(hidden_body, [shape(4, tok, cols)], [student, resid])[0]
    hidden = exchanged(hidden, "zl")
    up, down_, hidden, *rows_x, rows_z[0], rows_z[1], rows_z[2], rows_z[3] = tied(
        up, down_, hidden, *rows_x, *rows_z
    )
    up, down_ = tied(moved_by(up, "y", 1), moved_by(down_, "y", -1))
    over_y = (plus(mine[2], came[2]) + plus(up, down_)).astype(BF)
    terms = exchanged(over_y, Z)
    rows = jnp.stack([r for both in zip(rows_x, rows_z) for r in both])
    rows = [rows, swapped(rows, "c")]
    hidden = jnp.concatenate([hidden] + [moved_by(hidden, "y", -step) for step in (1, 2, 3)], axis=0)

    mapped = call(
        mapped_body,
        [shape(*t_resid.shape, dtype=F32)],
        [at_cols, hidden, *rows],
        [SMEM, VMEM, VMEM, VMEM],
    )[0]
    mapped, terms = tied(mapped, terms)
    err, back = call(
        err_body,
        [shape(*t_resid.shape), shape(4, 4, tok, cols)],
        [at_cols, mapped, t_resid, terms, *rows],
        [SMEM] + [VMEM] * 5,
    )
    back_moved = [moved_by(back[step], "y", step) for step in (1, 2, 3)]

    scale = 1.0 / math.sqrt(tok * 16)
    theirs_g = call(
        functools.partial(grad_body, scale, 8),
        [shape(8, *proj.shape)],
        [at_cols, hidden, err],
        [SMEM, VMEM, VMEM],
    )[0]
    came_g = swapped(theirs_g, "c")
    chip_g = call(
        functools.partial(grad_body, scale, 0),
        [shape(2, *proj.shape)] * 4,
        [at_cols, hidden, err, came_g],
        [SMEM, VMEM, VMEM, VMEM],
    )
    moved_g = [moved_by(chip_g[step], "x", step) for step in (1, 2, 3)]

    back_moved[0], _ = tied(back_moved[0], chip_g[0])
    back = call(terms_body, [shape(4, tok, cols)], [back[0], *back_moved])[0]
    back = exchanged(back, "zl")
    back = call(sum_body, [shape(4, tok, cols)], [back])[0]
    back = exchanged(back, "zl")
    back, *moved_g = tied(back, *moved_g)
    back_all = [back] + [moved_by(back, "y", -step) for step in (1, 2, 3)]

    own_g, sent_g = call(
        grad_sum_body, [shape(*proj.shape, dtype=F32), shape(*proj.shape)], [chip_g[0], *moved_g]
    )
    came_g = swapped(sent_g, "zh")
    attn_grad = call(attn_body, [shape(tok, cols)], [here, out_proj, *back_all], [SMEM] + [VMEM] * 5)[0]
    attn_grad, came_g = tied(attn_grad, came_g)
    proj_grad = own_g + came_g.astype(F32)
    return (attn_grad, proj_grad)


def solution(mesh):
    fine = Mesh(mesh.devices.reshape(2, 2, 4, 4, 4), ("zh", "c", "x", "y", "zl"))
    group, tensor = ("zh", "c", "x"), ("y", "zl")
    hidden_units = ("zh", "c", "y", "zl")
    return jax.shard_map(
        on_device,
        mesh=fine,
        in_specs=(
            P(None, "x", hidden_units),
            P(hidden_units, None),
            P(group, tensor),
            P(group, tensor),
            P(tensor, None),
            P(group, None),
            P(group, tensor),
        ),
        out_specs=(P(group, tensor), P(group, tensor)),
        check_vma=False,
    )
```

time: 305 us -> 216 us (0.71)
  waiting for transfers between devices: 161 us -> 81 us
  blocking collectives: 44.3 us -> 0 us
  starting transfers between devices: 38 us -> 79 us
  Pallas kernels: 0 us -> 28.2 us
  matrix products: 26.9 us -> 0 us
  between operations: 14.2 us -> 0.93 us
  local copies, waits for them, and re-layouts: 8.73 us -> 12.4 us
  other arithmetic: 9.62 us -> 13.1 us
    all_to_all x5 -> x6, waiting for transfers between devices: 132 us -> 11.6 us  [exchanged(): return lax.all_to_all(x, axes, 0, 0, tiled=True)]
    ppermute x2 -> x27, waiting for transfers between devices: 0.01 us -> 69.4 us  [the longest x22 63.3 us: moved_by(): return lax.ppermute(x, axes, [(i, (i + step) % n) for i in range(n)])]
    ppermute x2 -> x27, starting transfers between devices: 0.01 us -> 46.7 us  [the longest x22 39.7 us: moved_by(): return lax.ppermute(x, axes, [(i, (i + step) % n) for i in range(n)])]
    all_to_all x1 -> x0, blocking collectives: 44.3 us -> none  [gathered(): lax.all_to_all(jnp.broadcast_to(x[None], (n,) + x.shape), axes, 0, 0, til...]
    reduce_scatter x1 -> x0, waiting for transfers between devices: 28.2 us -> none  [on_device(): lax.psum_scatter(g_chip, ('zh', 'x'), scatter_dimension=0, tiled=True)]
    pallas_call x0 -> x12, Pallas kernels: none -> 28.2 us  [the longest x11 16.5 us: call(): pl.pallas_call(body, out_shape=outs, in_specs=specs or [VMEM] * len(args)...]
    dot_general x8 -> x0, matrix products: 26.9 us -> none  [the longest x1 7.7 us: on_device(): jnp.einsum('ksf,fd->ksd', theirs, down, preferred_element_type=F32)]
    unnamed x8 -> x48, local copies, waits for them, and re-layouts: 0.02 us -> 8.87 us
  transfers between devices with their start and end apart: 9 -> 33, of which waited for: 6 -> 21; matrix products, arithmetic and copies ran while one was open for 10% -> 10% of each run, Pallas kernels for 0% -> 10%
where the time goes in v2:
time: 216 us; the launch traced here: 215 us
  waiting for transfers between devices  81 us (38%)
  starting transfers between devices  79 us (37%)
  Pallas kernels  28.2 us (13%)
  other arithmetic  13.1 us (6%)
  local copies, waits for them, and re-layouts  12.4 us (6%)
    ppermute x22, waiting for transfers between devices, moved_by(): return lax.ppermute(x, axes, [(i, (i + step) % n) for i in range(n)])  63.3 us
    ppermute x22, starting transfers between devices, moved_by(): return lax.ppermute(x, axes, [(i, (i + step) % n) for i in range(n)])  39.7 us
    all_to_all x6, starting transfers between devices, exchanged(): return lax.all_to_all(x, axes, 0, 0, tiled=True)  32.3 us
    pallas_call x11, Pallas kernels, call(): pl.pallas_call(body, out_shape=outs, in_specs=specs or [VMEM] * len(args)...  16.5 us
    pallas_call x1, Pallas kernels, teacher_terms(): pl.pallas_call(teacher_body, grid_spec=pltpu.PrefetchScalarGridSpec(num_s...  11.7 us
    all_to_all x6, waiting for transfers between devices, exchanged(): return lax.all_to_all(x, axes, 0, 0, tiled=True)  11.6 us
    unnamed x48, local copies, waits for them, and re-layouts  8.87 us
    ppermute x5, starting transfers between devices, swapped(): return lax.ppermute(x, axis, [(0, 1), (1, 0)])  7.09 us
  transfers between devices with their start and end apart: 33, of which 21 were waited for; matrix products, arithmetic and copies ran while one was open for 10% of the time, Pallas kernels for 10%

profile of v2, /device:TPU:46, one launch (start us, length us, event | category | flops | bytes accessed | tf_op | source)
XLA Modules:
  0.0 214.6 jit_solution(15140069341474272325)
XLA Ops:
  0.7 1.7 copy-done.2
  2.3 0.8 copy-done.7
  3.2 1.5 shard_map.86
  4.6 4.9 %all-to-all-start = ((bf16[4,4,128,256]{3,2,1,0:T(8,128)(2,1)}), bf16[4,4,128,256]{3,2,1,0:T(8,128)(2,1)S(1)}, u32[]{:S(2)}, u32[]{:S(2)}) async-start(bf16[4,4,128,256]{3,2,1,0:T(8,128)(2,1)} %shard_map.86), calls=%async_computation | async-start | bytes 2097152 | tf_op jit(solution)/shard_map/all_to_all | solution.py:45
  10.2 11.7 %shard_map.87 = (bf16[4,2,4,128,512]{4,3,2,1,0:T(8,128)(2,1)}, bf16[4,2,4,128,512]{4,3,2,1,0:T(8,128)(2,1)}) custom-call(s32[2]{0:T(128)} %pad_add_fusion.at_ref.y_ref, bf16[4,448,128]{2,1,0:T(8,128)(2,1)} %bitcast.75, bf16[448,8192]{1,0:T(8,128)(2,1)} %w_ref.4), custom_call_target="tpu_custom_call" | custom-call | flops 1 | bytes 1 | tf_op jit(solution)/shard_map/pallas_call | solution.py:77
  21.9 1.3 all-to-all-done.x_ref
  24.0 6.3 %collective-permute-start.1 = (bf16[256,512]{1,0:T(8,128)(2,1)}, bf16[256,512]{1,0:T(8,128)(2,1)}, u32[]{:S(2)}, u32[]{:S(2)}) collective-permute-start(bf16[256,512]{1,0:T(8,128)(2,1)} %param.13), channel_id=1, source_target_pairs={{0,128},{128,0},{1,129},{129,1},{2,130},{130,2},{3,131},{131,3},{4... | collective-permute-start | bytes 786440 | tf_op jit(solution)/shard_map/ppermute | solution.py:41
  31.1 1.1 collective-permute-start.5
  32.3 2.1 collective-permute-start.6
  34.4 4.4 %all-to-all-start.1 = ((bf16[4,128,256]{2,1,0:T(8,128)(2,1)}), bf16[4,128,256]{2,1,0:T(8,128)(2,1)S(1)}, u32[]{:S(2)}, u32[]{:S(2)}) async-start(bf16[4,128,256]{2,1,0:T(8,128)(2,1)} %bitcast.21), calls=%async_computation.1 | async-start | bytes 524288 | tf_op jit(solution)/shard_map/all_to_all | solution.py:45
  38.7 3.1 %fusion.9 = (bf16[1,2,4,128,512]{4,3,2,1,0:T(8,128)(2,1)}, bf16[1,2,4,128,512]{4,3,2,1,0:T(8,128)(2,1)S(1)}, bf16[1,2,4,128,512]{4,3,2,1,0:T(8,128)(2,1)S(1)}) fusion(bf16[4,2,4,128,512]{4,3,2,1,0:T(8,128)(2,1)} %get-tuple-element.44), kind=kLoop, calls=%fused_computation.50 | loop fusion | bytes 6291456 | tf_op jit(solution)/shard_map/slice | solution.py:227
  41.9 2.8 %fusion.5 = (bf16[4,128,512]{2,1,0:T(8,128)(2,1)}, bf16[4,128,512]{2,1,0:T(8,128)(2,1)}) fusion(bf16[4,8,128,512]{3,2,1,0:T(8,128)(2,1)} %collective-permute-done, bf16[4,8,128,512]{3,2,1,0:T(8,128)(2,1)} %bitcast.74), kind=kLoop, calls=%fused_computation.19 | loop fusion | flops 2097152 | bytes 3145728 | tf_op jit(solution)/shard_map/convert_element_type | solution.py:212
  44.9 1.8 collective-permute-start.3
  46.7 1.2 all-to-all-done.1.x_ref
  48.7 6.0 %all-to-all-start.2 = ((bf16[4,128,256]{2,1,0:T(8,128)(2,1)}), bf16[4,128,256]{2,1,0:T(8,128)(2,1)S(1)}, u32[]{:S(2)}, u32[]{:S(2)}) async-start(bf16[4,128,256]{2,1,0:T(8,128)(2,1)} %shard_map.89), calls=%async_computation.2 | async-start | bytes 524288 | tf_op jit(solution)/shard_map/all_to_all | solution.py:45
  54.7 2.2 %convert_add_fusion.1 = (f32[8,128,512]{2,1,0:T(8,128)S(1)}, f32[8,128,512]{2,1,0:T(8,128)S(1)}) fusion(bf16[4,8,128,512]{3,2,1,0:T(8,128)(2,1)} %collective-permute-done, bf16[1,2,4,128,512]{4,3,2,1,0:T(8,128)(2,1)S(1)} %get-tuple-element.87, bf16[1,2,4,128,512]{4,3,2,1,0:T(8,128)(2,1)S(1)} %get-tuple-element.88), kind=kLoop, calls=%fused_computation.3 | loop fusion | flops 3145728 | bytes 8388608 | tf_op jit(solution)/shard_map/add | solution.py:186
  57.1 0.9 collective-permute-done.2
  58.8 1.5 collective-permute-start.8
  60.3 1.5 fusion.2
  61.8 2.5 %collective-permute-start.9 = (bf16[256,512]{1,0:T(8,128)(2,1)}, bf16[256,512]{1,0:T(8,128)(2,1)S(1)}, u32[]{:S(2)}, u32[]{:S(2)}) collective-permute-start(bf16[256,512]{1,0:T(8,128)(2,1)} %collective-permute-done.1), channel_id=1, source_target_pairs={{0,16},{16,32},{32,48},{48,0},{1,17},{17,33},{33,49},{49,1},{2,18}... | collective-permute-start | bytes 786440 | tf_op jit(solution)/shard_map/ppermute | solution.py:37
  64.3 1.1 pad_maximum_fusion.1
  65.4 1.1 pad_maximum_fusion
  66.6 5.3 %collective-permute-done.7 = bf16[256,512]{1,0:T(8,128)(2,1)S(1)} collective-permute-done((bf16[256,512]{1,0:T(8,128)(2,1)}, bf16[256,512]{1,0:T(8,128)(2,1)S(1)}, u32[]{:S(2)}, u32[]{:S(2)}) %collective-permute-start.7) | collective-permute-done | bytes 262176 | tf_op jit(solution)/shard_map/ppermute | solution.py:37
  73.2 2.1 %collective-permute-start.15 = (bf16[8,128,512]{2,1,0:T(8,128)(2,1)}, bf16[8,128,512]{2,1,0:T(8,128)(2,1)S(1)}, u32[]{:S(2)}, u32[]{:S(2)}) collective-permute-start(bf16[8,128,512]{2,1,0:T(8,128)(2,1)} %pad_maximum_fusion.1), channel_id=1, source_target_pairs={{0,12},{4,0},{8,4},{12,8},{1,13},{5,1},{9,5},{13,9},{2,14},{6,2},{... | collective-permute-start | bytes 3145736 | tf_op jit(solution)/shard_map/ppermute | solution.py:37
  75.3 1.0 bitcast_dynamic-update-slice_fusion.7
  76.4 1.0 bitcast_dynamic-update-slice_fusion.6
  77.3 1.0 bitcast_dynamic-update-slice_fusion.5
  78.3 1.0 bitcast_dynamic-update-slice_fusion.3
  79.3 1.0 bitcast_dynamic-update-slice_fusion.1
  80.4 15.2 %collective-permute-done.14 = bf16[8,128,512]{2,1,0:T(8,128)(2,1)S(1)} collective-permute-done((bf16[8,128,512]{2,1,0:T(8,128)(2,1)}, bf16[8,128,512]{2,1,0:T(8,128)(2,1)S(1)}, u32[]{:S(2)}, u32[]{:S(2)}) %collective-permute-start.14) | collective-permute-done | bytes 1048608 | tf_op jit(solution)/shard_map/ppermute | solution.py:37
  96.4 2.8 %fusion.1 = bf16[8,128,512]{2,1,0:T(8,128)(2,1)} fusion(bf16[8,128,512]{2,1,0:T(8,128)(2,1)S(1)} %collective-permute-done.15, bf16[8,128,512]{2,1,0:T(8,128)(2,1)S(1)} %collective-permute-done.14, bf16[4,8,128,512]{3,2,1,0:T(8,128)(2,1)} %collective-permute-done, bf16[1,2,4,128,512]{4,3,2,1,0:T(8,128)(2,1)S(1)} %copy-done.12), kind=kLoop, calls=%fused_computation.2 | loop fusion | flops 4194304 | bytes 5242880 | tf_op jit(solution)/shard_map/convert_element_type | solution.py:227
  99.2 6.6 %all-to-all-start.3 = ((bf16[8,128,512]{2,1,0:T(8,128)(2,1)}), bf16[8,128,512]{2,1,0:T(8,128)(2,1)}, u32[]{:S(2)}, u32[]{:S(2)}) async-start(bf16[8,128,512]{2,1,0:T(8,128)(2,1)} %fusion.1), calls=%async_computation.3 | async-start | bytes 2097152 | tf_op jit(solution)/shard_map/all_to_all | solution.py:45
  105.9 3.0 %collective-permute-start.10 = (bf16[4,128,256]{2,1,0:T(8,128)(2,1)S(1)}, bf16[4,128,256]{2,1,0:T(8,128)(2,1)S(1)}, u32[]{:S(2)}, u32[]{:S(2)}) collective-permute-start(bf16[4,128,256]{2,1,0:T(8,128)(2,1)S(1)} %copy-done.14), channel_id=1, source_target_pairs={{0,12},{4,0},{8,4},{12,8},{1,13},{5,1},{9,5},{13,9},{2,14},{6,2},{... | collective-permute-start | bytes 786440 | tf_op jit(solution)/shard_map/ppermute | solution.py:37
  108.9 2.1 collective-permute-start.11
  111.1 2.6 %collective-permute-start.12 = (bf16[4,128,256]{2,1,0:T(8,128)(2,1)S(1)}, bf16[4,128,256]{2,1,0:T(8,128)(2,1)S(1)}, u32[]{:S(2)}, u32[]{:S(2)}) collective-permute-start(bf16[4,128,256]{2,1,0:T(8,128)(2,1)S(1)} %copy-done.14), channel_id=1, source_target_pairs={{0,4},{4,8},{8,12},{12,0},{1,5},{5,9},{9,13},{13,1},{2,6},{6,10},{... | collective-permute-start | bytes 786440 | tf_op jit(solution)/shard_map/ppermute | solution.py:37
  113.7 2.0 collective-permute-done.10
  115.7 3.4 %collective-permute-done.11 = bf16[4,128,256]{2,1,0:T(8,128)(2,1)S(1)} collective-permute-done((bf16[4,128,256]{2,1,0:T(8,128)(2,1)S(1)}, bf16[4,128,256]{2,1,0:T(8,128)(2,1)S(1)}, u32[]{:S(2)}, u32[]{:S(2)}) %collective-permute-start.11) | collective-permute-done | bytes 262176 | tf_op jit(solution)/shard_map/ppermute | solution.py:37
  120.0 2.3 %shard_map.90.mapped_ref = f32[128,512]{1,0:T(8,128)S(1)} custom-call(s32[16]{0:T(128)S(1)} %fusion.6.at_ref, bf16[16,128,256]{2,1,0:T(8,128)(2,1)S(1)} %constant_dynamic-update-slice_fusion.h_ref, bf16[8,256,512]{2,1,0:T(8,128)(2,1)S(1)} %bitcast_dynamic-update-slice_fusion.one_ref, bf16[8,256,512]{2,1,0:T(8,128)(2,1)} %collective-permute-done.13.two_ref), custom_call_target="tpu_custom_call" | custom-call | flops 1 | bytes 1 | tf_op jit(solution)/shard_map/pallas_call | solution.py:25
  122.4 8.2 %all-to-all-done.3.terms_ref = bf16[8,128,512]{2,1,0:T(8,128)(2,1)} async-done(((bf16[8,128,512]{2,1,0:T(8,128)(2,1)}), bf16[8,128,512]{2,1,0:T(8,128)(2,1)}, u32[]{:S(2)}, u32[]{:S(2)}) %all-to-all-start.3) | async-done | bytes 1048608 | tf_op jit(solution)/shard_map/all_to_all | solution.py:45
  130.6 3.4 %shard_map.91 = (bf16[128,512]{1,0:T(8,128)(2,1)S(1)}, bf16[4,4,128,256]{3,2,1,0:T(8,128)(2,1)S(1)}) custom-call(s32[16]{0:T(128)S(1)} %fusion.6.at_ref, f32[128,512]{1,0:T(8,128)S(1)} %shard_map.90.mapped_ref, bf16[128,512]{1,0:T(8,128)(2,1)S(1)} %copy-done.6, bf16[8,128,512]{2,1,0:T(8,128)(2,1)} %all-to-all-done.3.terms_ref, ...), custom_call_target="tpu_custom_call" | custom-call | flops 1 | bytes 1 | tf_op jit(solution)/shard_map/pallas_call | solution.py:25
  133.9 1.3 shard_map.92
  135.4 2.3 %collective-permute-start.16 = (bf16[4,128,256]{2,1,0:T(8,128)(2,1)S(1)}, bf16[4,128,256]{2,1,0:T(8,128)(2,1)S(1)}, u32[]{:S(2)}, u32[]{:S(2)}) collective-permute-start(bf16[4,128,256]{2,1,0:T(8,128)(2,1)S(1)} %get-tuple-element.93), channel_id=1, source_target_pairs={{0,4},{4,8},{8,12},{12,0},{1,5},{5,9},{9,13},{13,1},{2,6},{6,10},{... | collective-permute-start | bytes 786440 | tf_op jit(solution)/shard_map/ppermute | solution.py:37
  137.8 2.4 %collective-permute-start.18 = (bf16[4,128,256]{2,1,0:T(8,128)(2,1)S(1)}, bf16[4,128,256]{2,1,0:T(8,128)(2,1)S(1)}, u32[]{:S(2)}, u32[]{:S(2)}) collective-permute-start(bf16[4,128,256]{2,1,0:T(8,128)(2,1)S(1)} %get-tuple-element.92), channel_id=1, source_target_pairs={{0,8},{4,12},{8,0},{12,4},{1,9},{5,13},{9,1},{13,5},{2,10},{6,14},... | collective-permute-start | bytes 786440 | tf_op jit(solution)/shard_map/ppermute | solution.py:37
  140.2 2.3 %collective-permute-start.19 = (bf16[4,128,256]{2,1,0:T(8,128)(2,1)S(1)}, bf16[4,128,256]{2,1,0:T(8,128)(2,1)S(1)}, u32[]{:S(2)}, u32[]{:S(2)}) collective-permute-start(bf16[4,128,256]{2,1,0:T(8,128)(2,1)S(1)} %get-tuple-element.91), channel_id=1, source_target_pairs={{0,12},{4,0},{8,4},{12,8},{1,13},{5,1},{9,5},{13,9},{2,14},{6,2},{... | collective-permute-start | bytes 786440 | tf_op jit(solution)/shard_map/ppermute | solution.py:37
  142.5 1.3 shard_map.93
  145.3 3.2 %collective-permute-done.18.refs_2_ = bf16[4,128,256]{2,1,0:T(8,128)(2,1)S(1)} collective-permute-done((bf16[4,128,256]{2,1,0:T(8,128)(2,1)S(1)}, bf16[4,128,256]{2,1,0:T(8,128)(2,1)S(1)}, u32[]{:S(2)}, u32[]{:S(2)}) %collective-permute-start.18) | collective-permute-done | bytes 262176 | tf_op jit(solution)/shard_map/ppermute | solution.py:37
  148.4 4.9 %collective-permute-done.19.refs_3_ = bf16[4,128,256]{2,1,0:T(8,128)(2,1)S(1)} collective-permute-done((bf16[4,128,256]{2,1,0:T(8,128)(2,1)S(1)}, bf16[4,128,256]{2,1,0:T(8,128)(2,1)S(1)}, u32[]{:S(2)}, u32[]{:S(2)}) %collective-permute-start.19) | collective-permute-done | bytes 262176 | tf_op jit(solution)/shard_map/ppermute | solution.py:37
  154.1 5.0 %all-to-all-start.4 = ((bf16[4,128,256]{2,1,0:T(8,128)(2,1)}), bf16[4,128,256]{2,1,0:T(8,128)(2,1)S(1)}, u32[]{:S(2)}, u32[]{:S(2)}) async-start(bf16[4,128,256]{2,1,0:T(8,128)(2,1)} %shard_map.94), calls=%async_computation.4 | async-start | bytes 524288 | tf_op jit(solution)/shard_map/all_to_all | solution.py:45
  159.1 4.4 %collective-permute-start.20 = (bf16[2,256,512]{2,1,0:T(8,128)(2,1)}, bf16[2,256,512]{2,1,0:T(8,128)(2,1)}, u32[]{:S(2)}, u32[]{:S(2)}) collective-permute-start(bf16[2,256,512]{2,1,0:T(8,128)(2,1)} %copy-done.11), channel_id=1, source_target_pairs={{0,16},{16,32},{32,48},{48,0},{1,17},{17,33},{33,49},{49,1},{2,18}... | collective-permute-start | bytes 1572872 | tf_op jit(solution)/shard_map/ppermute | solution.py:37
  163.6 2.0 collective-permute-start.21
  165.6 0.9 all-to-all-done.4.x_ref
  167.2 5.3 %all-to-all-start.5 = ((bf16[4,128,256]{2,1,0:T(8,128)(2,1)}), bf16[4,128,256]{2,1,0:T(8,128)(2,1)S(1)}, u32[]{:S(2)}, u32[]{:S(2)}) async-start(bf16[4,128,256]{2,1,0:T(8,128)(2,1)} %shard_map.95), calls=%async_computation.5 | async-start | bytes 524288 | tf_op jit(solution)/shard_map/all_to_all | solution.py:45
  172.6 13.7 %collective-permute-done.20.refs_1_ = bf16[2,256,512]{2,1,0:T(8,128)(2,1)} collective-permute-done((bf16[2,256,512]{2,1,0:T(8,128)(2,1)}, bf16[2,256,512]{2,1,0:T(8,128)(2,1)}, u32[]{:S(2)}, u32[]{:S(2)}) %collective-permute-start.20) | collective-permute-done | bytes 524320 | tf_op jit(solution)/shard_map/ppermute | solution.py:37
  186.2 3.7 %collective-permute-done.22.refs_3_ = bf16[2,256,512]{2,1,0:T(8,128)(2,1)} collective-permute-done((bf16[2,256,512]{2,1,0:T(8,128)(2,1)}, bf16[2,256,512]{2,1,0:T(8,128)(2,1)}, u32[]{:S(2)}, u32[]{:S(2)}) %collective-permute-start.22) | collective-permute-done | bytes 524320 | tf_op jit(solution)/shard_map/ppermute | solution.py:37
  189.9 1.2 collective-permute-start.23
  191.1 1.3 collective-permute-start.24
  192.5 2.6 %collective-permute-start.25 = (bf16[4,128,256]{2,1,0:T(8,128)(2,1)S(1)}, bf16[4,128,256]{2,1,0:T(8,128)(2,1)S(1)}, u32[]{:S(2)}, u32[]{:S(2)}) collective-permute-start(bf16[4,128,256]{2,1,0:T(8,128)(2,1)S(1)} %all-to-all-done.5.refs_0_), channel_id=1, source_target_pairs={{0,4},{4,8},{8,12},{12,0},{1,5},{5,9},{9,13},{13,1},{2,6},{6,10},{... | collective-permute-start | bytes 786440 | tf_op jit(solution)/shard_map/ppermute | solution.py:37
  195.1 1.6 shard_map.97
  197.3 0.8 collective-permute-done.23.refs_1_
  198.1 6.4 %collective-permute-done.24.refs_2_ = bf16[4,128,256]{2,1,0:T(8,128)(2,1)S(1)} collective-permute-done((bf16[4,128,256]{2,1,0:T(8,128)(2,1)S(1)}, bf16[4,128,256]{2,1,0:T(8,128)(2,1)S(1)}, u32[]{:S(2)}, u32[]{:S(2)}) %collective-permute-start.24) | collective-permute-done | bytes 262176 | tf_op jit(solution)/shard_map/ppermute | solution.py:37
  204.6 1.0 collective-permute-done.25.refs_3_
  205.6 2.0 shard_map.96
  207.6 6.1 %collective-permute-done.26 = bf16[256,512]{1,0:T(8,128)(2,1)S(1)} collective-permute-done((bf16[256,512]{1,0:T(8,128)(2,1)S(1)}, bf16[256,512]{1,0:T(8,128)(2,1)S(1)}, u32[]{:S(2)}, u32[]{:S(2)}) %collective-permute-start.26) | collective-permute-done | bytes 262176 | tf_op jit(solution)/shard_map/ppermute | solution.py:41
  213.7 0.9 convert_add_fusion.3
  (79 shorter events, 11.3 us)
Async XLA Ops:
  0.6 46.1 %copy-start = (bf16[128,4096]{1,0:T(8,128)(2,1)S(1)}, bf16[128,4096]{1,0:T(8,128)(2,1)}, u32[]{:S(2)}) copy-start(bf16[128,4096]{1,0:T(8,128)(2,1)} %param.12) | copy-start | bytes 3145732
  0.6 1.7 copy-start.2
  2.3 0.8 copy-start.7
  4.6 18.5 %all-to-all-start = ((bf16[4,4,128,256]{3,2,1,0:T(8,128)(2,1)}), bf16[4,4,128,256]{3,2,1,0:T(8,128)(2,1)S(1)}, u32[]{:S(2)}, u32[]{:S(2)}) async-start(bf16[4,4,128,256]{3,2,1,0:T(8,128)(2,1)} %shard_map.86), calls=%async_computation | async-start | bytes 2097152 | tf_op jit(solution)/shard_map/all_to_all | solution.py:45
  24.0 17.9 %collective-permute-start = (bf16[4,8,128,512]{3,2,1,0:T(8,128)(2,1)}, bf16[4,8,128,512]{3,2,1,0:T(8,128)(2,1)}, u32[]{:S(2)}, u32[]{:S(2)}) collective-permute-start(bf16[4,8,128,512]{3,2,1,0:T(8,128)(2,1)} %bitcast.76), channel_id=1, source_target_pairs={{0,64},{64,0},{1,65},{65,1},{2,66},{66,2},{3,67},{67,3},{4,68},{68... | collective-permute-start | bytes 12582920 | tf_op jit(solution)/shard_map/ppermute | solution.py:41
  24.0 20.7 %collective-permute-start.1 = (bf16[256,512]{1,0:T(8,128)(2,1)}, bf16[256,512]{1,0:T(8,128)(2,1)}, u32[]{:S(2)}, u32[]{:S(2)}) collective-permute-start(bf16[256,512]{1,0:T(8,128)(2,1)} %param.13), channel_id=1, source_target_pairs={{0,128},{128,0},{1,129},{129,1},{2,130},{130,2},{3,131},{131,3},{4... | collective-permute-start | bytes 786440 | tf_op jit(solution)/shard_map/ppermute | solution.py:41
  30.3 31.5 %collective-permute-start.4 = (bf16[256,512]{1,0:T(8,128)(2,1)}, bf16[256,512]{1,0:T(8,128)(2,1)}, u32[]{:S(2)}, u32[]{:S(2)}) collective-permute-start(bf16[256,512]{1,0:T(8,128)(2,1)} %param.13), channel_id=1, source_target_pairs={{0,48},{16,0},{32,16},{48,32},{1,49},{17,1},{33,17},{49,33},{2,50}... | collective-permute-start | bytes 786440 | tf_op jit(solution)/shard_map/ppermute | solution.py:37
  31.1 35.4 %collective-permute-start.5 = (bf16[256,512]{1,0:T(8,128)(2,1)}, bf16[256,512]{1,0:T(8,128)(2,1)}, u32[]{:S(2)}, u32[]{:S(2)}) collective-permute-start(bf16[256,512]{1,0:T(8,128)(2,1)} %param.13), channel_id=1, source_target_pairs={{0,32},{16,48},{32,0},{48,16},{1,33},{17,49},{33,1},{49,17},{2,34}... | collective-permute-start | bytes 786440 | tf_op jit(solution)/shard_map/ppermute | solution.py:37
  32.3 34.3 %collective-permute-start.6 = (bf16[256,512]{1,0:T(8,128)(2,1)}, bf16[256,512]{1,0:T(8,128)(2,1)}, u32[]{:S(2)}, u32[]{:S(2)}) collective-permute-start(bf16[256,512]{1,0:T(8,128)(2,1)} %param.13), channel_id=1, source_target_pairs={{0,16},{16,32},{32,48},{48,0},{1,17},{17,33},{33,49},{49,1},{2,18}... | collective-permute-start | bytes 786440 | tf_op jit(solution)/shard_map/ppermute | solution.py:37
  34.4 13.6 %all-to-all-start.1 = ((bf16[4,128,256]{2,1,0:T(8,128)(2,1)}), bf16[4,128,256]{2,1,0:T(8,128)(2,1)S(1)}, u32[]{:S(2)}, u32[]{:S(2)}) async-start(bf16[4,128,256]{2,1,0:T(8,128)(2,1)} %bitcast.21), calls=%async_computation.1 | async-start | bytes 524288 | tf_op jit(solution)/shard_map/all_to_all | solution.py:45
  44.7 13.3 %collective-permute-start.2 = (bf16[4,128,512]{2,1,0:T(8,128)(2,1)}, bf16[4,128,512]{2,1,0:T(8,128)(2,1)}, u32[]{:S(2)}, u32[]{:S(2)}) collective-permute-start(bf16[4,128,512]{2,1,0:T(8,128)(2,1)} %get-tuple-element.48), channel_id=1, source_target_pairs={{0,4},{4,8},{8,12},{12,0},{1,5},{5,9},{9,13},{13,1},{2,6},{6,10},{... | collective-permute-start | bytes 1572872 | tf_op jit(solution)/shard_map/ppermute | solution.py:37
  44.9 13.9 %collective-permute-start.3 = (bf16[4,128,512]{2,1,0:T(8,128)(2,1)}, bf16[4,128,512]{2,1,0:T(8,128)(2,1)}, u32[]{:S(2)}, u32[]{:S(2)}) collective-permute-start(bf16[4,128,512]{2,1,0:T(8,128)(2,1)} %get-tuple-element.49), channel_id=1, source_target_pairs={{0,12},{4,0},{8,4},{12,8},{1,13},{5,1},{9,5},{13,9},{2,14},{6,2},{... | collective-permute-start | bytes 1572872 | tf_op jit(solution)/shard_map/ppermute | solution.py:37
  48.7 17.9 %all-to-all-start.2 = ((bf16[4,128,256]{2,1,0:T(8,128)(2,1)}), bf16[4,128,256]{2,1,0:T(8,128)(2,1)S(1)}, u32[]{:S(2)}, u32[]{:S(2)}) async-start(bf16[4,128,256]{2,1,0:T(8,128)(2,1)} %shard_map.89), calls=%async_computation.2 | async-start | bytes 524288 | tf_op jit(solution)/shard_map/all_to_all | solution.py:45
  57.9 14.0 %collective-permute-start.7 = (bf16[256,512]{1,0:T(8,128)(2,1)}, bf16[256,512]{1,0:T(8,128)(2,1)S(1)}, u32[]{:S(2)}, u32[]{:S(2)}) collective-permute-start(bf16[256,512]{1,0:T(8,128)(2,1)} %collective-permute-done.1), channel_id=1, source_target_pairs={{0,48},{16,0},{32,16},{48,32},{1,49},{17,1},{33,17},{49,33},{2,50}... | collective-permute-start | bytes 786440 | tf_op jit(solution)/shard_map/ppermute | solution.py:37
  58.8 13.1 %collective-permute-start.8 = (bf16[256,512]{1,0:T(8,128)(2,1)}, bf16[256,512]{1,0:T(8,128)(2,1)S(1)}, u32[]{:S(2)}, u32[]{:S(2)}) collective-permute-start(bf16[256,512]{1,0:T(8,128)(2,1)} %collective-permute-done.1), channel_id=1, source_target_pairs={{0,32},{16,48},{32,0},{48,16},{1,33},{17,49},{33,1},{49,17},{2,34}... | collective-permute-start | bytes 786440 | tf_op jit(solution)/shard_map/ppermute | solution.py:37
  61.8 10.6 %collective-permute-start.9 = (bf16[256,512]{1,0:T(8,128)(2,1)}, bf16[256,512]{1,0:T(8,128)(2,1)S(1)}, u32[]{:S(2)}, u32[]{:S(2)}) collective-permute-start(bf16[256,512]{1,0:T(8,128)(2,1)} %collective-permute-done.1), channel_id=1, source_target_pairs={{0,16},{16,32},{32,48},{48,0},{1,17},{17,33},{33,49},{49,1},{2,18}... | collective-permute-start | bytes 786440 | tf_op jit(solution)/shard_map/ppermute | solution.py:37
  66.5 29.9 %copy-start.12 = (bf16[1,2,4,128,512]{4,3,2,1,0:T(8,128)(2,1)S(1)}, bf16[1,2,4,128,512]{4,3,2,1,0:T(8,128)(2,1)}, u32[]{:S(2)}) copy-start(bf16[1,2,4,128,512]{4,3,2,1,0:T(8,128)(2,1)} %get-tuple-element.86) | copy-start | bytes 3145732
  66.6 6.1 %copy-start.13 = (bf16[4,128,256]{2,1,0:T(8,128)(2,1)}, bf16[4,128,256]{2,1,0:T(8,128)(2,1)S(1)}, u32[]{:S(2)}) copy-start(bf16[4,128,256]{2,1,0:T(8,128)(2,1)S(1)} %all-to-all-done.2) | copy-start | bytes 786436
  71.9 0.8 copy-start.15
  72.5 0.7 copy-start.17
  72.5 23.2 %collective-permute-start.14 = (bf16[8,128,512]{2,1,0:T(8,128)(2,1)}, bf16[8,128,512]{2,1,0:T(8,128)(2,1)S(1)}, u32[]{:S(2)}, u32[]{:S(2)}) collective-permute-start(bf16[8,128,512]{2,1,0:T(8,128)(2,1)} %pad_maximum_fusion), channel_id=1, source_target_pairs={{0,4},{4,8},{8,12},{12,0},{1,5},{5,9},{9,13},{13,1},{2,6},{6,10},{... | collective-permute-start | bytes 3145736 | tf_op jit(solution)/shard_map/ppermute | solution.py:37
  73.2 23.2 %collective-permute-start.15 = (bf16[8,128,512]{2,1,0:T(8,128)(2,1)}, bf16[8,128,512]{2,1,0:T(8,128)(2,1)S(1)}, u32[]{:S(2)}, u32[]{:S(2)}) collective-permute-start(bf16[8,128,512]{2,1,0:T(8,128)(2,1)} %pad_maximum_fusion.1), channel_id=1, source_target_pairs={{0,12},{4,0},{8,4},{12,8},{1,13},{5,1},{9,5},{13,9},{2,14},{6,2},{... | collective-permute-start | bytes 3145736 | tf_op jit(solution)/shard_map/ppermute | solution.py:37
  75.3 4.0 %copy-start.16 = (bf16[256,512]{1,0:T(8,128)(2,1)S(1)}, bf16[256,512]{1,0:T(8,128)(2,1)}, u32[]{:S(2)}) copy-start(bf16[256,512]{1,0:T(8,128)(2,1)} %copy-done.15) | copy-start | bytes 786436
  75.3 5.0 %copy-start.18 = (bf16[256,512]{1,0:T(8,128)(2,1)S(1)}, bf16[256,512]{1,0:T(8,128)(2,1)}, u32[]{:S(2)}) copy-start(bf16[256,512]{1,0:T(8,128)(2,1)} %copy-done.17) | copy-start | bytes 786436
  80.3 39.7 %collective-permute-start.13 = (bf16[8,256,512]{2,1,0:T(8,128)(2,1)S(1)}, bf16[8,256,512]{2,1,0:T(8,128)(2,1)}, u32[]{:S(2)}, u32[]{:S(2)}) collective-permute-start(bf16[8,256,512]{2,1,0:T(8,128)(2,1)S(1)} %bitcast_dynamic-update-slice_fusion.one_ref), channel_id=1, source_target_pairs={{0,64},{64,0},{1,65},{65,1},{2,66},{66,2},{3,67},{67,3},{4,68},{68... | collective-permute-start | bytes 6291464 | tf_op jit(solution)/shard_map/ppermute | solution.py:41
  99.2 6.7 %copy-start.14 = (bf16[4,128,256]{2,1,0:T(8,128)(2,1)S(1)}, bf16[4,128,256]{2,1,0:T(8,128)(2,1)}, u32[]{:S(2)}) copy-start(bf16[4,128,256]{2,1,0:T(8,128)(2,1)} %copy-done.13) | copy-start | bytes 786436
  99.2 31.4 %all-to-all-start.3 = ((bf16[8,128,512]{2,1,0:T(8,128)(2,1)}), bf16[8,128,512]{2,1,0:T(8,128)(2,1)}, u32[]{:S(2)}, u32[]{:S(2)}) async-start(bf16[8,128,512]{2,1,0:T(8,128)(2,1)} %fusion.1), calls=%async_computation.3 | async-start | bytes 2097152 | tf_op jit(solution)/shard_map/all_to_all | solution.py:45
  105.9 9.8 %collective-permute-start.10 = (bf16[4,128,256]{2,1,0:T(8,128)(2,1)S(1)}, bf16[4,128,256]{2,1,0:T(8,128)(2,1)S(1)}, u32[]{:S(2)}, u32[]{:S(2)}) collective-permute-start(bf16[4,128,256]{2,1,0:T(8,128)(2,1)S(1)} %copy-done.14), channel_id=1, source_target_pairs={{0,12},{4,0},{8,4},{12,8},{1,13},{5,1},{9,5},{13,9},{2,14},{6,2},{... | collective-permute-start | bytes 786440 | tf_op jit(solution)/shard_map/ppermute | solution.py:37
  108.9 10.2 %collective-permute-start.11 = (bf16[4,128,256]{2,1,0:T(8,128)(2,1)S(1)}, bf16[4,128,256]{2,1,0:T(8,128)(2,1)S(1)}, u32[]{:S(2)}, u32[]{:S(2)}) collective-permute-start(bf16[4,128,256]{2,1,0:T(8,128)(2,1)S(1)} %copy-done.14), channel_id=1, source_target_pairs={{0,8},{4,12},{8,0},{12,4},{1,9},{5,13},{9,1},{13,5},{2,10},{6,14},... | collective-permute-start | bytes 786440 | tf_op jit(solution)/shard_map/ppermute | solution.py:37
  111.1 8.9 %collective-permute-start.12 = (bf16[4,128,256]{2,1,0:T(8,128)(2,1)S(1)}, bf16[4,128,256]{2,1,0:T(8,128)(2,1)S(1)}, u32[]{:S(2)}, u32[]{:S(2)}) collective-permute-start(bf16[4,128,256]{2,1,0:T(8,128)(2,1)S(1)} %copy-done.14), channel_id=1, source_target_pairs={{0,4},{4,8},{8,12},{12,0},{1,5},{5,9},{9,13},{13,1},{2,6},{6,10},{... | collective-permute-start | bytes 786440 | tf_op jit(solution)/shard_map/ppermute | solution.py:37
  120.0 10.6 %copy-start.6 = (bf16[128,512]{1,0:T(8,128)(2,1)S(1)}, bf16[128,512]{1,0:T(8,128)(2,1)}, u32[]{:S(2)}) copy-start(bf16[128,512]{1,0:T(8,128)(2,1)} %resid_ref.1) | copy-start | bytes 393220
  135.2 7.3 %collective-permute-start.17 = (bf16[8,256,512]{2,1,0:T(8,128)(2,1)S(1)}, bf16[8,256,512]{2,1,0:T(8,128)(2,1)S(1)}, u32[]{:S(2)}, u32[]{:S(2)}) collective-permute-start(bf16[8,256,512]{2,1,0:T(8,128)(2,1)S(1)} %shard_map.92), channel_id=1, source_target_pairs={{0,64},{64,0},{1,65},{65,1},{2,66},{66,2},{3,67},{67,3},{4,68},{68... | collective-permute-start | bytes 6291464 | tf_op jit(solution)/shard_map/ppermute | solution.py:41
  135.4 9.8 %collective-permute-start.16 = (bf16[4,128,256]{2,1,0:T(8,128)(2,1)S(1)}, bf16[4,128,256]{2,1,0:T(8,128)(2,1)S(1)}, u32[]{:S(2)}, u32[]{:S(2)}) collective-permute-start(bf16[4,128,256]{2,1,0:T(8,128)(2,1)S(1)} %get-tuple-element.93), channel_id=1, source_target_pairs={{0,4},{4,8},{8,12},{12,0},{1,5},{5,9},{9,13},{13,1},{2,6},{6,10},{... | collective-permute-start | bytes 786440 | tf_op jit(solution)/shard_map/ppermute | solution.py:37
  137.8 10.7 %collective-permute-start.18 = (bf16[4,128,256]{2,1,0:T(8,128)(2,1)S(1)}, bf16[4,128,256]{2,1,0:T(8,128)(2,1)S(1)}, u32[]{:S(2)}, u32[]{:S(2)}) collective-permute-start(bf16[4,128,256]{2,1,0:T(8,128)(2,1)S(1)} %get-tuple-element.92), channel_id=1, source_target_pairs={{0,8},{4,12},{8,0},{12,4},{1,9},{5,13},{9,1},{13,5},{2,10},{6,14},... | collective-permute-start | bytes 786440 | tf_op jit(solution)/shard_map/ppermute | solution.py:37
  140.2 13.1 %collective-permute-start.19 = (bf16[4,128,256]{2,1,0:T(8,128)(2,1)S(1)}, bf16[4,128,256]{2,1,0:T(8,128)(2,1)S(1)}, u32[]{:S(2)}, u32[]{:S(2)}) collective-permute-start(bf16[4,128,256]{2,1,0:T(8,128)(2,1)S(1)} %get-tuple-element.91), channel_id=1, source_target_pairs={{0,12},{4,0},{8,4},{12,8},{1,13},{5,1},{9,5},{13,9},{2,14},{6,2},{... | collective-permute-start | bytes 786440 | tf_op jit(solution)/shard_map/ppermute | solution.py:37
  143.8 0.8 copy-start.4
  144.6 8.7 %copy-start.9 = (bf16[2,256,512]{2,1,0:T(8,128)(2,1)}, bf16[2,256,512]{2,1,0:T(8,128)(2,1)S(1)}, u32[]{:S(2)}) copy-start(bf16[2,256,512]{2,1,0:T(8,128)(2,1)S(1)} %get-tuple-element.75) | copy-start | bytes 1572868
  144.6 8.7 %copy-start.10 = (bf16[2,256,512]{2,1,0:T(8,128)(2,1)}, bf16[2,256,512]{2,1,0:T(8,128)(2,1)S(1)}, u32[]{:S(2)}) copy-start(bf16[2,256,512]{2,1,0:T(8,128)(2,1)S(1)} %get-tuple-element.74) | copy-start | bytes 1572868
  144.6 8.7 %copy-start.11 = (bf16[2,256,512]{2,1,0:T(8,128)(2,1)}, bf16[2,256,512]{2,1,0:T(8,128)(2,1)S(1)}, u32[]{:S(2)}) copy-start(bf16[2,256,512]{2,1,0:T(8,128)(2,1)S(1)} %get-tuple-element.73) | copy-start | bytes 1572868
  145.3 49.8 %copy-start.5 = (bf16[2,256,512]{2,1,0:T(8,128)(2,1)S(1)}, bf16[2,256,512]{2,1,0:T(8,128)(2,1)}, u32[]{:S(2)}) copy-start(bf16[2,256,512]{2,1,0:T(8,128)(2,1)} %copy-done.4) | copy-start | bytes 1572868
  154.1 51.5 %copy-start.3 = (bf16[256,4096]{1,0:T(8,128)(2,1)S(1)}, bf16[256,4096]{1,0:T(8,128)(2,1)}, u32[]{:S(2)}) copy-start(bf16[256,4096]{1,0:T(8,128)(2,1)} %w_ref.5) | copy-start | bytes 6291460
  154.1 51.5 %copy-start.8 = (s32[2]{0:T(128)S(1)}, s32[2]{0:T(128)}, u32[]{:S(2)}) copy-start(s32[2]{0:T(128)} %pad_add_fusion.at_ref.y_ref) | copy-start | bytes 28
  154.1 12.4 %all-to-all-start.4 = ((bf16[4,128,256]{2,1,0:T(8,128)(2,1)}), bf16[4,128,256]{2,1,0:T(8,128)(2,1)S(1)}, u32[]{:S(2)}, u32[]{:S(2)}) async-start(bf16[4,128,256]{2,1,0:T(8,128)(2,1)} %shard_map.94), calls=%async_computation.4 | async-start | bytes 524288 | tf_op jit(solution)/shard_map/all_to_all | solution.py:45
  159.1 27.1 %collective-permute-start.20 = (bf16[2,256,512]{2,1,0:T(8,128)(2,1)}, bf16[2,256,512]{2,1,0:T(8,128)(2,1)}, u32[]{:S(2)}, u32[]{:S(2)}) collective-permute-start(bf16[2,256,512]{2,1,0:T(8,128)(2,1)} %copy-done.11), channel_id=1, source_target_pairs={{0,16},{16,32},{32,48},{48,0},{1,17},{17,33},{33,49},{49,1},{2,18}... | collective-permute-start | bytes 1572872 | tf_op jit(solution)/shard_map/ppermute | solution.py:37
  163.6 22.7 %collective-permute-start.21 = (bf16[2,256,512]{2,1,0:T(8,128)(2,1)}, bf16[2,256,512]{2,1,0:T(8,128)(2,1)}, u32[]{:S(2)}, u32[]{:S(2)}) collective-permute-start(bf16[2,256,512]{2,1,0:T(8,128)(2,1)} %copy-done.10), channel_id=1, source_target_pairs={{0,32},{16,48},{32,0},{48,16},{1,33},{17,49},{33,1},{49,17},{2,34}... | collective-permute-start | bytes 1572872 | tf_op jit(solution)/shard_map/ppermute | solution.py:37
  165.6 24.3 %collective-permute-start.22 = (bf16[2,256,512]{2,1,0:T(8,128)(2,1)}, bf16[2,256,512]{2,1,0:T(8,128)(2,1)}, u32[]{:S(2)}, u32[]{:S(2)}) collective-permute-start(bf16[2,256,512]{2,1,0:T(8,128)(2,1)} %copy-done.9), channel_id=1, source_target_pairs={{0,48},{16,0},{32,16},{48,32},{1,49},{17,1},{33,17},{49,33},{2,50}... | collective-permute-start | bytes 1572872 | tf_op jit(solution)/shard_map/ppermute | solution.py:37
  167.2 22.7 %all-to-all-start.5 = ((bf16[4,128,256]{2,1,0:T(8,128)(2,1)}), bf16[4,128,256]{2,1,0:T(8,128)(2,1)S(1)}, u32[]{:S(2)}, u32[]{:S(2)}) async-start(bf16[4,128,256]{2,1,0:T(8,128)(2,1)} %shard_map.95), calls=%async_computation.5 | async-start | bytes 524288 | tf_op jit(solution)/shard_map/all_to_all | solution.py:45
  189.9 8.2 %collective-permute-start.23 = (bf16[4,128,256]{2,1,0:T(8,128)(2,1)S(1)}, bf16[4,128,256]{2,1,0:T(8,128)(2,1)S(1)}, u32[]{:S(2)}, u32[]{:S(2)}) collective-permute-start(bf16[4,128,256]{2,1,0:T(8,128)(2,1)S(1)} %all-to-all-done.5.refs_0_), channel_id=1, source_target_pairs={{0,12},{4,0},{8,4},{12,8},{1,13},{5,1},{9,5},{13,9},{2,14},{6,2},{... | collective-permute-start | bytes 786440 | tf_op jit(solution)/shard_map/ppermute | solution.py:37
  191.1 13.4 %collective-permute-start.24 = (bf16[4,128,256]{2,1,0:T(8,128)(2,1)S(1)}, bf16[4,128,256]{2,1,0:T(8,128)(2,1)S(1)}, u32[]{:S(2)}, u32[]{:S(2)}) collective-permute-start(bf16[4,128,256]{2,1,0:T(8,128)(2,1)S(1)} %all-to-all-done.5.refs_0_), channel_id=1, source_target_pairs={{0,8},{4,12},{8,0},{12,4},{1,9},{5,13},{9,1},{13,5},{2,10},{6,14},... | collective-permute-start | bytes 786440 | tf_op jit(solution)/shard_map/ppermute | solution.py:37
  192.5 13.1 %collective-permute-start.25 = (bf16[4,128,256]{2,1,0:T(8,128)(2,1)S(1)}, bf16[4,128,256]{2,1,0:T(8,128)(2,1)S(1)}, u32[]{:S(2)}, u32[]{:S(2)}) collective-permute-start(bf16[4,128,256]{2,1,0:T(8,128)(2,1)S(1)} %all-to-all-done.5.refs_0_), channel_id=1, source_target_pairs={{0,4},{4,8},{8,12},{12,0},{1,5},{5,9},{9,13},{13,1},{2,6},{6,10},{... | collective-permute-start | bytes 786440 | tf_op jit(solution)/shard_map/ppermute | solution.py:37
  196.7 17.9 %copy-start.1 = (bf16[128,4096]{1,0:T(8,128)(2,1)S(1)}, bf16[128,4096]{1,0:T(8,128)(2,1)}, u32[]{:S(2)}) copy-start(bf16[128,4096]{1,0:T(8,128)(2,1)} %param.12) | copy-start | bytes 3145732
  196.7 17.0 %collective-permute-start.26 = (bf16[256,512]{1,0:T(8,128)(2,1)S(1)}, bf16[256,512]{1,0:T(8,128)(2,1)S(1)}, u32[]{:S(2)}, u32[]{:S(2)}) collective-permute-start(bf16[256,512]{1,0:T(8,128)(2,1)S(1)} %get-tuple-element.80), channel_id=1, source_target_pairs={{0,128},{128,0},{1,129},{129,1},{2,130},{130,2},{3,131},{131,3},{4... | collective-permute-start | bytes 786440 | tf_op jit(solution)/shard_map/ppermute | solution.py:41

commit v3 on v2

--- a/solution.py
+++ b/solution.py
@@ -69,19 +69,19 @@
                 ref[0, zh, zl] = part[row : row + tok]
 
 
-def teacher_terms(at, act, w):
+def teacher_terms(at, act, w, first, count):
     _, tok, depth = act.shape
     width = w.shape[1] // 16
-    shape = jax.ShapeDtypeStruct((4, 2, 4, tok, width), BF)
+    shape = jax.ShapeDtypeStruct((count, 2, 4, tok, width), BF)
     out = pl.BlockSpec((1, 2, 2, tok, width), lambda i, at: (i // 2, 0, i % 2, 0, 0))
     terms = pl.pallas_call(
         teacher_body,
         grid_spec=pltpu.PrefetchScalarGridSpec(
             num_scalar_prefetch=1,
-            grid=(8,),
+            grid=(2 * count,),
             in_specs=[
                 pl.BlockSpec((4, depth, tok), lambda i, at: (0, 0, 0)),
-                pl.BlockSpec((depth, 2 * width), lambda i, at: (0, lax.rem(at[0] + 2 + i // 2, 4) * 2 + i % 2)),
+                pl.BlockSpec((depth, 2 * width), lambda i, at: (0, lax.rem(at[0] + first + i // 2, 4) * 2 + i % 2)),
             ],
             out_specs=[out, out],
             scratch_shapes=[pltpu.VMEM((4 * tok, depth), BF)],
@@ -90,7 +90,42 @@
         compiler_params=pltpu.CompilerParams(vmem_limit_bytes=56 * 2**20),
         cost_estimate=COST,
     )(at, jnp.swapaxes(act, 1, 2), w)
-    return [t.reshape(4, 8, tok, width) for t in terms]
+    return [t.reshape(count, 8, tok, width) for t in terms]
+
+
+def far_body(mine_ref, came_ref, up_ref, down_ref):
+    half = up_ref.shape[0]
+    total = mine_ref[0].astype(F32) + came_ref[0].astype(F32)
+    up_ref[...] = total[:half].astype(BF)
+    down_ref[...] = total[half:].astype(BF)
+
+
+def chip_body(*refs):
+    for k in range(3):
+        refs[6 + k][...] = (refs[2 * k][0].astype(F32) + refs[2 * k + 1][0].astype(F32)).astype(BF)
+
+
+def near_body(near_up, near_down, far_up, far_down, up_ref, down_ref):
+    half = far_up.shape[0]
+    up_ref[:half] = (near_up[:half].astype(F32) + far_up[...].astype(F32)).astype(BF)
+    up_ref[half:] = near_up[half:]
+    down_ref[:half] = near_down[:half]
+    down_ref[half:] = (near_down[half:].astype(F32) + far_down[...].astype(F32)).astype(BF)
+
+
+def on_blocks(body, outs, blocks):
+    def spec(shape, at):
+        return pl.BlockSpec(shape, lambda i: at)
+
+    return pl.pallas_call(
+        body,
+        grid=(1,),
+        in_specs=[spec(shape, at) for _, shape, at in blocks],
+        out_specs=[spec(o.shape, (0,) * len(o.shape)) for o in outs],
+        out_shape=outs,
+        compiler_params=pltpu.CompilerParams(vmem_limit_bytes=56 * 2**20),
+        cost_estimate=COST,
+    )(*[a for a, _, _ in blocks])
 
 
 def student_body(a_ref, w_ref, o_ref):
@@ -106,35 +141,53 @@
         o_ref[i] = hidden
 
 
-def mapped_body(at_ref, h_ref, one_ref, two_ref, out_ref):
+def block_of(refs, i):
+    pair, next_, last_, far_one, far_two = refs[5 * (i // 8) : 5 * (i // 8) + 5]
+    x, z = i % 8 // 2, i % 2
+    if x == 2:
+        return (far_one, far_two)[z][...]
+    return {0: pair, 1: next_, 3: last_}[x][z]
+
+
+def mapped_body(at_ref, h_ref, *refs):
+    out_ref, rows_ref = refs[-2:]
     total = None
     for i in range(16):
-        block = (one_ref, two_ref)[i // 8][i % 8]
+        block = block_of(refs, i)
+        rows_ref[i] = block
         term = jnp.dot(h_ref[at_ref[i]], block, preferred_element_type=F32)
         total = term if total is None else total + term
     out_ref[...] = total
 
 
-def err_body(at_ref, mapped_ref, resid_ref, terms_ref, one_ref, two_ref, err_ref, back_ref):
+def err_body(at_ref, mapped_ref, resid_ref, terms_ref, rows_ref, err_ref, back_ref):
     teacher = (resid_ref[...].astype(F32) + added(terms_ref[...])).astype(BF)
-    err = (mapped_ref[...] - teacher.astype(F32)).astype(BF)
-    err_ref[...] = err
+    err_ref[...] = (mapped_ref[...] - teacher.astype(F32)).astype(BF)
+    err = err_ref[...]
     for i in range(16):
-        block = (one_ref, two_ref)[i // 8][i % 8]
         at = at_ref[i]
-        back = lax.dot_general(err, block, NT, preferred_element_type=F32)
+        back = lax.dot_general(err, rows_ref[i], NT, preferred_element_type=F32)
         back_ref[at // 4, lax.rem(at, 4)] = back.astype(BF)
 
 
 def grad_body(scale, first, at_ref, h_ref, err_ref, *refs):
     err = err_ref[...]
-    outs = refs[-4:] if first == 0 else refs
+    if first == 0:
+        near, left, right, far_up, far_down = refs[1:]
+        outs = [near.at[0], near.at[1], left.at[0], left.at[1], far_up, far_down, right.at[0], right.at[1]]
     for i in range(8):
         term = lax.dot_general(h_ref[at_ref[first + i]], err, TN, preferred_element_type=F32) * scale
         if first == 0:
-            outs[i // 2][i % 2] = (term + refs[0][i].astype(F32)).astype(BF)
+            outs[i][...] = (term + refs[0][i].astype(F32)).astype(BF)
         else:
-            outs[0][i] = term.astype(BF)
+            refs[0][i] = term.astype(BF)
+
+
+def grad_near_body(left_ref, right_ref, up_ref, down_ref, up_out, down_out):
+    up_out[0] = (left_ref[0].astype(F32) + up_ref[...].astype(F32)).astype(BF)
+    up_out[1] = left_ref[1]
+    down_out[0] = right_ref[0]
+    down_out[1] = (right_ref[1].astype(F32) + down_ref[...].astype(F32)).astype(BF)
 
 
 def grad_sum_body(*refs):
@@ -187,8 +240,7 @@
     shape = lambda *dims, dtype=BF: jax.ShapeDtypeStruct(dims, dtype)
     here = jnp.stack([y, core]).astype(jnp.int32)
 
-    proj_z = swapped(proj, "zh")
-    rows_x = [proj] + [moved_by(proj, "x", -step) for step in (1, 2, 3)]
+    pair = jnp.stack([proj, swapped(proj, "zh")])
     idx = jnp.stack(
         [
             ((zh + dz) % 2 * 2 + (core + dc) % 2) * 4 + (x + dx) % 4
@@ -205,45 +257,52 @@
     act, part = tied(act, part)
     student = exchanged(part, "y")
 
-    sent, mine = teacher_terms(here, act, down)
+    sent, mine = teacher_terms(here, act, down, 2, 4)
     student = call(sum_body, [shape(1, 4, tok, cols)], [student])[0][0]
     sent, student = tied(sent, student)
     came = swapped(sent, "c")
-    up, down_ = plus(mine[0, :4], came[0, :4]).astype(BF), plus(mine[0, 4:], came[0, 4:]).astype(BF)
-    up, down_, proj_z = tied(up, down_, proj_z)
+    student = exchanged(student, "zl")
+    width = t_resid.shape[1]
+    piece = (1, 8, tok, width)
+    blocks = [(a, piece, (0, 0, 0, 0)) for a in (mine, came)]
+    up, down_ = on_blocks(far_body, [shape(4, tok, width)] * 2, blocks)
     up, down_ = tied(moved_by(up, "y", 1), moved_by(down_, "y", -1))
-    rows_z = [proj_z] + [moved_by(proj_z, "x", -step) for step in (1, 2, 3)]
-    student = exchanged(student, "zl")
-    near = plus(mine[3], came[3])
-    up = jnp.concatenate([near[:4] + up.astype(F32), near[4:]], axis=0).astype(BF)
-    near = plus(mine[1], came[1])
-    down_ = jnp.concatenate([near[:4], near[4:] + down_.astype(F32)], axis=0).astype(BF)
+    blocks = [(a, piece, (d, 0, 0, 0)) for d in (3, 1, 2) for a in (mine, came)]
+    near_up, near_down, chip = on_blocks(chip_body, [shape(8, tok, width)] * 3, blocks)
+    student, near_up, near_down, chip = tied(student, near_up, near_down, chip)
     hidden = call(hidden_body, [shape(4, tok, cols)], [student, resid])[0]
+    ups = call(near_body, [shape(8, tok, width)] * 2, [near_up, near_down, up, down_])
+    hidden, *ups = tied(hidden, *ups)
     hidden = exchanged(hidden, "zl")
-    up, down_, hidden, *rows_x, rows_z[0], rows_z[1], rows_z[2], rows_z[3] = tied(
-        up, down_, hidden, *rows_x, *rows_z
-    )
-    up, down_ = tied(moved_by(up, "y", 1), moved_by(down_, "y", -1))
-    over_y = (plus(mine[2], came[2]) + plus(up, down_)).astype(BF)
-    terms = exchanged(over_y, Z)
-    rows = jnp.stack([r for both in zip(rows_x, rows_z) for r in both])
-    rows = [rows, swapped(rows, "c")]
-    hidden = jnp.concatenate([hidden] + [moved_by(hidden, "y", -step) for step in (1, 2, 3)], axis=0)
-
-    mapped = call(
+    pair = tied(pair, hidden)[0]
+    ups = tied(moved_by(ups[0], "y", 1), moved_by(ups[1], "y", -1))
+
+    next_, last_ = tied(moved_by(pair, "x", -1), moved_by(pair, "x", 1))
+    far_rows = tied(moved_by(next_[0], "x", -1), moved_by(last_[1], "x", 1))
+
+    over = call(terms_body, [shape(8, tok, width)], [chip, *ups])[0]
+    over, hidden = tied(over, hidden)
+    terms = exchanged(over, Z)
+    hidden = jnp.concatenate(
+        [hidden, *tied(*(moved_by(hidden, "y", -step) for step in (1, 2, 3)))], axis=0
+    )
+    rows = [pair, next_, last_, *far_rows]
+    rows = rows + [swapped(r, "c") for r in rows]
+
+    mapped, rows = call(
         mapped_body,
-        [shape(*t_resid.shape, dtype=F32)],
+        [shape(*t_resid.shape, dtype=F32), shape(16, *proj.shape)],
         [at_cols, hidden, *rows],
-        [SMEM, VMEM, VMEM, VMEM],
-    )[0]
+        [SMEM] + [VMEM] * 11,
+    )
     mapped, terms = tied(mapped, terms)
     err, back = call(
         err_body,
         [shape(*t_resid.shape), shape(4, 4, tok, cols)],
-        [at_cols, mapped, t_resid, terms, *rows],
-        [SMEM] + [VMEM] * 5,
-    )
-    back_moved = [moved_by(back[step], "y", step) for step in (1, 2, 3)]
+        [at_cols, mapped, t_resid, terms, rows],
+        [SMEM] + [VMEM] * 4,
+    )
+    back_moved = tied(*(moved_by(back[step], "y", step) for step in (1, 2, 3)))
 
     scale = 1.0 / math.sqrt(tok * 16)
     theirs_g = call(
@@ -253,24 +312,27 @@
         [SMEM, VMEM, VMEM],
     )[0]
     came_g = swapped(theirs_g, "c")
-    chip_g = call(
+    near_g, left_g, right_g, far_up, far_down = call(
         functools.partial(grad_body, scale, 0),
-        [shape(2, *proj.shape)] * 4,
+        [shape(2, *proj.shape)] * 3 + [shape(*proj.shape)] * 2,
         [at_cols, hidden, err, came_g],
         [SMEM, VMEM, VMEM, VMEM],
     )
-    moved_g = [moved_by(chip_g[step], "x", step) for step in (1, 2, 3)]
-
-    back_moved[0], _ = tied(back_moved[0], chip_g[0])
+    far_up, far_down = moved_by(far_up, "x", 1), moved_by(far_down, "x", -1)
+    moved_g = call(grad_near_body, [shape(2, *proj.shape)] * 2, [left_g, right_g, far_up, far_down])
+    *back_moved, up_g, down_g = tied(*back_moved, *moved_g)
+    moved_g = [up_g, down_g]
+    moved_g = [moved_by(moved_g[0], "x", 1), moved_by(moved_g[1], "x", -1)]
+
     back = call(terms_body, [shape(4, tok, cols)], [back[0], *back_moved])[0]
     back = exchanged(back, "zl")
     back = call(sum_body, [shape(4, tok, cols)], [back])[0]
     back = exchanged(back, "zl")
     back, *moved_g = tied(back, *moved_g)
-    back_all = [back] + [moved_by(back, "y", -step) for step in (1, 2, 3)]
+    back_all = [back, *tied(*(moved_by(back, "y", -step) for step in (1, 2, 3)))]
 
     own_g, sent_g = call(
-        grad_sum_body, [shape(*proj.shape, dtype=F32), shape(*proj.shape)], [chip_g[0], *moved_g]
+        grad_sum_body, [shape(*proj.shape, dtype=F32), shape(*proj.shape)], [near_g, *moved_g]
     )
     came_g = swapped(sent_g, "zh")
     attn_grad = call(attn_body, [shape(tok, cols)], [here, out_proj, *back_all], [SMEM] + [VMEM] * 5)[0]

time: 216 us -> 204 us (0.944)
  waiting for transfers between devices: 81 us -> 62.5 us
  other arithmetic: 13.1 us -> 3.33 us
  Pallas kernels: 28.2 us -> 37.5 us
  local copies, waits for them, and re-layouts: 12.4 us -> 18.8 us
    ppermute x22 -> x21, waiting for transfers between devices: 63.3 us -> 26.7 us  [moved_by(): return lax.ppermute(x, axes, [(i, (i + step) % n) for i in range(n)])]
    ppermute x5 -> x9, waiting for transfers between devices: 6.12 us -> 23.8 us  [swapped(): return lax.ppermute(x, axis, [(0, 1), (1, 0)])]
    unnamed x48 -> x37, local copies, waits for them, and re-layouts: 8.87 us -> 16.6 us
    pallas_call x0 -> x2, Pallas kernels: none -> 7.32 us  [on_blocks(): pl.pallas_call(body, grid=(1,), in_specs=[spec(shape, at) for _, shape, a...]
    ppermute x22 -> x21, starting transfers between devices: 39.7 us -> 33.1 us  [moved_by(): return lax.ppermute(x, axes, [(i, (i + step) % n) for i in range(n)])]
    convert_element_type x2 -> x0, other arithmetic: 5.59 us -> none  [the longest x1 2.8 us: on_device(): plus(mine[0, 4:], came[0, 4:]).astype(BF)]
    all_to_all x6, starting transfers between devices: 32.3 us -> 37.1 us  [exchanged(): return lax.all_to_all(x, axes, 0, 0, tiled=True)]
    slice x3 -> x0, local copies, waits for them, and re-layouts: 3.27 us -> none  [the longest x1 3.14 us: on_device(): over_y = (plus(mine[2], came[2]) + plus(up, down_)).astype(BF)]
  transfers between devices with their start and end apart: 33 -> 36, of which waited for: 21 -> 19; matrix products, arithmetic and copies ran while one was open for 10% -> 3% of each run, Pallas kernels for 10% -> 13%
where the time goes in v3:
time: 204 us; the launch traced here: 202 us
  starting transfers between devices  79.1 us (39%)
  waiting for transfers between devices  62.5 us (31%)
  Pallas kernels  37.5 us (18%)
  local copies, waits for them, and re-layouts  18.8 us (9%)
  other arithmetic  3.33 us (2%)
    all_to_all x6, starting transfers between devices, exchanged(): return lax.all_to_all(x, axes, 0, 0, tiled=True)  37.1 us
    ppermute x21, starting transfers between devices, moved_by(): return lax.ppermute(x, axes, [(i, (i + step) % n) for i in range(n)])  33.1 us
    ppermute x21, waiting for transfers between devices, moved_by(): return lax.ppermute(x, axes, [(i, (i + step) % n) for i in range(n)])  26.7 us
    ppermute x9, waiting for transfers between devices, swapped(): return lax.ppermute(x, axis, [(0, 1), (1, 0)])  23.8 us
    pallas_call x14, Pallas kernels, call(): pl.pallas_call(body, out_shape=outs, in_specs=specs or [VMEM] * len(args)...  18.4 us
    unnamed x37, local copies, waits for them, and re-layouts  16.6 us
    all_to_all x6, waiting for transfers between devices, exchanged(): return lax.all_to_all(x, axes, 0, 0, tiled=True)  12.1 us
    pallas_call x1, Pallas kernels, teacher_terms(): pl.pallas_call(teacher_body, grid_spec=pltpu.PrefetchScalarGridSpec(num_s...  11.7 us
  transfers between devices with their start and end apart: 36, of which 19 were waited for; matrix products, arithmetic and copies ran while one was open for 3% of the time, Pallas kernels for 13%

profile of v3, /device:TPU:46, one launch (start us, length us, event | category | flops | bytes accessed | tf_op | source)
XLA Modules:
  0.0 202.1 jit_solution(12474418897097933498)
XLA Ops:
  0.7 1.7 copy-done.1
  3.2 1.4 shard_map.86
  4.6 4.9 %all-to-all-start = ((bf16[4,4,128,256]{3,2,1,0:T(8,128)(2,1)}), bf16[4,4,128,256]{3,2,1,0:T(8,128)(2,1)S(1)}, u32[]{:S(2)}, u32[]{:S(2)}) async-start(bf16[4,4,128,256]{3,2,1,0:T(8,128)(2,1)} %shard_map.86), calls=%async_computation | async-start | bytes 2097152 | tf_op jit(solution)/shard_map/all_to_all | solution.py:45
  10.1 11.7 %shard_map.87 = (bf16[4,2,4,128,512]{4,3,2,1,0:T(8,128)(2,1)}, bf16[4,2,4,128,512]{4,3,2,1,0:T(8,128)(2,1)}) custom-call(s32[2]{0:T(128)} %pad_add_fusion.at_ref.y_ref, bf16[4,448,128]{2,1,0:T(8,128)(2,1)} %bitcast.40, bf16[448,8192]{1,0:T(8,128)(2,1)} %w_ref.4), custom_call_target="tpu_custom_call" | custom-call | flops 1 | bytes 1 | tf_op jit(solution)/shard_map/pallas_call | solution.py:77
  21.9 1.2 all-to-all-done.x_ref
  23.1 0.9 shard_map.88
  24.0 7.4 %collective-permute-done.refs_1_.refs_3_.refs_5_.came_ref = bf16[4,8,128,512]{3,2,1,0:T(8,128)(2,1)S(1)} collective-permute-done((bf16[4,8,128,512]{3,2,1,0:T(8,128)(2,1)}, bf16[4,8,128,512]{3,2,1,0:T(8,128)(2,1)S(1)}, u32[]{:S(2)}, u32[]{:S(2)}) %collective-permute-start) | collective-permute-done | bytes 4194336 | tf_op jit(solution)/shard_map/ppermute | solution.py:41
  31.3 2.0 copy-done.15
  33.3 2.6 %shard_map.91 = (bf16[4,128,512]{2,1,0:T(8,128)(2,1)}, bf16[4,128,512]{2,1,0:T(8,128)(2,1)}) custom-call(bf16[4,8,128,512]{3,2,1,0:T(8,128)(2,1)} %bitcast.36, bf16[4,8,128,512]{3,2,1,0:T(8,128)(2,1)} %copy-done.15), custom_call_target="tpu_custom_call" | custom-call | flops 1 | bytes 1 | tf_op jit(solution)/shard_map/pallas_call | solution.py:120
  36.2 1.8 collective-permute-start.2
  38.0 6.0 %all-to-all-start.1 = ((bf16[4,128,256]{2,1,0:T(8,128)(2,1)}), bf16[4,128,256]{2,1,0:T(8,128)(2,1)S(1)}, u32[]{:S(2)}, u32[]{:S(2)}) async-start(bf16[4,128,256]{2,1,0:T(8,128)(2,1)} %bitcast.20), calls=%async_computation.1 | async-start | bytes 524288 | tf_op jit(solution)/shard_map/all_to_all | solution.py:45
  44.0 4.7 %shard_map.89 = (bf16[8,128,512]{2,1,0:T(8,128)(2,1)}, bf16[8,128,512]{2,1,0:T(8,128)(2,1)}, bf16[8,128,512]{2,1,0:T(8,128)(2,1)}) custom-call(bf16[4,8,128,512]{3,2,1,0:T(8,128)(2,1)} %bitcast.37, bf16[4,8,128,512]{3,2,1,0:T(8,128)(2,1)} %copy-done.15, bf16[4,8,128,512]{3,2,1,0:T(8,128)(2,1)} %bitcast.38, bf16[4,8,128,512]{3,2,1,0:T(8,128)(2,1)} %copy-done.15, ...), custom_call_target="tpu_custom_call" | custom-call | flops 1 | bytes 1 | tf_op jit(solution)/shard_map/pallas_call | solution.py:120
  48.7 2.1 %all-to-all-done.1.x_ref = bf16[4,128,256]{2,1,0:T(8,128)(2,1)S(1)} async-done(((bf16[4,128,256]{2,1,0:T(8,128)(2,1)}), bf16[4,128,256]{2,1,0:T(8,128)(2,1)S(1)}, u32[]{:S(2)}, u32[]{:S(2)}) %all-to-all-start.1) | async-done | bytes 262176 | tf_op jit(solution)/shard_map/all_to_all | solution.py:45
  51.6 1.2 copy-done.5
  52.8 1.2 copy-done.6
  54.0 1.6 shard_map.92
  56.3 2.0 collective-permute-start.4
  58.3 5.2 %all-to-all-start.2 = ((bf16[4,128,256]{2,1,0:T(8,128)(2,1)}), bf16[4,128,256]{2,1,0:T(8,128)(2,1)S(1)}, u32[]{:S(2)}, u32[]{:S(2)}) async-start(bf16[4,128,256]{2,1,0:T(8,128)(2,1)} %shard_map.90), calls=%async_computation.2 | async-start | bytes 524288 | tf_op jit(solution)/shard_map/all_to_all | solution.py:45
  63.5 5.0 %collective-permute-start.8 = (bf16[256,512]{1,0:T(8,128)(2,1)}, bf16[256,512]{1,0:T(8,128)(2,1)S(1)}, u32[]{:S(2)}, u32[]{:S(2)}) collective-permute-start(bf16[256,512]{1,0:T(8,128)(2,1)} %param.13), channel_id=1, source_target_pairs={{0,128},{128,0},{1,129},{129,1},{2,130},{130,2},{3,131},{131,3},{4... | collective-permute-start | bytes 786440 | tf_op jit(solution)/shard_map/ppermute | solution.py:41
  68.5 10.9 %collective-permute-done.8 = bf16[256,512]{1,0:T(8,128)(2,1)S(1)} collective-permute-done((bf16[256,512]{1,0:T(8,128)(2,1)}, bf16[256,512]{1,0:T(8,128)(2,1)S(1)}, u32[]{:S(2)}, u32[]{:S(2)}) %collective-permute-start.8) | collective-permute-done | bytes 262176 | tf_op jit(solution)/shard_map/ppermute | solution.py:41
  79.4 1.8 pad_maximum_fusion.refs_0_
  82.0 2.4 %collective-permute-start.10 = (bf16[2,256,512]{2,1,0:T(8,128)(2,1)}, bf16[2,256,512]{2,1,0:T(8,128)(2,1)}, u32[]{:S(2)}, u32[]{:S(2)}) collective-permute-start(bf16[2,256,512]{2,1,0:T(8,128)(2,1)} %pad_maximum_fusion.refs_0_), channel_id=1, source_target_pairs={{0,16},{16,32},{32,48},{48,0},{1,17},{17,33},{33,49},{49,1},{2,18}... | collective-permute-start | bytes 1572872 | tf_op jit(solution)/shard_map/ppermute | solution.py:37
  84.4 2.6 %shard_map.93 = bf16[8,128,512]{2,1,0:T(8,128)(2,1)} custom-call(bf16[8,128,512]{2,1,0:T(8,128)(2,1)S(1)} %copy-done.7, bf16[8,128,512]{2,1,0:T(8,128)(2,1)S(1)} %collective-permute-done.3.refs_1_, bf16[8,128,512]{2,1,0:T(8,128)(2,1)} %collective-permute-done.4.refs_2_), custom_call_target="tpu_custom_call" | custom-call | flops 1 | bytes 1 | tf_op jit(solution)/shard_map/pallas_call | solution.py:25
  87.0 8.6 %all-to-all-start.3 = ((bf16[8,128,512]{2,1,0:T(8,128)(2,1)}), bf16[8,128,512]{2,1,0:T(8,128)(2,1)S(1)}, u32[]{:S(2)}, u32[]{:S(2)}) async-start(bf16[8,128,512]{2,1,0:T(8,128)(2,1)} %shard_map.93), calls=%async_computation.3 | async-start | bytes 2097152 | tf_op jit(solution)/shard_map/all_to_all | solution.py:45
  95.6 1.0 slice_bitcast_fusion.5
  96.7 1.0 slice_bitcast_fusion.4
  97.7 3.3 %collective-permute-start.12 = (bf16[256,512]{1,0:T(8,128)(2,1)S(1)}, bf16[256,512]{1,0:T(8,128)(2,1)S(1)}, u32[]{:S(2)}, u32[]{:S(2)}) collective-permute-start(bf16[256,512]{1,0:T(8,128)(2,1)S(1)} %slice_bitcast_fusion.4), channel_id=1, source_target_pairs={{0,16},{16,32},{32,48},{48,0},{1,17},{17,33},{33,49},{49,1},{2,18}... | collective-permute-start | bytes 786440 | tf_op jit(solution)/shard_map/ppermute | solution.py:37
  101.0 3.0 %collective-permute-start.5 = (bf16[4,128,256]{2,1,0:T(8,128)(2,1)}, bf16[4,128,256]{2,1,0:T(8,128)(2,1)}, u32[]{:S(2)}, u32[]{:S(2)}) collective-permute-start(bf16[4,128,256]{2,1,0:T(8,128)(2,1)} %copy-done.16), channel_id=1, source_target_pairs={{0,12},{4,0},{8,4},{12,8},{1,13},{5,1},{9,5},{13,9},{2,14},{6,2},{... | collective-permute-start | bytes 786440 | tf_op jit(solution)/shard_map/ppermute | solution.py:37
  104.9 3.2 %collective-permute-start.6 = (bf16[4,128,256]{2,1,0:T(8,128)(2,1)}, bf16[4,128,256]{2,1,0:T(8,128)(2,1)S(1)}, u32[]{:S(2)}, u32[]{:S(2)}) collective-permute-start(bf16[4,128,256]{2,1,0:T(8,128)(2,1)} %copy-done.16), channel_id=1, source_target_pairs={{0,8},{4,12},{8,0},{12,4},{1,9},{5,13},{9,1},{13,5},{2,10},{6,14},... | collective-permute-start | bytes 786440 | tf_op jit(solution)/shard_map/ppermute | solution.py:37
  108.1 1.6 collective-permute-start.7
  109.8 1.0 constant_dynamic-update-slice_fusion.3
  110.7 4.5 %collective-permute-done.6 = bf16[4,128,256]{2,1,0:T(8,128)(2,1)S(1)} collective-permute-done((bf16[4,128,256]{2,1,0:T(8,128)(2,1)}, bf16[4,128,256]{2,1,0:T(8,128)(2,1)S(1)}, u32[]{:S(2)}, u32[]{:S(2)}) %collective-permute-start.6) | collective-permute-done | bytes 262176 | tf_op jit(solution)/shard_map/ppermute | solution.py:37
  115.3 5.7 %collective-permute-done.7 = bf16[4,128,256]{2,1,0:T(8,128)(2,1)S(1)} collective-permute-done((bf16[4,128,256]{2,1,0:T(8,128)(2,1)}, bf16[4,128,256]{2,1,0:T(8,128)(2,1)S(1)}, u32[]{:S(2)}, u32[]{:S(2)}) %collective-permute-start.7) | collective-permute-done | bytes 262176 | tf_op jit(solution)/shard_map/ppermute | solution.py:37
  121.0 1.0 constant_dynamic-update-slice_fusion.2
  122.7 0.9 copy-done.9
  123.7 0.9 copy-done.11
  124.6 2.1 %shard_map.94 = (f32[128,512]{1,0:T(8,128)S(1)}, bf16[16,256,512]{2,1,0:T(8,128)(2,1)S(1)}) custom-call(s32[16]{0:T(128)S(1)} %fusion.at_ref, bf16[16,128,256]{2,1,0:T(8,128)(2,1)S(1)} %constant_dynamic-update-slice_fusion.h_ref, bf16[2,256,512]{2,1,0:T(8,128)(2,1)} %pad_maximum_fusion.refs_0_, bf16[2,256,512]{2,1,0:T(8,128)(2,1)} %collective-permute-done.9.refs_1_, ...), custom_call_target="tpu_custom_call" | custom-call | flops 1 | bytes 1 | tf_op jit(solution)/shard_map/pallas_call | solution.py:25
  126.8 2.0 copy-done.3
  128.8 2.2 %copy-done.4 = bf16[16,256,512]{2,1,0:T(8,128)(2,1)S(1)} copy-done((bf16[16,256,512]{2,1,0:T(8,128)(2,1)S(1)}, bf16[16,256,512]{2,1,0:T(8,128)(2,1)}, u32[]{:S(2)}) %copy-start.4) | copy-done | bytes 4194328
  130.9 2.0 shard_map.95
  132.9 1.3 shard_map.96
  134.5 1.5 collective-permute-start.18
  136.0 2.9 %collective-permute-start.19 = (bf16[4,128,256]{2,1,0:T(8,128)(2,1)S(1)}, bf16[4,128,256]{2,1,0:T(8,128)(2,1)S(1)}, u32[]{:S(2)}, u32[]{:S(2)}) collective-permute-start(bf16[4,128,256]{2,1,0:T(8,128)(2,1)S(1)} %get-tuple-element.133), channel_id=1, source_target_pairs={{0,8},{4,12},{8,0},{12,4},{1,9},{5,13},{9,1},{13,5},{2,10},{6,14},... | collective-permute-start | bytes 786440 | tf_op jit(solution)/shard_map/ppermute | solution.py:37
  139.0 1.3 shard_map.97
  140.9 1.5 collective-permute-start.23
  142.4 1.7 collective-permute-done.18.refs_1_
  144.0 2.7 %collective-permute-done.19.refs_2_ = bf16[4,128,256]{2,1,0:T(8,128)(2,1)S(1)} collective-permute-done((bf16[4,128,256]{2,1,0:T(8,128)(2,1)S(1)}, bf16[4,128,256]{2,1,0:T(8,128)(2,1)S(1)}, u32[]{:S(2)}, u32[]{:S(2)}) %collective-permute-start.19) | collective-permute-done | bytes 262176 | tf_op jit(solution)/shard_map/ppermute | solution.py:37
  146.7 4.7 %collective-permute-done.20.refs_3_ = bf16[4,128,256]{2,1,0:T(8,128)(2,1)S(1)} collective-permute-done((bf16[4,128,256]{2,1,0:T(8,128)(2,1)S(1)}, bf16[4,128,256]{2,1,0:T(8,128)(2,1)S(1)}, u32[]{:S(2)}, u32[]{:S(2)}) %collective-permute-start.20) | collective-permute-done | bytes 262176 | tf_op jit(solution)/shard_map/ppermute | solution.py:37
  151.5 0.9 shard_map.98
  153.2 7.1 %all-to-all-start.4 = ((bf16[4,128,256]{2,1,0:T(8,128)(2,1)}), bf16[4,128,256]{2,1,0:T(8,128)(2,1)S(1)}, u32[]{:S(2)}, u32[]{:S(2)}) async-start(bf16[4,128,256]{2,1,0:T(8,128)(2,1)} %shard_map.99), calls=%async_computation.4 | async-start | bytes 524288 | tf_op jit(solution)/shard_map/all_to_all | solution.py:45
  160.2 1.8 collective-permute-start.24
  162.3 5.2 %all-to-all-done.4.x_ref = bf16[4,128,256]{2,1,0:T(8,128)(2,1)S(1)} async-done(((bf16[4,128,256]{2,1,0:T(8,128)(2,1)}), bf16[4,128,256]{2,1,0:T(8,128)(2,1)S(1)}, u32[]{:S(2)}, u32[]{:S(2)}) %all-to-all-start.4) | async-done | bytes 262176 | tf_op jit(solution)/shard_map/all_to_all | solution.py:45
  168.2 5.3 %all-to-all-start.5 = ((bf16[4,128,256]{2,1,0:T(8,128)(2,1)}), bf16[4,128,256]{2,1,0:T(8,128)(2,1)S(1)}, u32[]{:S(2)}, u32[]{:S(2)}) async-start(bf16[4,128,256]{2,1,0:T(8,128)(2,1)} %shard_map.100), calls=%async_computation.5 | async-start | bytes 524288 | tf_op jit(solution)/shard_map/all_to_all | solution.py:45
  173.7 2.5 %collective-permute-done.25.refs_2_ = bf16[2,256,512]{2,1,0:T(8,128)(2,1)S(1)} collective-permute-done((bf16[2,256,512]{2,1,0:T(8,128)(2,1)S(1)}, bf16[2,256,512]{2,1,0:T(8,128)(2,1)S(1)}, u32[]{:S(2)}, u32[]{:S(2)}) %collective-permute-start.25) | collective-permute-done | bytes 524320 | tf_op jit(solution)/shard_map/ppermute | solution.py:37
  176.2 3.6 %all-to-all-done.5.refs_0_ = bf16[4,128,256]{2,1,0:T(8,128)(2,1)S(1)} async-done(((bf16[4,128,256]{2,1,0:T(8,128)(2,1)}), bf16[4,128,256]{2,1,0:T(8,128)(2,1)S(1)}, u32[]{:S(2)}, u32[]{:S(2)}) %all-to-all-start.5) | async-done | bytes 262176 | tf_op jit(solution)/shard_map/all_to_all | solution.py:45
  180.5 2.1 %collective-permute-start.27 = (bf16[4,128,256]{2,1,0:T(8,128)(2,1)S(1)}, bf16[4,128,256]{2,1,0:T(8,128)(2,1)S(1)}, u32[]{:S(2)}, u32[]{:S(2)}) collective-permute-start(bf16[4,128,256]{2,1,0:T(8,128)(2,1)S(1)} %all-to-all-done.5.refs_0_), channel_id=1, source_target_pairs={{0,8},{4,12},{8,0},{12,4},{1,9},{5,13},{9,1},{13,5},{2,10},{6,14},... | collective-permute-start | bytes 786440 | tf_op jit(solution)/shard_map/ppermute | solution.py:37
  182.6 2.6 %collective-permute-start.28 = (bf16[4,128,256]{2,1,0:T(8,128)(2,1)S(1)}, bf16[4,128,256]{2,1,0:T(8,128)(2,1)S(1)}, u32[]{:S(2)}, u32[]{:S(2)}) collective-permute-start(bf16[4,128,256]{2,1,0:T(8,128)(2,1)S(1)} %all-to-all-done.5.refs_0_), channel_id=1, source_target_pairs={{0,4},{4,8},{8,12},{12,0},{1,5},{5,9},{9,13},{13,1},{2,6},{6,10},{... | collective-permute-start | bytes 786440 | tf_op jit(solution)/shard_map/ppermute | solution.py:37
  185.5 2.9 %collective-permute-start.29 = (bf16[256,512]{1,0:T(8,128)(2,1)S(1)}, bf16[256,512]{1,0:T(8,128)(2,1)S(1)}, u32[]{:S(2)}, u32[]{:S(2)}) collective-permute-start(bf16[256,512]{1,0:T(8,128)(2,1)S(1)} %get-tuple-element.128), channel_id=1, source_target_pairs={{0,128},{128,0},{1,129},{129,1},{2,130},{130,2},{3,131},{131,3},{4... | collective-permute-start | bytes 786440 | tf_op jit(solution)/shard_map/ppermute | solution.py:41
  188.9 2.9 %collective-permute-done.27.refs_2_ = bf16[4,128,256]{2,1,0:T(8,128)(2,1)S(1)} collective-permute-done((bf16[4,128,256]{2,1,0:T(8,128)(2,1)S(1)}, bf16[4,128,256]{2,1,0:T(8,128)(2,1)S(1)}, u32[]{:S(2)}, u32[]{:S(2)}) %collective-permute-start.27) | collective-permute-done | bytes 262176 | tf_op jit(solution)/shard_map/ppermute | solution.py:37
  191.9 0.9 collective-permute-done.28.refs_3_
  192.8 1.6 copy-done.2
  194.4 2.0 shard_map.101
  196.4 4.8 %collective-permute-done.29 = bf16[256,512]{1,0:T(8,128)(2,1)S(1)} collective-permute-done((bf16[256,512]{1,0:T(8,128)(2,1)S(1)}, bf16[256,512]{1,0:T(8,128)(2,1)S(1)}, u32[]{:S(2)}, u32[]{:S(2)}) %collective-permute-start.29) | collective-permute-done | bytes 262176 | tf_op jit(solution)/shard_map/ppermute | solution.py:41
  201.2 0.9 convert_add_fusion
  (72 shorter events, 10.5 us)
Async XLA Ops:
  0.6 43.4 %copy-start = (bf16[128,4096]{1,0:T(8,128)(2,1)S(1)}, bf16[128,4096]{1,0:T(8,128)(2,1)}, u32[]{:S(2)}) copy-start(bf16[128,4096]{1,0:T(8,128)(2,1)} %param.12) | copy-start | bytes 3145732
  0.6 1.7 copy-start.1
  2.3 0.8 copy-start.13
  4.6 18.5 %all-to-all-start = ((bf16[4,4,128,256]{3,2,1,0:T(8,128)(2,1)}), bf16[4,4,128,256]{3,2,1,0:T(8,128)(2,1)S(1)}, u32[]{:S(2)}, u32[]{:S(2)}) async-start(bf16[4,4,128,256]{3,2,1,0:T(8,128)(2,1)} %shard_map.86), calls=%async_computation | async-start | bytes 2097152 | tf_op jit(solution)/shard_map/all_to_all | solution.py:45
  24.0 7.4 %collective-permute-start = (bf16[4,8,128,512]{3,2,1,0:T(8,128)(2,1)}, bf16[4,8,128,512]{3,2,1,0:T(8,128)(2,1)S(1)}, u32[]{:S(2)}, u32[]{:S(2)}) collective-permute-start(bf16[4,8,128,512]{3,2,1,0:T(8,128)(2,1)} %bitcast.43), channel_id=1, source_target_pairs={{0,64},{64,0},{1,65},{65,1},{2,66},{66,2},{3,67},{67,3},{4,68},{68... | collective-permute-start | bytes 12582920 | tf_op jit(solution)/shard_map/ppermute | solution.py:41
  31.3 2.0 copy-start.15
  36.0 15.6 %collective-permute-start.1 = (bf16[4,128,512]{2,1,0:T(8,128)(2,1)}, bf16[4,128,512]{2,1,0:T(8,128)(2,1)S(1)}, u32[]{:S(2)}, u32[]{:S(2)}) collective-permute-start(bf16[4,128,512]{2,1,0:T(8,128)(2,1)} %get-tuple-element.80), channel_id=1, source_target_pairs={{0,4},{4,8},{8,12},{12,0},{1,5},{5,9},{9,13},{13,1},{2,6},{6,10},{... | collective-permute-start | bytes 1572872 | tf_op jit(solution)/shard_map/ppermute | solution.py:37
  36.2 15.4 %collective-permute-start.2 = (bf16[4,128,512]{2,1,0:T(8,128)(2,1)}, bf16[4,128,512]{2,1,0:T(8,128)(2,1)S(1)}, u32[]{:S(2)}, u32[]{:S(2)}) collective-permute-start(bf16[4,128,512]{2,1,0:T(8,128)(2,1)} %get-tuple-element.81), channel_id=1, source_target_pairs={{0,12},{4,0},{8,4},{12,8},{1,13},{5,1},{9,5},{13,9},{2,14},{6,2},{... | collective-permute-start | bytes 1572872 | tf_op jit(solution)/shard_map/ppermute | solution.py:37
  38.0 12.8 %all-to-all-start.1 = ((bf16[4,128,256]{2,1,0:T(8,128)(2,1)}), bf16[4,128,256]{2,1,0:T(8,128)(2,1)S(1)}, u32[]{:S(2)}, u32[]{:S(2)}) async-start(bf16[4,128,256]{2,1,0:T(8,128)(2,1)} %bitcast.20), calls=%async_computation.1 | async-start | bytes 524288 | tf_op jit(solution)/shard_map/all_to_all | solution.py:45
  51.6 1.2 copy-start.5
  52.8 1.2 copy-start.6
  54.0 30.4 %copy-start.7 = (bf16[8,128,512]{2,1,0:T(8,128)(2,1)S(1)}, bf16[8,128,512]{2,1,0:T(8,128)(2,1)}, u32[]{:S(2)}) copy-start(bf16[8,128,512]{2,1,0:T(8,128)(2,1)} %get-tuple-element.76.refs_0_) | copy-start | bytes 3145732
  55.6 28.8 %collective-permute-start.3 = (bf16[8,128,512]{2,1,0:T(8,128)(2,1)}, bf16[8,128,512]{2,1,0:T(8,128)(2,1)S(1)}, u32[]{:S(2)}, u32[]{:S(2)}) collective-permute-start(bf16[8,128,512]{2,1,0:T(8,128)(2,1)} %get-tuple-element.86), channel_id=1, source_target_pairs={{0,4},{4,8},{8,12},{12,0},{1,5},{5,9},{9,13},{13,1},{2,6},{6,10},{... | collective-permute-start | bytes 3145736 | tf_op jit(solution)/shard_map/ppermute | solution.py:37
  56.3 28.1 %collective-permute-start.4 = (bf16[8,128,512]{2,1,0:T(8,128)(2,1)}, bf16[8,128,512]{2,1,0:T(8,128)(2,1)}, u32[]{:S(2)}, u32[]{:S(2)}) collective-permute-start(bf16[8,128,512]{2,1,0:T(8,128)(2,1)} %get-tuple-element.87), channel_id=1, source_target_pairs={{0,12},{4,0},{8,4},{12,8},{1,13},{5,1},{9,5},{13,9},{2,14},{6,2},{... | collective-permute-start | bytes 3145736 | tf_op jit(solution)/shard_map/ppermute | solution.py:37
  58.3 22.9 %all-to-all-start.2 = ((bf16[4,128,256]{2,1,0:T(8,128)(2,1)}), bf16[4,128,256]{2,1,0:T(8,128)(2,1)S(1)}, u32[]{:S(2)}, u32[]{:S(2)}) async-start(bf16[4,128,256]{2,1,0:T(8,128)(2,1)} %shard_map.90), calls=%async_computation.2 | async-start | bytes 524288 | tf_op jit(solution)/shard_map/all_to_all | solution.py:45
  63.5 15.9 %collective-permute-start.8 = (bf16[256,512]{1,0:T(8,128)(2,1)}, bf16[256,512]{1,0:T(8,128)(2,1)S(1)}, u32[]{:S(2)}, u32[]{:S(2)}) collective-permute-start(bf16[256,512]{1,0:T(8,128)(2,1)} %param.13), channel_id=1, source_target_pairs={{0,128},{128,0},{1,129},{129,1},{2,130},{130,2},{3,131},{131,3},{4... | collective-permute-start | bytes 786440 | tf_op jit(solution)/shard_map/ppermute | solution.py:41
  81.2 14.5 %copy-start.16 = (bf16[4,128,256]{2,1,0:T(8,128)(2,1)}, bf16[4,128,256]{2,1,0:T(8,128)(2,1)S(1)}, u32[]{:S(2)}) copy-start(bf16[4,128,256]{2,1,0:T(8,128)(2,1)S(1)} %all-to-all-done.2) | copy-start | bytes 786436
  81.2 14.5 %collective-permute-start.9 = (bf16[2,256,512]{2,1,0:T(8,128)(2,1)}, bf16[2,256,512]{2,1,0:T(8,128)(2,1)}, u32[]{:S(2)}, u32[]{:S(2)}) collective-permute-start(bf16[2,256,512]{2,1,0:T(8,128)(2,1)} %pad_maximum_fusion.refs_0_), channel_id=1, source_target_pairs={{0,48},{16,0},{32,16},{48,32},{1,49},{17,1},{33,17},{49,33},{2,50}... | collective-permute-start | bytes 1572872 | tf_op jit(solution)/shard_map/ppermute | solution.py:37
  82.0 13.6 %collective-permute-start.10 = (bf16[2,256,512]{2,1,0:T(8,128)(2,1)}, bf16[2,256,512]{2,1,0:T(8,128)(2,1)}, u32[]{:S(2)}, u32[]{:S(2)}) collective-permute-start(bf16[2,256,512]{2,1,0:T(8,128)(2,1)} %pad_maximum_fusion.refs_0_), channel_id=1, source_target_pairs={{0,16},{16,32},{32,48},{48,0},{1,17},{17,33},{33,49},{49,1},{2,18}... | collective-permute-start | bytes 1572872 | tf_op jit(solution)/shard_map/ppermute | solution.py:37
  87.0 41.7 %all-to-all-start.3 = ((bf16[8,128,512]{2,1,0:T(8,128)(2,1)}), bf16[8,128,512]{2,1,0:T(8,128)(2,1)S(1)}, u32[]{:S(2)}, u32[]{:S(2)}) async-start(bf16[8,128,512]{2,1,0:T(8,128)(2,1)} %shard_map.93), calls=%async_computation.3 | async-start | bytes 2097152 | tf_op jit(solution)/shard_map/all_to_all | solution.py:45
  96.6 32.2 %copy-start.12 = (bf16[128,512]{1,0:T(8,128)(2,1)S(1)}, bf16[128,512]{1,0:T(8,128)(2,1)}, u32[]{:S(2)}) copy-start(bf16[128,512]{1,0:T(8,128)(2,1)} %resid_ref.1) | copy-start | bytes 393220
  96.6 8.2 %collective-permute-start.11 = (bf16[256,512]{1,0:T(8,128)(2,1)S(1)}, bf16[256,512]{1,0:T(8,128)(2,1)S(1)}, u32[]{:S(2)}, u32[]{:S(2)}) collective-permute-start(bf16[256,512]{1,0:T(8,128)(2,1)S(1)} %slice_bitcast_fusion.5), channel_id=1, source_target_pairs={{0,48},{16,0},{32,16},{48,32},{1,49},{17,1},{33,17},{49,33},{2,50}... | collective-permute-start | bytes 786440 | tf_op jit(solution)/shard_map/ppermute | solution.py:37
  97.7 7.2 %collective-permute-start.12 = (bf16[256,512]{1,0:T(8,128)(2,1)S(1)}, bf16[256,512]{1,0:T(8,128)(2,1)S(1)}, u32[]{:S(2)}, u32[]{:S(2)}) collective-permute-start(bf16[256,512]{1,0:T(8,128)(2,1)S(1)} %slice_bitcast_fusion.4), channel_id=1, source_target_pairs={{0,16},{16,32},{32,48},{48,0},{1,17},{17,33},{33,49},{49,1},{2,18}... | collective-permute-start | bytes 786440 | tf_op jit(solution)/shard_map/ppermute | solution.py:37
  101.0 7.2 %collective-permute-start.5 = (bf16[4,128,256]{2,1,0:T(8,128)(2,1)}, bf16[4,128,256]{2,1,0:T(8,128)(2,1)}, u32[]{:S(2)}, u32[]{:S(2)}) collective-permute-start(bf16[4,128,256]{2,1,0:T(8,128)(2,1)} %copy-done.16), channel_id=1, source_target_pairs={{0,12},{4,0},{8,4},{12,8},{1,13},{5,1},{9,5},{13,9},{2,14},{6,2},{... | collective-permute-start | bytes 786440 | tf_op jit(solution)/shard_map/ppermute | solution.py:37
  104.0 18.0 %collective-permute-start.13 = (bf16[2,256,512]{2,1,0:T(8,128)(2,1)}, bf16[2,256,512]{2,1,0:T(8,128)(2,1)S(1)}, u32[]{:S(2)}, u32[]{:S(2)}) collective-permute-start(bf16[2,256,512]{2,1,0:T(8,128)(2,1)} %pad_maximum_fusion.refs_0_), channel_id=1, source_target_pairs={{0,64},{64,0},{1,65},{65,1},{2,66},{66,2},{3,67},{67,3},{4,68},{68... | collective-permute-start | bytes 1572872 | tf_op jit(solution)/shard_map/ppermute | solution.py:41
  104.3 17.7 %collective-permute-start.14 = (bf16[2,256,512]{2,1,0:T(8,128)(2,1)}, bf16[2,256,512]{2,1,0:T(8,128)(2,1)S(1)}, u32[]{:S(2)}, u32[]{:S(2)}) collective-permute-start(bf16[2,256,512]{2,1,0:T(8,128)(2,1)} %collective-permute-done.9.refs_1_), channel_id=1, source_target_pairs={{0,64},{64,0},{1,65},{65,1},{2,66},{66,2},{3,67},{67,3},{4,68},{68... | collective-permute-start | bytes 1572872 | tf_op jit(solution)/shard_map/ppermute | solution.py:41
  104.8 17.3 %copy-start.8 = (bf16[256,512]{1,0:T(8,128)(2,1)}, bf16[256,512]{1,0:T(8,128)(2,1)S(1)}, u32[]{:S(2)}) copy-start(bf16[256,512]{1,0:T(8,128)(2,1)S(1)} %collective-permute-done.11.refs_3_) | copy-start | bytes 786436
  104.8 17.2 %collective-permute-start.15 = (bf16[2,256,512]{2,1,0:T(8,128)(2,1)}, bf16[2,256,512]{2,1,0:T(8,128)(2,1)S(1)}, u32[]{:S(2)}, u32[]{:S(2)}) collective-permute-start(bf16[2,256,512]{2,1,0:T(8,128)(2,1)} %collective-permute-done.10.refs_2_), channel_id=1, source_target_pairs={{0,64},{64,0},{1,65},{65,1},{2,66},{66,2},{3,67},{67,3},{4,68},{68... | collective-permute-start | bytes 1572872 | tf_op jit(solution)/shard_map/ppermute | solution.py:41
  104.9 4.8 %copy-start.10 = (bf16[256,512]{1,0:T(8,128)(2,1)}, bf16[256,512]{1,0:T(8,128)(2,1)S(1)}, u32[]{:S(2)}) copy-start(bf16[256,512]{1,0:T(8,128)(2,1)S(1)} %collective-permute-done.12.refs_4_) | copy-start | bytes 786436
  104.9 10.4 %collective-permute-start.6 = (bf16[4,128,256]{2,1,0:T(8,128)(2,1)}, bf16[4,128,256]{2,1,0:T(8,128)(2,1)S(1)}, u32[]{:S(2)}, u32[]{:S(2)}) collective-permute-start(bf16[4,128,256]{2,1,0:T(8,128)(2,1)} %copy-done.16), channel_id=1, source_target_pairs={{0,8},{4,12},{8,0},{12,4},{1,9},{5,13},{9,1},{13,5},{2,10},{6,14},... | collective-permute-start | bytes 786440 | tf_op jit(solution)/shard_map/ppermute | solution.py:37
  108.1 12.9 %collective-permute-start.7 = (bf16[4,128,256]{2,1,0:T(8,128)(2,1)}, bf16[4,128,256]{2,1,0:T(8,128)(2,1)S(1)}, u32[]{:S(2)}, u32[]{:S(2)}) collective-permute-start(bf16[4,128,256]{2,1,0:T(8,128)(2,1)} %copy-done.16), channel_id=1, source_target_pairs={{0,4},{4,8},{8,12},{12,0},{1,5},{5,9},{9,13},{13,1},{2,6},{6,10},{... | collective-permute-start | bytes 786440 | tf_op jit(solution)/shard_map/ppermute | solution.py:37
  115.3 6.8 %collective-permute-start.16 = (bf16[256,512]{1,0:T(8,128)(2,1)S(1)}, bf16[256,512]{1,0:T(8,128)(2,1)S(1)}, u32[]{:S(2)}, u32[]{:S(2)}) collective-permute-start(bf16[256,512]{1,0:T(8,128)(2,1)S(1)} %collective-permute-done.11.refs_3_), channel_id=1, source_target_pairs={{0,64},{64,0},{1,65},{65,1},{2,66},{66,2},{3,67},{67,3},{4,68},{68... | collective-permute-start | bytes 786440 | tf_op jit(solution)/shard_map/ppermute | solution.py:41
  121.0 1.7 collective-permute-start.17
  122.7 1.0 copy-start.9
  123.7 0.9 copy-start.11
  126.8 2.0 copy-start.3
  128.8 2.2 %copy-start.4 = (bf16[16,256,512]{2,1,0:T(8,128)(2,1)S(1)}, bf16[16,256,512]{2,1,0:T(8,128)(2,1)}, u32[]{:S(2)}) copy-start(bf16[16,256,512]{2,1,0:T(8,128)(2,1)} %copy-done.3) | copy-start | bytes 12582916
  134.2 4.8 %collective-permute-start.21 = (bf16[8,256,512]{2,1,0:T(8,128)(2,1)S(1)}, bf16[8,256,512]{2,1,0:T(8,128)(2,1)S(1)}, u32[]{:S(2)}, u32[]{:S(2)}) collective-permute-start(bf16[8,256,512]{2,1,0:T(8,128)(2,1)S(1)} %shard_map.96), channel_id=1, source_target_pairs={{0,64},{64,0},{1,65},{65,1},{2,66},{66,2},{3,67},{67,3},{4,68},{68... | collective-permute-start | bytes 6291464 | tf_op jit(solution)/shard_map/ppermute | solution.py:41
  134.5 9.5 %collective-permute-start.18 = (bf16[4,128,256]{2,1,0:T(8,128)(2,1)S(1)}, bf16[4,128,256]{2,1,0:T(8,128)(2,1)S(1)}, u32[]{:S(2)}, u32[]{:S(2)}) collective-permute-start(bf16[4,128,256]{2,1,0:T(8,128)(2,1)S(1)} %get-tuple-element.134), channel_id=1, source_target_pairs={{0,4},{4,8},{8,12},{12,0},{1,5},{5,9},{9,13},{13,1},{2,6},{6,10},{... | collective-permute-start | bytes 786440 | tf_op jit(solution)/shard_map/ppermute | solution.py:37
  136.0 10.7 %collective-permute-start.19 = (bf16[4,128,256]{2,1,0:T(8,128)(2,1)S(1)}, bf16[4,128,256]{2,1,0:T(8,128)(2,1)S(1)}, u32[]{:S(2)}, u32[]{:S(2)}) collective-permute-start(bf16[4,128,256]{2,1,0:T(8,128)(2,1)S(1)} %get-tuple-element.133), channel_id=1, source_target_pairs={{0,8},{4,12},{8,0},{12,4},{1,9},{5,13},{9,1},{13,5},{2,10},{6,14},... | collective-permute-start | bytes 786440 | tf_op jit(solution)/shard_map/ppermute | solution.py:37
  139.0 53.8 %copy-start.14 = (s32[2]{0:T(128)S(1)}, s32[2]{0:T(128)}, u32[]{:S(2)}) copy-start(s32[2]{0:T(128)} %pad_add_fusion.at_ref.y_ref) | copy-start | bytes 28
  139.0 12.5 %collective-permute-start.20 = (bf16[4,128,256]{2,1,0:T(8,128)(2,1)S(1)}, bf16[4,128,256]{2,1,0:T(8,128)(2,1)S(1)}, u32[]{:S(2)}, u32[]{:S(2)}) collective-permute-start(bf16[4,128,256]{2,1,0:T(8,128)(2,1)S(1)} %get-tuple-element.132), channel_id=1, source_target_pairs={{0,12},{4,0},{8,4},{12,8},{1,13},{5,1},{9,5},{13,9},{2,14},{6,2},{... | collective-permute-start | bytes 786440 | tf_op jit(solution)/shard_map/ppermute | solution.py:37
  140.3 11.2 %collective-permute-start.22 = (bf16[256,512]{1,0:T(8,128)(2,1)S(1)}, bf16[256,512]{1,0:T(8,128)(2,1)S(1)}, u32[]{:S(2)}, u32[]{:S(2)}) collective-permute-start(bf16[256,512]{1,0:T(8,128)(2,1)S(1)} %get-tuple-element.112), channel_id=1, source_target_pairs={{0,16},{16,32},{32,48},{48,0},{1,17},{17,33},{33,49},{49,1},{2,18}... | collective-permute-start | bytes 786440 | tf_op jit(solution)/shard_map/ppermute | solution.py:37
  140.9 10.6 %collective-permute-start.23 = (bf16[256,512]{1,0:T(8,128)(2,1)S(1)}, bf16[256,512]{1,0:T(8,128)(2,1)S(1)}, u32[]{:S(2)}, u32[]{:S(2)}) collective-permute-start(bf16[256,512]{1,0:T(8,128)(2,1)S(1)} %get-tuple-element.113), channel_id=1, source_target_pairs={{0,48},{16,0},{32,16},{48,32},{1,49},{17,1},{33,17},{49,33},{2,50}... | collective-permute-start | bytes 786440 | tf_op jit(solution)/shard_map/ppermute | solution.py:37
  153.2 14.3 %all-to-all-start.4 = ((bf16[4,128,256]{2,1,0:T(8,128)(2,1)}), bf16[4,128,256]{2,1,0:T(8,128)(2,1)S(1)}, u32[]{:S(2)}, u32[]{:S(2)}) async-start(bf16[4,128,256]{2,1,0:T(8,128)(2,1)} %shard_map.99), calls=%async_computation.4 | async-start | bytes 524288 | tf_op jit(solution)/shard_map/all_to_all | solution.py:45
  160.2 13.5 %collective-permute-start.24 = (bf16[2,256,512]{2,1,0:T(8,128)(2,1)}, bf16[2,256,512]{2,1,0:T(8,128)(2,1)S(1)}, u32[]{:S(2)}, u32[]{:S(2)}) collective-permute-start(bf16[2,256,512]{2,1,0:T(8,128)(2,1)} %get-tuple-element.119), channel_id=1, source_target_pairs={{0,16},{16,32},{32,48},{48,0},{1,17},{17,33},{33,49},{49,1},{2,18}... | collective-permute-start | bytes 1572872 | tf_op jit(solution)/shard_map/ppermute | solution.py:37
  162.0 14.2 %collective-permute-start.25 = (bf16[2,256,512]{2,1,0:T(8,128)(2,1)S(1)}, bf16[2,256,512]{2,1,0:T(8,128)(2,1)S(1)}, u32[]{:S(2)}, u32[]{:S(2)}) collective-permute-start(bf16[2,256,512]{2,1,0:T(8,128)(2,1)S(1)} %get-tuple-element.120), channel_id=1, source_target_pairs={{0,48},{16,0},{32,16},{48,32},{1,49},{17,1},{33,17},{49,33},{2,50}... | collective-permute-start | bytes 1572872 | tf_op jit(solution)/shard_map/ppermute | solution.py:37
  168.2 11.6 %all-to-all-start.5 = ((bf16[4,128,256]{2,1,0:T(8,128)(2,1)}), bf16[4,128,256]{2,1,0:T(8,128)(2,1)S(1)}, u32[]{:S(2)}, u32[]{:S(2)}) async-start(bf16[4,128,256]{2,1,0:T(8,128)(2,1)} %shard_map.100), calls=%async_computation.5 | async-start | bytes 524288 | tf_op jit(solution)/shard_map/all_to_all | solution.py:45
  179.8 9.2 %collective-permute-start.26 = (bf16[4,128,256]{2,1,0:T(8,128)(2,1)S(1)}, bf16[4,128,256]{2,1,0:T(8,128)(2,1)S(1)}, u32[]{:S(2)}, u32[]{:S(2)}) collective-permute-start(bf16[4,128,256]{2,1,0:T(8,128)(2,1)S(1)} %all-to-all-done.5.refs_0_), channel_id=1, source_target_pairs={{0,12},{4,0},{8,4},{12,8},{1,13},{5,1},{9,5},{13,9},{2,14},{6,2},{... | collective-permute-start | bytes 786440 | tf_op jit(solution)/shard_map/ppermute | solution.py:37
  180.5 11.4 %collective-permute-start.27 = (bf16[4,128,256]{2,1,0:T(8,128)(2,1)S(1)}, bf16[4,128,256]{2,1,0:T(8,128)(2,1)S(1)}, u32[]{:S(2)}, u32[]{:S(2)}) collective-permute-start(bf16[4,128,256]{2,1,0:T(8,128)(2,1)S(1)} %all-to-all-done.5.refs_0_), channel_id=1, source_target_pairs={{0,8},{4,12},{8,0},{12,4},{1,9},{5,13},{9,1},{13,5},{2,10},{6,14},... | collective-permute-start | bytes 786440 | tf_op jit(solution)/shard_map/ppermute | solution.py:37
  182.6 10.2 %collective-permute-start.28 = (bf16[4,128,256]{2,1,0:T(8,128)(2,1)S(1)}, bf16[4,128,256]{2,1,0:T(8,128)(2,1)S(1)}, u32[]{:S(2)}, u32[]{:S(2)}) collective-permute-start(bf16[4,128,256]{2,1,0:T(8,128)(2,1)S(1)} %all-to-all-done.5.refs_0_), channel_id=1, source_target_pairs={{0,4},{4,8},{8,12},{12,0},{1,5},{5,9},{9,13},{13,1},{2,6},{6,10},{... | collective-permute-start | bytes 786440 | tf_op jit(solution)/shard_map/ppermute | solution.py:37
  185.5 15.8 %collective-permute-start.29 = (bf16[256,512]{1,0:T(8,128)(2,1)S(1)}, bf16[256,512]{1,0:T(8,128)(2,1)S(1)}, u32[]{:S(2)}, u32[]{:S(2)}) collective-permute-start(bf16[256,512]{1,0:T(8,128)(2,1)S(1)} %get-tuple-element.128), channel_id=1, source_target_pairs={{0,128},{128,0},{1,129},{129,1},{2,130},{130,2},{3,131},{131,3},{4... | collective-permute-start | bytes 786440 | tf_op jit(solution)/shard_map/ppermute | solution.py:41
  192.8 1.6 copy-start.2

commit v4 on v3

--- a/solution.py
+++ b/solution.py
@@ -259,7 +259,7 @@
 
     sent, mine = teacher_terms(here, act, down, 2, 4)
     student = call(sum_body, [shape(1, 4, tok, cols)], [student])[0][0]
-    sent, student = tied(sent, student)
+    sent, student, pair = tied(sent, student, pair)
     came = swapped(sent, "c")
     student = exchanged(student, "zl")
     width = t_resid.shape[1]

time: 204 us -> 196 us (0.961)
  starting transfers between devices: 79.1 us -> 66.4 us
  blocking collectives: 0 us -> 10.3 us
  Pallas kernels: 37.5 us -> 34.3 us
  waiting for transfers between devices: 62.5 us -> 59.8 us
    ppermute x9, waiting for transfers between devices: 23.8 us -> 9.7 us  [swapped(): return lax.ppermute(x, axis, [(0, 1), (1, 0)])]
    all_to_all x6 -> x5, starting transfers between devices: 37.1 us -> 26.1 us  [exchanged(): return lax.all_to_all(x, axes, 0, 0, tiled=True)]
    ppermute x21, waiting for transfers between devices: 26.7 us -> 37.6 us  [moved_by(): return lax.ppermute(x, axes, [(i, (i + step) % n) for i in range(n)])]
    all_to_all x0 -> x1, blocking collectives: none -> 10.3 us  [exchanged(): return lax.all_to_all(x, axes, 0, 0, tiled=True)]
    ppermute x21, starting transfers between devices: 33.1 us -> 28.5 us  [moved_by(): return lax.ppermute(x, axes, [(i, (i + step) % n) for i in range(n)])]
    pallas_call x14, Pallas kernels: 18.4 us -> 15.2 us  [call(): pl.pallas_call(body, out_shape=outs, in_specs=specs or [VMEM] * len(args)...]
    ppermute x9, starting transfers between devices: 8.96 us -> 11.8 us  [swapped(): return lax.ppermute(x, axis, [(0, 1), (1, 0)])]
    all_to_all x6 -> x5, waiting for transfers between devices: 12.1 us -> 12.6 us  [exchanged(): return lax.all_to_all(x, axes, 0, 0, tiled=True)]
  transfers between devices with their start and end apart: 36 -> 35, of which waited for: 19 -> 22; matrix products, arithmetic and copies ran while one was open for 3% -> 3% of each run, Pallas kernels for 13% -> 13%
where the time goes in v4:
time: 196 us; the launch traced here: 193 us
  starting transfers between devices  66.4 us (34%)
  waiting for transfers between devices  59.8 us (31%)
  Pallas kernels  34.3 us (17%)
  local copies, waits for them, and re-layouts  18.8 us (10%)
  blocking collectives  10.3 us (5%)
  other arithmetic  2.39 us (1%)
    ppermute x21, waiting for transfers between devices, moved_by(): return lax.ppermute(x, axes, [(i, (i + step) % n) for i in range(n)])  37.6 us
    ppermute x21, starting transfers between devices, moved_by(): return lax.ppermute(x, axes, [(i, (i + step) % n) for i in range(n)])  28.5 us
    all_to_all x5, starting transfers between devices, exchanged(): return lax.all_to_all(x, axes, 0, 0, tiled=True)  26.1 us
    unnamed x37, local copies, waits for them, and re-layouts  16.6 us
    pallas_call x14, Pallas kernels, call(): pl.pallas_call(body, out_shape=outs, in_specs=specs or [VMEM] * len(args)...  15.2 us
    all_to_all x5, waiting for transfers between devices, exchanged(): return lax.all_to_all(x, axes, 0, 0, tiled=True)  12.6 us
    ppermute x9, starting transfers between devices, swapped(): return lax.ppermute(x, axis, [(0, 1), (1, 0)])  11.8 us
    pallas_call x1, Pallas kernels, teacher_terms(): pl.pallas_call(teacher_body, grid_spec=pltpu.PrefetchScalarGridSpec(num_s...  11.7 us
  transfers between devices with their start and end apart: 35, of which 22 were waited for; matrix products, arithmetic and copies ran while one was open for 3% of the time, Pallas kernels for 13%

profile of v4, /device:TPU:46, one launch (start us, length us, event | category | flops | bytes accessed | tf_op | source)
XLA Modules:
  0.0 192.9 jit_solution(11942275051514496326)
XLA Ops:
  0.7 1.7 copy-done.1
  3.2 1.4 shard_map.86
  4.6 4.9 %all-to-all-start = ((bf16[4,4,128,256]{3,2,1,0:T(8,128)(2,1)}), bf16[4,4,128,256]{3,2,1,0:T(8,128)(2,1)S(1)}, u32[]{:S(2)}, u32[]{:S(2)}) async-start(bf16[4,4,128,256]{3,2,1,0:T(8,128)(2,1)} %shard_map.86), calls=%async_computation | async-start | bytes 2097152 | tf_op jit(solution)/shard_map/all_to_all | solution.py:45
  9.5 6.3 %collective-permute-start = (bf16[256,512]{1,0:T(8,128)(2,1)S(1)}, bf16[256,512]{1,0:T(8,128)(2,1)S(1)}, u32[]{:S(2)}, u32[]{:S(2)}) collective-permute-start(bf16[256,512]{1,0:T(8,128)(2,1)S(1)} %copy-done.16), channel_id=1, source_target_pairs={{0,128},{128,0},{1,129},{129,1},{2,130},{130,2},{3,131},{131,3},{4... | collective-permute-start | bytes 786440 | tf_op jit(solution)/shard_map/ppermute | solution.py:41
  16.4 11.7 %shard_map.87 = (bf16[4,2,4,128,512]{4,3,2,1,0:T(8,128)(2,1)}, bf16[4,2,4,128,512]{4,3,2,1,0:T(8,128)(2,1)}) custom-call(s32[2]{0:T(128)} %pad_add_fusion.at_ref.y_ref, bf16[4,448,128]{2,1,0:T(8,128)(2,1)} %bitcast.40, bf16[448,8192]{1,0:T(8,128)(2,1)} %w_ref.4), custom_call_target="tpu_custom_call" | custom-call | flops 1 | bytes 1 | tf_op jit(solution)/shard_map/pallas_call | solution.py:77
  29.9 7.4 %collective-permute-done.1.refs_1_.refs_3_.refs_5_.came_ref = bf16[4,8,128,512]{3,2,1,0:T(8,128)(2,1)S(1)} collective-permute-done((bf16[4,8,128,512]{3,2,1,0:T(8,128)(2,1)}, bf16[4,8,128,512]{3,2,1,0:T(8,128)(2,1)S(1)}, u32[]{:S(2)}, u32[]{:S(2)}) %collective-permute-start.1) | collective-permute-done | bytes 4194336 | tf_op jit(solution)/shard_map/ppermute | solution.py:41
  37.2 2.0 %copy-done.15 = bf16[4,8,128,512]{3,2,1,0:T(8,128)(2,1)} copy-done((bf16[4,8,128,512]{3,2,1,0:T(8,128)(2,1)}, bf16[4,8,128,512]{3,2,1,0:T(8,128)(2,1)S(1)}, u32[]{:S(2)}) %copy-start.15) | copy-done | bytes 4194328
  39.2 2.7 %shard_map.91 = (bf16[4,128,512]{2,1,0:T(8,128)(2,1)}, bf16[4,128,512]{2,1,0:T(8,128)(2,1)}) custom-call(bf16[4,8,128,512]{3,2,1,0:T(8,128)(2,1)} %bitcast.36, bf16[4,8,128,512]{3,2,1,0:T(8,128)(2,1)} %copy-done.15), custom_call_target="tpu_custom_call" | custom-call | flops 1 | bytes 1 | tf_op jit(solution)/shard_map/pallas_call | solution.py:120
  41.9 1.5 collective-permute-start.2
  44.0 4.4 %all-to-all-start.1 = ((bf16[4,128,256]{2,1,0:T(8,128)(2,1)}), bf16[4,128,256]{2,1,0:T(8,128)(2,1)S(1)}, u32[]{:S(2)}, u32[]{:S(2)}) async-start(bf16[4,128,256]{2,1,0:T(8,128)(2,1)} %bitcast.20), calls=%async_computation.1 | async-start | bytes 524288 | tf_op jit(solution)/shard_map/all_to_all | solution.py:45
  48.4 4.7 %shard_map.89 = (bf16[8,128,512]{2,1,0:T(8,128)(2,1)}, bf16[8,128,512]{2,1,0:T(8,128)(2,1)}, bf16[8,128,512]{2,1,0:T(8,128)(2,1)}) custom-call(bf16[4,8,128,512]{3,2,1,0:T(8,128)(2,1)} %bitcast.37, bf16[4,8,128,512]{3,2,1,0:T(8,128)(2,1)} %copy-done.15, bf16[4,8,128,512]{3,2,1,0:T(8,128)(2,1)} %bitcast.38, bf16[4,8,128,512]{3,2,1,0:T(8,128)(2,1)} %copy-done.15, ...), custom_call_target="tpu_custom_call" | custom-call | flops 1 | bytes 1 | tf_op jit(solution)/shard_map/pallas_call | solution.py:120
  53.1 2.4 %all-to-all-done.1.x_ref = bf16[4,128,256]{2,1,0:T(8,128)(2,1)S(1)} async-done(((bf16[4,128,256]{2,1,0:T(8,128)(2,1)}), bf16[4,128,256]{2,1,0:T(8,128)(2,1)S(1)}, u32[]{:S(2)}, u32[]{:S(2)}) %all-to-all-start.1) | async-done | bytes 262176 | tf_op jit(solution)/shard_map/all_to_all | solution.py:45
  56.1 1.2 collective-permute-done.3.far_down
  57.3 1.2 copy-done.5
  58.5 1.2 copy-done.6
  60.0 1.2 collective-permute-start.4
  62.1 10.3 %all_to_all.30 = bf16[4,128,256]{2,1,0:T(8,128)(2,1)} all-to-all(bf16[4,128,256]{2,1,0:T(8,128)(2,1)S(1)} %shard_map.90), channel_id=1, replica_groups=mesh['zh'=2,'c'=2,'x'=4,'y'=4,'zl'=4] {'zl'}, dimensions={0} | all-to-all | bytes 524288 | tf_op jit(solution)/shard_map/all_to_all | solution.py:45
  73.3 2.4 %collective-permute-start.10 = (bf16[2,256,512]{2,1,0:T(8,128)(2,1)}, bf16[2,256,512]{2,1,0:T(8,128)(2,1)}, u32[]{:S(2)}, u32[]{:S(2)}) collective-permute-start(bf16[2,256,512]{2,1,0:T(8,128)(2,1)} %pad_maximum_fusion.refs_0_), channel_id=1, source_target_pairs={{0,16},{16,32},{32,48},{48,0},{1,17},{17,33},{33,49},{49,1},{2,18}... | collective-permute-start | bytes 1572872 | tf_op jit(solution)/shard_map/ppermute | solution.py:37
  75.7 8.5 %collective-permute-done.4.refs_1_ = bf16[8,128,512]{2,1,0:T(8,128)(2,1)S(1)} collective-permute-done((bf16[8,128,512]{2,1,0:T(8,128)(2,1)S(1)}, bf16[8,128,512]{2,1,0:T(8,128)(2,1)S(1)}, u32[]{:S(2)}, u32[]{:S(2)}) %collective-permute-start.4) | collective-permute-done | bytes 1048608 | tf_op jit(solution)/shard_map/ppermute | solution.py:37
  84.2 1.0 collective-permute-done.5.refs_2_
  85.1 1.4 shard_map.93
  86.5 6.4 %all-to-all-start.3 = ((bf16[8,128,512]{2,1,0:T(8,128)(2,1)}), bf16[8,128,512]{2,1,0:T(8,128)(2,1)S(1)}, u32[]{:S(2)}, u32[]{:S(2)}) async-start(bf16[8,128,512]{2,1,0:T(8,128)(2,1)} %shard_map.93), calls=%async_computation.3 | async-start | bytes 2097152 | tf_op jit(solution)/shard_map/all_to_all | solution.py:45
  92.9 1.0 slice_bitcast_fusion.5
  93.9 0.9 collective-permute-start.11
  94.8 1.0 slice_bitcast_fusion.4
  95.8 2.5 %collective-permute-start.12 = (bf16[256,512]{1,0:T(8,128)(2,1)S(1)}, bf16[256,512]{1,0:T(8,128)(2,1)S(1)}, u32[]{:S(2)}, u32[]{:S(2)}) collective-permute-start(bf16[256,512]{1,0:T(8,128)(2,1)S(1)} %slice_bitcast_fusion.4), channel_id=1, source_target_pairs={{0,16},{16,32},{32,48},{48,0},{1,17},{17,33},{33,49},{49,1},{2,18}... | collective-permute-start | bytes 786440 | tf_op jit(solution)/shard_map/ppermute | solution.py:37
  98.2 1.0 collective-permute-start.6
  100.1 1.5 collective-permute-done.11.refs_3_
  102.2 2.7 %collective-permute-start.7 = (bf16[4,128,256]{2,1,0:T(8,128)(2,1)}, bf16[4,128,256]{2,1,0:T(8,128)(2,1)S(1)}, u32[]{:S(2)}, u32[]{:S(2)}) collective-permute-start(bf16[4,128,256]{2,1,0:T(8,128)(2,1)} %all_to_all.30), channel_id=1, source_target_pairs={{0,8},{4,12},{8,0},{12,4},{1,9},{5,13},{9,1},{13,5},{2,10},{6,14},... | collective-permute-start | bytes 786440 | tf_op jit(solution)/shard_map/ppermute | solution.py:37
  105.0 1.5 collective-permute-start.8
  106.4 1.0 constant_dynamic-update-slice_fusion.3
  107.4 4.6 %collective-permute-done.7 = bf16[4,128,256]{2,1,0:T(8,128)(2,1)S(1)} collective-permute-done((bf16[4,128,256]{2,1,0:T(8,128)(2,1)}, bf16[4,128,256]{2,1,0:T(8,128)(2,1)S(1)}, u32[]{:S(2)}, u32[]{:S(2)}) %collective-permute-start.7) | collective-permute-done | bytes 262176 | tf_op jit(solution)/shard_map/ppermute | solution.py:37
  112.0 5.7 %collective-permute-done.8 = bf16[4,128,256]{2,1,0:T(8,128)(2,1)S(1)} collective-permute-done((bf16[4,128,256]{2,1,0:T(8,128)(2,1)}, bf16[4,128,256]{2,1,0:T(8,128)(2,1)S(1)}, u32[]{:S(2)}, u32[]{:S(2)}) %collective-permute-start.8) | collective-permute-done | bytes 262176 | tf_op jit(solution)/shard_map/ppermute | solution.py:37
  117.7 1.0 constant_dynamic-update-slice_fusion.2
  119.4 0.9 copy-done.9
  120.4 0.9 copy-done.11
  121.3 2.1 %shard_map.94 = (f32[128,512]{1,0:T(8,128)S(1)}, bf16[16,256,512]{2,1,0:T(8,128)(2,1)S(1)}) custom-call(s32[16]{0:T(128)S(1)} %fusion.at_ref, bf16[16,128,256]{2,1,0:T(8,128)(2,1)S(1)} %constant_dynamic-update-slice_fusion.h_ref, bf16[2,256,512]{2,1,0:T(8,128)(2,1)} %pad_maximum_fusion.refs_0_, bf16[2,256,512]{2,1,0:T(8,128)(2,1)} %collective-permute-done.9.refs_1_, ...), custom_call_target="tpu_custom_call" | custom-call | flops 1 | bytes 1 | tf_op jit(solution)/shard_map/pallas_call | solution.py:25
  123.5 2.0 %copy-done.3 = bf16[16,256,512]{2,1,0:T(8,128)(2,1)} copy-done((bf16[16,256,512]{2,1,0:T(8,128)(2,1)}, bf16[16,256,512]{2,1,0:T(8,128)(2,1)S(1)}, u32[]{:S(2)}) %copy-start.3) | copy-done | bytes 4194328
  125.4 2.2 %copy-done.4 = bf16[16,256,512]{2,1,0:T(8,128)(2,1)S(1)} copy-done((bf16[16,256,512]{2,1,0:T(8,128)(2,1)S(1)}, bf16[16,256,512]{2,1,0:T(8,128)(2,1)}, u32[]{:S(2)}) %copy-start.4) | copy-done | bytes 4194328
  127.6 2.0 %shard_map.95 = (bf16[128,512]{1,0:T(8,128)(2,1)S(1)}, bf16[4,4,128,256]{3,2,1,0:T(8,128)(2,1)S(1)}) custom-call(s32[16]{0:T(128)S(1)} %fusion.at_ref, f32[128,512]{1,0:T(8,128)S(1)} %get-tuple-element.104.mapped_ref, bf16[128,512]{1,0:T(8,128)(2,1)S(1)} %copy-done.12, bf16[8,128,512]{2,1,0:T(8,128)(2,1)S(1)} %all-to-all-done.3.terms_ref, ...), custom_call_target="tpu_custom_call" | custom-call | flops 1 | bytes 1 | tf_op jit(solution)/shard_map/pallas_call | solution.py:25
  129.6 1.3 shard_map.96
  131.2 1.3 collective-permute-start.18
  132.5 2.3 %collective-permute-start.19 = (bf16[4,128,256]{2,1,0:T(8,128)(2,1)S(1)}, bf16[4,128,256]{2,1,0:T(8,128)(2,1)S(1)}, u32[]{:S(2)}, u32[]{:S(2)}) collective-permute-start(bf16[4,128,256]{2,1,0:T(8,128)(2,1)S(1)} %get-tuple-element.135), channel_id=1, source_target_pairs={{0,8},{4,12},{8,0},{12,4},{1,9},{5,13},{9,1},{13,5},{2,10},{6,14},... | collective-permute-start | bytes 786440 | tf_op jit(solution)/shard_map/ppermute | solution.py:37
  135.1 1.3 shard_map.97
  136.5 2.0 %collective-permute-start.23 = (bf16[256,512]{1,0:T(8,128)(2,1)S(1)}, bf16[256,512]{1,0:T(8,128)(2,1)S(1)}, u32[]{:S(2)}, u32[]{:S(2)}) collective-permute-start(bf16[256,512]{1,0:T(8,128)(2,1)S(1)} %get-tuple-element.115), channel_id=1, source_target_pairs={{0,48},{16,0},{32,16},{48,32},{1,49},{17,1},{33,17},{49,33},{2,50}... | collective-permute-start | bytes 786440 | tf_op jit(solution)/shard_map/ppermute | solution.py:37
  138.5 1.9 collective-permute-done.18.refs_1_
  140.4 2.8 %collective-permute-done.19.refs_2_ = bf16[4,128,256]{2,1,0:T(8,128)(2,1)S(1)} collective-permute-done((bf16[4,128,256]{2,1,0:T(8,128)(2,1)S(1)}, bf16[4,128,256]{2,1,0:T(8,128)(2,1)S(1)}, u32[]{:S(2)}, u32[]{:S(2)}) %collective-permute-start.19) | collective-permute-done | bytes 262176 | tf_op jit(solution)/shard_map/ppermute | solution.py:37
  143.2 4.7 %collective-permute-done.20.refs_3_ = bf16[4,128,256]{2,1,0:T(8,128)(2,1)S(1)} collective-permute-done((bf16[4,128,256]{2,1,0:T(8,128)(2,1)S(1)}, bf16[4,128,256]{2,1,0:T(8,128)(2,1)S(1)}, u32[]{:S(2)}, u32[]{:S(2)}) %collective-permute-start.20) | collective-permute-done | bytes 262176 | tf_op jit(solution)/shard_map/ppermute | solution.py:37
  147.9 0.9 shard_map.98
  149.6 5.1 %all-to-all-start.4 = ((bf16[4,128,256]{2,1,0:T(8,128)(2,1)}), bf16[4,128,256]{2,1,0:T(8,128)(2,1)S(1)}, u32[]{:S(2)}, u32[]{:S(2)}) async-start(bf16[4,128,256]{2,1,0:T(8,128)(2,1)} %shard_map.99), calls=%async_computation.4 | async-start | bytes 524288 | tf_op jit(solution)/shard_map/all_to_all | solution.py:45
  154.8 2.0 %collective-permute-start.25 = (bf16[2,256,512]{2,1,0:T(8,128)(2,1)S(1)}, bf16[2,256,512]{2,1,0:T(8,128)(2,1)S(1)}, u32[]{:S(2)}, u32[]{:S(2)}) collective-permute-start(bf16[2,256,512]{2,1,0:T(8,128)(2,1)S(1)} %get-tuple-element.122), channel_id=1, source_target_pairs={{0,48},{16,0},{32,16},{48,32},{1,49},{17,1},{33,17},{49,33},{2,50}... | collective-permute-start | bytes 1572872 | tf_op jit(solution)/shard_map/ppermute | solution.py:37
  156.8 5.2 %all-to-all-done.4.x_ref = bf16[4,128,256]{2,1,0:T(8,128)(2,1)S(1)} async-done(((bf16[4,128,256]{2,1,0:T(8,128)(2,1)}), bf16[4,128,256]{2,1,0:T(8,128)(2,1)S(1)}, u32[]{:S(2)}, u32[]{:S(2)}) %all-to-all-start.4) | async-done | bytes 262176 | tf_op jit(solution)/shard_map/all_to_all | solution.py:45
  162.7 5.3 %all-to-all-start.5 = ((bf16[4,128,256]{2,1,0:T(8,128)(2,1)}), bf16[4,128,256]{2,1,0:T(8,128)(2,1)S(1)}, u32[]{:S(2)}, u32[]{:S(2)}) async-start(bf16[4,128,256]{2,1,0:T(8,128)(2,1)} %shard_map.100), calls=%async_computation.5 | async-start | bytes 524288 | tf_op jit(solution)/shard_map/all_to_all | solution.py:45
  168.2 1.0 collective-permute-done.25.refs_2_
  169.2 5.0 %all-to-all-done.5.refs_0_ = bf16[4,128,256]{2,1,0:T(8,128)(2,1)S(1)} async-done(((bf16[4,128,256]{2,1,0:T(8,128)(2,1)}), bf16[4,128,256]{2,1,0:T(8,128)(2,1)S(1)}, u32[]{:S(2)}, u32[]{:S(2)}) %all-to-all-start.5) | async-done | bytes 262176 | tf_op jit(solution)/shard_map/all_to_all | solution.py:45
  174.3 2.3 %collective-permute-start.27 = (bf16[4,128,256]{2,1,0:T(8,128)(2,1)S(1)}, bf16[4,128,256]{2,1,0:T(8,128)(2,1)S(1)}, u32[]{:S(2)}, u32[]{:S(2)}) collective-permute-start(bf16[4,128,256]{2,1,0:T(8,128)(2,1)S(1)} %all-to-all-done.5.refs_0_), channel_id=1, source_target_pairs={{0,8},{4,12},{8,0},{12,4},{1,9},{5,13},{9,1},{13,5},{2,10},{6,14},... | collective-permute-start | bytes 786440 | tf_op jit(solution)/shard_map/ppermute | solution.py:37
  176.5 2.6 %collective-permute-start.28 = (bf16[4,128,256]{2,1,0:T(8,128)(2,1)S(1)}, bf16[4,128,256]{2,1,0:T(8,128)(2,1)S(1)}, u32[]{:S(2)}, u32[]{:S(2)}) collective-permute-start(bf16[4,128,256]{2,1,0:T(8,128)(2,1)S(1)} %all-to-all-done.5.refs_0_), channel_id=1, source_target_pairs={{0,4},{4,8},{8,12},{12,0},{1,5},{5,9},{9,13},{13,1},{2,6},{6,10},{... | collective-permute-start | bytes 786440 | tf_op jit(solution)/shard_map/ppermute | solution.py:37
  179.4 4.5 %collective-permute-start.29 = (bf16[256,512]{1,0:T(8,128)(2,1)S(1)}, bf16[256,512]{1,0:T(8,128)(2,1)S(1)}, u32[]{:S(2)}, u32[]{:S(2)}) collective-permute-start(bf16[256,512]{1,0:T(8,128)(2,1)S(1)} %get-tuple-element.130), channel_id=1, source_target_pairs={{0,128},{128,0},{1,129},{129,1},{2,130},{130,2},{3,131},{131,3},{4... | collective-permute-start | bytes 786440 | tf_op jit(solution)/shard_map/ppermute | solution.py:41
  183.9 1.9 collective-permute-done.27.refs_2_
  185.8 1.3 collective-permute-done.28.refs_3_
  187.1 1.6 copy-done.2
  188.7 2.0 %shard_map.101 = bf16[128,256]{1,0:T(8,128)(2,1)} custom-call(s32[2]{0:T(128)S(1)} %copy-done.14, bf16[256,4096]{1,0:T(8,128)(2,1)S(1)} %copy-done.2, bf16[4,128,256]{2,1,0:T(8,128)(2,1)S(1)} %all-to-all-done.5.refs_0_, bf16[4,128,256]{2,1,0:T(8,128)(2,1)S(1)} %collective-permute-done.26.refs_1_, bf16[4,128,256]{2,1,0:T(8,128)(2,1)S(1)} %collective-permute-done.27.refs_2_, ...), custom_call_target="tpu_custom_call" | custom-call | flops 1 | bytes 1 | tf_op jit(solution)/shard_map/pallas_call | solution.py:25
  190.7 1.3 collective-permute-done.29
  192.1 0.9 convert_add_fusion
  (71 shorter events, 11.6 us)
Async XLA Ops:
  0.6 47.7 %copy-start = (bf16[128,4096]{1,0:T(8,128)(2,1)S(1)}, bf16[128,4096]{1,0:T(8,128)(2,1)}, u32[]{:S(2)}) copy-start(bf16[128,4096]{1,0:T(8,128)(2,1)} %param.12) | copy-start | bytes 3145732
  0.6 1.7 copy-start.1
  2.3 0.8 copy-start.13
  3.2 6.3 %copy-start.16 = (bf16[256,512]{1,0:T(8,128)(2,1)S(1)}, bf16[256,512]{1,0:T(8,128)(2,1)}, u32[]{:S(2)}) copy-start(bf16[256,512]{1,0:T(8,128)(2,1)} %param.13) | copy-start | bytes 786436
  4.6 24.4 %all-to-all-start = ((bf16[4,4,128,256]{3,2,1,0:T(8,128)(2,1)}), bf16[4,4,128,256]{3,2,1,0:T(8,128)(2,1)S(1)}, u32[]{:S(2)}, u32[]{:S(2)}) async-start(bf16[4,4,128,256]{3,2,1,0:T(8,128)(2,1)} %shard_map.86), calls=%async_computation | async-start | bytes 2097152 | tf_op jit(solution)/shard_map/all_to_all | solution.py:45
  9.5 18.7 %collective-permute-start = (bf16[256,512]{1,0:T(8,128)(2,1)S(1)}, bf16[256,512]{1,0:T(8,128)(2,1)S(1)}, u32[]{:S(2)}, u32[]{:S(2)}) collective-permute-start(bf16[256,512]{1,0:T(8,128)(2,1)S(1)} %copy-done.16), channel_id=1, source_target_pairs={{0,128},{128,0},{1,129},{129,1},{2,130},{130,2},{3,131},{131,3},{4... | collective-permute-start | bytes 786440 | tf_op jit(solution)/shard_map/ppermute | solution.py:41
  29.9 7.4 %collective-permute-start.1 = (bf16[4,8,128,512]{3,2,1,0:T(8,128)(2,1)}, bf16[4,8,128,512]{3,2,1,0:T(8,128)(2,1)S(1)}, u32[]{:S(2)}, u32[]{:S(2)}) collective-permute-start(bf16[4,8,128,512]{3,2,1,0:T(8,128)(2,1)} %bitcast.43), channel_id=1, source_target_pairs={{0,64},{64,0},{1,65},{65,1},{2,66},{66,2},{3,67},{67,3},{4,68},{68... | collective-permute-start | bytes 12582920 | tf_op jit(solution)/shard_map/ppermute | solution.py:41
  37.2 2.0 %copy-start.15 = (bf16[4,8,128,512]{3,2,1,0:T(8,128)(2,1)}, bf16[4,8,128,512]{3,2,1,0:T(8,128)(2,1)S(1)}, u32[]{:S(2)}) copy-start(bf16[4,8,128,512]{3,2,1,0:T(8,128)(2,1)S(1)} %collective-permute-done.1.refs_1_.refs_3_.refs_5_.came_ref) | copy-start | bytes 12582916
  41.9 14.2 %collective-permute-start.2 = (bf16[4,128,512]{2,1,0:T(8,128)(2,1)}, bf16[4,128,512]{2,1,0:T(8,128)(2,1)S(1)}, u32[]{:S(2)}, u32[]{:S(2)}) collective-permute-start(bf16[4,128,512]{2,1,0:T(8,128)(2,1)} %get-tuple-element.81), channel_id=1, source_target_pairs={{0,4},{4,8},{8,12},{12,0},{1,5},{5,9},{9,13},{13,1},{2,6},{6,10},{... | collective-permute-start | bytes 1572872 | tf_op jit(solution)/shard_map/ppermute | solution.py:37
  43.4 13.9 %collective-permute-start.3 = (bf16[4,128,512]{2,1,0:T(8,128)(2,1)}, bf16[4,128,512]{2,1,0:T(8,128)(2,1)S(1)}, u32[]{:S(2)}, u32[]{:S(2)}) collective-permute-start(bf16[4,128,512]{2,1,0:T(8,128)(2,1)} %get-tuple-element.82), channel_id=1, source_target_pairs={{0,12},{4,0},{8,4},{12,8},{1,13},{5,1},{9,5},{13,9},{2,14},{6,2},{... | collective-permute-start | bytes 1572872 | tf_op jit(solution)/shard_map/ppermute | solution.py:37
  44.0 11.5 %all-to-all-start.1 = ((bf16[4,128,256]{2,1,0:T(8,128)(2,1)}), bf16[4,128,256]{2,1,0:T(8,128)(2,1)S(1)}, u32[]{:S(2)}, u32[]{:S(2)}) async-start(bf16[4,128,256]{2,1,0:T(8,128)(2,1)} %bitcast.20), calls=%async_computation.1 | async-start | bytes 524288 | tf_op jit(solution)/shard_map/all_to_all | solution.py:45
  57.3 1.2 copy-start.5
  58.5 1.2 copy-start.6
  59.8 25.4 %copy-start.7 = (bf16[8,128,512]{2,1,0:T(8,128)(2,1)S(1)}, bf16[8,128,512]{2,1,0:T(8,128)(2,1)}, u32[]{:S(2)}) copy-start(bf16[8,128,512]{2,1,0:T(8,128)(2,1)} %get-tuple-element.77.refs_0_) | copy-start | bytes 3145732
  60.0 24.1 %collective-permute-start.4 = (bf16[8,128,512]{2,1,0:T(8,128)(2,1)S(1)}, bf16[8,128,512]{2,1,0:T(8,128)(2,1)S(1)}, u32[]{:S(2)}, u32[]{:S(2)}) collective-permute-start(bf16[8,128,512]{2,1,0:T(8,128)(2,1)S(1)} %get-tuple-element.87), channel_id=1, source_target_pairs={{0,4},{4,8},{8,12},{12,0},{1,5},{5,9},{9,13},{13,1},{2,6},{6,10},{... | collective-permute-start | bytes 3145736 | tf_op jit(solution)/shard_map/ppermute | solution.py:37
  61.3 23.8 %collective-permute-start.5 = (bf16[8,128,512]{2,1,0:T(8,128)(2,1)S(1)}, bf16[8,128,512]{2,1,0:T(8,128)(2,1)S(1)}, u32[]{:S(2)}, u32[]{:S(2)}) collective-permute-start(bf16[8,128,512]{2,1,0:T(8,128)(2,1)S(1)} %get-tuple-element.88), channel_id=1, source_target_pairs={{0,12},{4,0},{8,4},{12,8},{1,13},{5,1},{9,5},{13,9},{2,14},{6,2},{... | collective-permute-start | bytes 3145736 | tf_op jit(solution)/shard_map/ppermute | solution.py:37
  72.5 20.4 %collective-permute-start.9 = (bf16[2,256,512]{2,1,0:T(8,128)(2,1)}, bf16[2,256,512]{2,1,0:T(8,128)(2,1)}, u32[]{:S(2)}, u32[]{:S(2)}) collective-permute-start(bf16[2,256,512]{2,1,0:T(8,128)(2,1)} %pad_maximum_fusion.refs_0_), channel_id=1, source_target_pairs={{0,48},{16,0},{32,16},{48,32},{1,49},{17,1},{33,17},{49,33},{2,50}... | collective-permute-start | bytes 1572872 | tf_op jit(solution)/shard_map/ppermute | solution.py:37
  73.3 19.6 %collective-permute-start.10 = (bf16[2,256,512]{2,1,0:T(8,128)(2,1)}, bf16[2,256,512]{2,1,0:T(8,128)(2,1)}, u32[]{:S(2)}, u32[]{:S(2)}) collective-permute-start(bf16[2,256,512]{2,1,0:T(8,128)(2,1)} %pad_maximum_fusion.refs_0_), channel_id=1, source_target_pairs={{0,16},{16,32},{32,48},{48,0},{1,17},{17,33},{33,49},{49,1},{2,18}... | collective-permute-start | bytes 1572872 | tf_op jit(solution)/shard_map/ppermute | solution.py:37
  86.5 38.9 %all-to-all-start.3 = ((bf16[8,128,512]{2,1,0:T(8,128)(2,1)}), bf16[8,128,512]{2,1,0:T(8,128)(2,1)S(1)}, u32[]{:S(2)}, u32[]{:S(2)}) async-start(bf16[8,128,512]{2,1,0:T(8,128)(2,1)} %shard_map.93), calls=%async_computation.3 | async-start | bytes 2097152 | tf_op jit(solution)/shard_map/all_to_all | solution.py:45
  93.9 31.6 %copy-start.12 = (bf16[128,512]{1,0:T(8,128)(2,1)S(1)}, bf16[128,512]{1,0:T(8,128)(2,1)}, u32[]{:S(2)}) copy-start(bf16[128,512]{1,0:T(8,128)(2,1)} %resid_ref.1) | copy-start | bytes 393220
  93.9 7.7 %collective-permute-start.11 = (bf16[256,512]{1,0:T(8,128)(2,1)S(1)}, bf16[256,512]{1,0:T(8,128)(2,1)S(1)}, u32[]{:S(2)}, u32[]{:S(2)}) collective-permute-start(bf16[256,512]{1,0:T(8,128)(2,1)S(1)} %slice_bitcast_fusion.5), channel_id=1, source_target_pairs={{0,48},{16,0},{32,16},{48,32},{1,49},{17,1},{33,17},{49,33},{2,50}... | collective-permute-start | bytes 786440 | tf_op jit(solution)/shard_map/ppermute | solution.py:37
  95.8 6.4 %collective-permute-start.12 = (bf16[256,512]{1,0:T(8,128)(2,1)S(1)}, bf16[256,512]{1,0:T(8,128)(2,1)S(1)}, u32[]{:S(2)}, u32[]{:S(2)}) collective-permute-start(bf16[256,512]{1,0:T(8,128)(2,1)S(1)} %slice_bitcast_fusion.4), channel_id=1, source_target_pairs={{0,16},{16,32},{32,48},{48,0},{1,17},{17,33},{33,49},{49,1},{2,18}... | collective-permute-start | bytes 786440 | tf_op jit(solution)/shard_map/ppermute | solution.py:37
  98.2 6.7 %collective-permute-start.6 = (bf16[4,128,256]{2,1,0:T(8,128)(2,1)}, bf16[4,128,256]{2,1,0:T(8,128)(2,1)}, u32[]{:S(2)}, u32[]{:S(2)}) collective-permute-start(bf16[4,128,256]{2,1,0:T(8,128)(2,1)} %all_to_all.30), channel_id=1, source_target_pairs={{0,12},{4,0},{8,4},{12,8},{1,13},{5,1},{9,5},{13,9},{2,14},{6,2},{... | collective-permute-start | bytes 786440 | tf_op jit(solution)/shard_map/ppermute | solution.py:37
  99.3 19.4 %collective-permute-start.13 = (bf16[2,256,512]{2,1,0:T(8,128)(2,1)}, bf16[2,256,512]{2,1,0:T(8,128)(2,1)S(1)}, u32[]{:S(2)}, u32[]{:S(2)}) collective-permute-start(bf16[2,256,512]{2,1,0:T(8,128)(2,1)} %pad_maximum_fusion.refs_0_), channel_id=1, source_target_pairs={{0,64},{64,0},{1,65},{65,1},{2,66},{66,2},{3,67},{67,3},{4,68},{68... | collective-permute-start | bytes 1572872 | tf_op jit(solution)/shard_map/ppermute | solution.py:41
  99.6 19.2 %collective-permute-start.14 = (bf16[2,256,512]{2,1,0:T(8,128)(2,1)}, bf16[2,256,512]{2,1,0:T(8,128)(2,1)S(1)}, u32[]{:S(2)}, u32[]{:S(2)}) collective-permute-start(bf16[2,256,512]{2,1,0:T(8,128)(2,1)} %collective-permute-done.9.refs_1_), channel_id=1, source_target_pairs={{0,64},{64,0},{1,65},{65,1},{2,66},{66,2},{3,67},{67,3},{4,68},{68... | collective-permute-start | bytes 1572872 | tf_op jit(solution)/shard_map/ppermute | solution.py:41
  101.5 17.2 %copy-start.8 = (bf16[256,512]{1,0:T(8,128)(2,1)}, bf16[256,512]{1,0:T(8,128)(2,1)S(1)}, u32[]{:S(2)}) copy-start(bf16[256,512]{1,0:T(8,128)(2,1)S(1)} %collective-permute-done.11.refs_3_) | copy-start | bytes 786436
  101.5 17.2 %collective-permute-start.15 = (bf16[2,256,512]{2,1,0:T(8,128)(2,1)}, bf16[2,256,512]{2,1,0:T(8,128)(2,1)S(1)}, u32[]{:S(2)}, u32[]{:S(2)}) collective-permute-start(bf16[2,256,512]{2,1,0:T(8,128)(2,1)} %collective-permute-done.10.refs_2_), channel_id=1, source_target_pairs={{0,64},{64,0},{1,65},{65,1},{2,66},{66,2},{3,67},{67,3},{4,68},{68... | collective-permute-start | bytes 1572872 | tf_op jit(solution)/shard_map/ppermute | solution.py:41
  102.2 4.2 %copy-start.10 = (bf16[256,512]{1,0:T(8,128)(2,1)}, bf16[256,512]{1,0:T(8,128)(2,1)S(1)}, u32[]{:S(2)}) copy-start(bf16[256,512]{1,0:T(8,128)(2,1)S(1)} %collective-permute-done.12.refs_4_) | copy-start | bytes 786436
  102.2 9.8 %collective-permute-start.7 = (bf16[4,128,256]{2,1,0:T(8,128)(2,1)}, bf16[4,128,256]{2,1,0:T(8,128)(2,1)S(1)}, u32[]{:S(2)}, u32[]{:S(2)}) collective-permute-start(bf16[4,128,256]{2,1,0:T(8,128)(2,1)} %all_to_all.30), channel_id=1, source_target_pairs={{0,8},{4,12},{8,0},{12,4},{1,9},{5,13},{9,1},{13,5},{2,10},{6,14},... | collective-permute-start | bytes 786440 | tf_op jit(solution)/shard_map/ppermute | solution.py:37
  105.0 12.7 %collective-permute-start.8 = (bf16[4,128,256]{2,1,0:T(8,128)(2,1)}, bf16[4,128,256]{2,1,0:T(8,128)(2,1)S(1)}, u32[]{:S(2)}, u32[]{:S(2)}) collective-permute-start(bf16[4,128,256]{2,1,0:T(8,128)(2,1)} %all_to_all.30), channel_id=1, source_target_pairs={{0,4},{4,8},{8,12},{12,0},{1,5},{5,9},{9,13},{13,1},{2,6},{6,10},{... | collective-permute-start | bytes 786440 | tf_op jit(solution)/shard_map/ppermute | solution.py:37
  112.0 6.8 %collective-permute-start.16 = (bf16[256,512]{1,0:T(8,128)(2,1)S(1)}, bf16[256,512]{1,0:T(8,128)(2,1)S(1)}, u32[]{:S(2)}, u32[]{:S(2)}) collective-permute-start(bf16[256,512]{1,0:T(8,128)(2,1)S(1)} %collective-permute-done.11.refs_3_), channel_id=1, source_target_pairs={{0,64},{64,0},{1,65},{65,1},{2,66},{66,2},{3,67},{67,3},{4,68},{68... | collective-permute-start | bytes 786440 | tf_op jit(solution)/shard_map/ppermute | solution.py:41
  117.7 1.7 collective-permute-start.17
  119.4 1.0 copy-start.9
  120.4 0.9 copy-start.11
  123.4 2.0 %copy-start.3 = (bf16[16,256,512]{2,1,0:T(8,128)(2,1)}, bf16[16,256,512]{2,1,0:T(8,128)(2,1)S(1)}, u32[]{:S(2)}) copy-start(bf16[16,256,512]{2,1,0:T(8,128)(2,1)S(1)} %get-tuple-element.106.rows_ref) | copy-start | bytes 12582916
  125.4 2.2 %copy-start.4 = (bf16[16,256,512]{2,1,0:T(8,128)(2,1)S(1)}, bf16[16,256,512]{2,1,0:T(8,128)(2,1)}, u32[]{:S(2)}) copy-start(bf16[16,256,512]{2,1,0:T(8,128)(2,1)} %copy-done.3) | copy-start | bytes 12582916
  130.9 4.2 %collective-permute-start.21 = (bf16[8,256,512]{2,1,0:T(8,128)(2,1)S(1)}, bf16[8,256,512]{2,1,0:T(8,128)(2,1)S(1)}, u32[]{:S(2)}, u32[]{:S(2)}) collective-permute-start(bf16[8,256,512]{2,1,0:T(8,128)(2,1)S(1)} %shard_map.96), channel_id=1, source_target_pairs={{0,64},{64,0},{1,65},{65,1},{2,66},{66,2},{3,67},{67,3},{4,68},{68... | collective-permute-start | bytes 6291464 | tf_op jit(solution)/shard_map/ppermute | solution.py:41
  131.2 9.2 %collective-permute-start.18 = (bf16[4,128,256]{2,1,0:T(8,128)(2,1)S(1)}, bf16[4,128,256]{2,1,0:T(8,128)(2,1)S(1)}, u32[]{:S(2)}, u32[]{:S(2)}) collective-permute-start(bf16[4,128,256]{2,1,0:T(8,128)(2,1)S(1)} %get-tuple-element.136), channel_id=1, source_target_pairs={{0,4},{4,8},{8,12},{12,0},{1,5},{5,9},{9,13},{13,1},{2,6},{6,10},{... | collective-permute-start | bytes 786440 | tf_op jit(solution)/shard_map/ppermute | solution.py:37
  132.5 10.7 %collective-permute-start.19 = (bf16[4,128,256]{2,1,0:T(8,128)(2,1)S(1)}, bf16[4,128,256]{2,1,0:T(8,128)(2,1)S(1)}, u32[]{:S(2)}, u32[]{:S(2)}) collective-permute-start(bf16[4,128,256]{2,1,0:T(8,128)(2,1)S(1)} %get-tuple-element.135), channel_id=1, source_target_pairs={{0,8},{4,12},{8,0},{12,4},{1,9},{5,13},{9,1},{13,5},{2,10},{6,14},... | collective-permute-start | bytes 786440 | tf_op jit(solution)/shard_map/ppermute | solution.py:37
  134.8 52.4 %copy-start.14 = (s32[2]{0:T(128)S(1)}, s32[2]{0:T(128)}, u32[]{:S(2)}) copy-start(s32[2]{0:T(128)} %pad_add_fusion.at_ref.y_ref) | copy-start | bytes 28
  134.8 13.1 %collective-permute-start.20 = (bf16[4,128,256]{2,1,0:T(8,128)(2,1)S(1)}, bf16[4,128,256]{2,1,0:T(8,128)(2,1)S(1)}, u32[]{:S(2)}, u32[]{:S(2)}) collective-permute-start(bf16[4,128,256]{2,1,0:T(8,128)(2,1)S(1)} %get-tuple-element.134), channel_id=1, source_target_pairs={{0,12},{4,0},{8,4},{12,8},{1,13},{5,1},{9,5},{13,9},{2,14},{6,2},{... | collective-permute-start | bytes 786440 | tf_op jit(solution)/shard_map/ppermute | solution.py:37
  136.4 11.5 %collective-permute-start.22 = (bf16[256,512]{1,0:T(8,128)(2,1)S(1)}, bf16[256,512]{1,0:T(8,128)(2,1)S(1)}, u32[]{:S(2)}, u32[]{:S(2)}) collective-permute-start(bf16[256,512]{1,0:T(8,128)(2,1)S(1)} %get-tuple-element.114), channel_id=1, source_target_pairs={{0,16},{16,32},{32,48},{48,0},{1,17},{17,33},{33,49},{49,1},{2,18}... | collective-permute-start | bytes 786440 | tf_op jit(solution)/shard_map/ppermute | solution.py:37
  136.5 11.4 %collective-permute-start.23 = (bf16[256,512]{1,0:T(8,128)(2,1)S(1)}, bf16[256,512]{1,0:T(8,128)(2,1)S(1)}, u32[]{:S(2)}, u32[]{:S(2)}) collective-permute-start(bf16[256,512]{1,0:T(8,128)(2,1)S(1)} %get-tuple-element.115), channel_id=1, source_target_pairs={{0,48},{16,0},{32,16},{48,32},{1,49},{17,1},{33,17},{49,33},{2,50}... | collective-permute-start | bytes 786440 | tf_op jit(solution)/shard_map/ppermute | solution.py:37
  149.6 12.3 %all-to-all-start.4 = ((bf16[4,128,256]{2,1,0:T(8,128)(2,1)}), bf16[4,128,256]{2,1,0:T(8,128)(2,1)S(1)}, u32[]{:S(2)}, u32[]{:S(2)}) async-start(bf16[4,128,256]{2,1,0:T(8,128)(2,1)} %shard_map.99), calls=%async_computation.4 | async-start | bytes 524288 | tf_op jit(solution)/shard_map/all_to_all | solution.py:45
  154.7 13.5 %collective-permute-start.24 = (bf16[2,256,512]{2,1,0:T(8,128)(2,1)}, bf16[2,256,512]{2,1,0:T(8,128)(2,1)S(1)}, u32[]{:S(2)}, u32[]{:S(2)}) collective-permute-start(bf16[2,256,512]{2,1,0:T(8,128)(2,1)} %get-tuple-element.121), channel_id=1, source_target_pairs={{0,16},{16,32},{32,48},{48,0},{1,17},{17,33},{33,49},{49,1},{2,18}... | collective-permute-start | bytes 1572872 | tf_op jit(solution)/shard_map/ppermute | solution.py:37
  154.8 14.5 %collective-permute-start.25 = (bf16[2,256,512]{2,1,0:T(8,128)(2,1)S(1)}, bf16[2,256,512]{2,1,0:T(8,128)(2,1)S(1)}, u32[]{:S(2)}, u32[]{:S(2)}) collective-permute-start(bf16[2,256,512]{2,1,0:T(8,128)(2,1)S(1)} %get-tuple-element.122), channel_id=1, source_target_pairs={{0,48},{16,0},{32,16},{48,32},{1,49},{17,1},{33,17},{49,33},{2,50}... | collective-permute-start | bytes 1572872 | tf_op jit(solution)/shard_map/ppermute | solution.py:37
  162.7 11.6 %all-to-all-start.5 = ((bf16[4,128,256]{2,1,0:T(8,128)(2,1)}), bf16[4,128,256]{2,1,0:T(8,128)(2,1)S(1)}, u32[]{:S(2)}, u32[]{:S(2)}) async-start(bf16[4,128,256]{2,1,0:T(8,128)(2,1)} %shard_map.100), calls=%async_computation.5 | async-start | bytes 524288 | tf_op jit(solution)/shard_map/all_to_all | solution.py:45
  174.3 9.6 %collective-permute-start.26 = (bf16[4,128,256]{2,1,0:T(8,128)(2,1)S(1)}, bf16[4,128,256]{2,1,0:T(8,128)(2,1)S(1)}, u32[]{:S(2)}, u32[]{:S(2)}) collective-permute-start(bf16[4,128,256]{2,1,0:T(8,128)(2,1)S(1)} %all-to-all-done.5.refs_0_), channel_id=1, source_target_pairs={{0,12},{4,0},{8,4},{12,8},{1,13},{5,1},{9,5},{13,9},{2,14},{6,2},{... | collective-permute-start | bytes 786440 | tf_op jit(solution)/shard_map/ppermute | solution.py:37
  174.3 11.6 %collective-permute-start.27 = (bf16[4,128,256]{2,1,0:T(8,128)(2,1)S(1)}, bf16[4,128,256]{2,1,0:T(8,128)(2,1)S(1)}, u32[]{:S(2)}, u32[]{:S(2)}) collective-permute-start(bf16[4,128,256]{2,1,0:T(8,128)(2,1)S(1)} %all-to-all-done.5.refs_0_), channel_id=1, source_target_pairs={{0,8},{4,12},{8,0},{12,4},{1,9},{5,13},{9,1},{13,5},{2,10},{6,14},... | collective-permute-start | bytes 786440 | tf_op jit(solution)/shard_map/ppermute | solution.py:37
  176.5 10.6 %collective-permute-start.28 = (bf16[4,128,256]{2,1,0:T(8,128)(2,1)S(1)}, bf16[4,128,256]{2,1,0:T(8,128)(2,1)S(1)}, u32[]{:S(2)}, u32[]{:S(2)}) collective-permute-start(bf16[4,128,256]{2,1,0:T(8,128)(2,1)S(1)} %all-to-all-done.5.refs_0_), channel_id=1, source_target_pairs={{0,4},{4,8},{8,12},{12,0},{1,5},{5,9},{9,13},{13,1},{2,6},{6,10},{... | collective-permute-start | bytes 786440 | tf_op jit(solution)/shard_map/ppermute | solution.py:37
  179.4 12.7 %collective-permute-start.29 = (bf16[256,512]{1,0:T(8,128)(2,1)S(1)}, bf16[256,512]{1,0:T(8,128)(2,1)S(1)}, u32[]{:S(2)}, u32[]{:S(2)}) collective-permute-start(bf16[256,512]{1,0:T(8,128)(2,1)S(1)} %get-tuple-element.130), channel_id=1, source_target_pairs={{0,128},{128,0},{1,129},{129,1},{2,130},{130,2},{3,131},{131,3},{4... | collective-permute-start | bytes 786440 | tf_op jit(solution)/shard_map/ppermute | solution.py:41
  187.1 1.6 copy-start.2
